TPU v7x, 512 devices: a whole 4x8x8 slice. The times are simulated.
512 devices in a mesh: rep: 8 (over z), fsdp: 64 (over y, x, core).
Axes of the slice: x: 4, y: 8, z: 8, core: 2. Of those that a mesh axis runs over, the one named last changes fastest.
Arguments:
- grads: bfloat16 [8, 2, 1024, 8192], P('rep', None, 'fsdp'), may hold values from -6 to 6
- params: bfloat16 [2, 1024, 8192], P(None, 'fsdp', 'rep'), may hold values from -6 to 6
- left_basis: bfloat16 [2, 1024, 1024], P(None, 'fsdp'), may hold values from -0.1875 to 0.1875
- right_basis: bfloat16 [2, 8192, 1024], P(None, ('rep', 'fsdp')), may hold values from -0.1875 to 0.1875
- moment: float32 [2, 1024, 8192], P(None, 'fsdp', 'rep'), may hold values from -6 to 6
- codes: int32 [2, 1024, 8192], P(None, 'fsdp', 'rep'), may hold values from 0 to 15, as said below
- level_low: float32 [2, 64], P(None, 'rep'), may hold values from 0.2 to 2
- level_span: float32 [2, 64], P(None, 'rep'), may hold values from 0.5 to 8
Outputs:
- params_new: bfloat16 [2, 1024, 8192], P(None, 'fsdp')
- moment_new: float32 [2, 1024, 8192], P(None, 'fsdp', 'rep')
- update: float32 [2, 1024, 8192], P(None, 'fsdp', 'rep')
- levels: float32 [2, 1024, 8192], P(None, 'fsdp', 'rep')
- low_new: float32 [2, 64], P(None, 'rep')
- span_new: float32 [2, 64], P(None, 'rep')
Inputs may be any that keep to these rules, and one draw needn't show every extreme that they name: `codes`: in each layer and quantization group exactly one entry has code 0; all others are 1 to 15.
All inputs are finite; a program needn't handle non-finite values.
Results may differ from a plain program's by a relative error of at most 0.017.
Values may be sent and summed in bfloat16 or wider, within the bound.
No kernel may reach another device: no remote copies, remote signals or barrier semaphores. Data moves between devices by JAX's collectives and lax.ppermute only.
A program may use at most 64 MiB of HBM per device.

v0:
```python
import jax
import jax.numpy as jnp
from jax import lax
from jax.sharding import PartitionSpec as P

QGROUP = 128


def on_device(grads, params, left_basis, right_basis, moment, codes, level_low, level_span):
    summed = lax.psum_scatter(
        grads.astype(jnp.float32).astype(jnp.bfloat16), "rep", scatter_dimension=3, tiled=True
    ).astype(jnp.float32)[0]
    grad16 = summed.astype(jnp.bfloat16)
    layers, rows_here, width = grad16.shape
    panels = lax.all_gather(right_basis, "fsdp", axis=1, tiled=True)
    projected = jnp.einsum(
        "lik,lkj->lij", grad16, panels, preferred_element_type=jnp.float32
    ).astype(jnp.bfloat16)
    left_cols = lax.all_to_all(left_basis, "fsdp", split_axis=2, concat_axis=1, tiled=True)
    slab = left_cols
    rotated = jnp.einsum(
        "lki,lkj->lij",
        slab,
        lax.all_gather(projected, "fsdp", axis=1, tiled=True),
        preferred_element_type=jnp.float32,
    )
    moment_new = 0.9 * moment + 0.1 * rotated
    groups_here = width // QGROUP
    rotated_grouped = rotated.reshape(layers, rows_here, groups_here, QGROUP)
    code_grouped = codes.reshape(layers, rows_here, groups_here, QGROUP).astype(jnp.float32)
    second = level_low[:, None, :, None] + code_grouped / 15.0 * level_span[:, None, :, None]
    second_new = 0.95 * second + 0.05 * rotated_grouped * rotated_grouped
    second_flat = second_new.reshape(layers, rows_here, width)
    scaled = (moment_new / (jnp.sqrt(second_flat) + 1e-08)).astype(jnp.bfloat16)
    returned = jnp.einsum(
        "lik,ljk->lij", scaled, panels, preferred_element_type=jnp.float32
    ).astype(jnp.bfloat16)
    slab = left_basis
    update = jnp.einsum(
        "lik,lkj->lij",
        slab,
        lax.all_gather(returned, "fsdp", axis=1, tiled=True),
        preferred_element_type=jnp.float32,
    )
    local_low = jnp.min(second_new, axis=(1, 3))
    local_high = jnp.max(second_new, axis=(1, 3))
    low_new = lax.pmin(local_low, "fsdp")
    highest = lax.pmax(local_high, "fsdp")
    span_new = highest - low_new
    levels = 15.0 * (second_new - low_new[:, None, :, None]) / span_new[:, None, :, None]
    levels = levels.reshape(layers, rows_here, width)
    stepped = (params.astype(jnp.float32) * (1.0 - 0.05 * 0.1) - 0.05 * update).astype(jnp.bfloat16)
    params_new = lax.all_gather(stepped, "rep", axis=2, tiled=True)
    return (params_new, moment_new, update, levels, low_new, span_new)


def solution(mesh):
    return jax.shard_map(
        on_device,
        mesh=mesh,
        in_specs=(
            P("rep", None, "fsdp", None),
            P(None, "fsdp", "rep"),
            P(None, "fsdp", None),
            P(None, ("rep", "fsdp"), None),
            P(None, "fsdp", "rep"),
            P(None, "fsdp", "rep"),
            P(None, "rep"),
            P(None, "rep"),
        ),
        out_specs=(
            P(None, "fsdp", None),
            P(None, "fsdp", "rep"),
            P(None, "fsdp", "rep"),
            P(None, "fsdp", "rep"),
            P(None, "rep"),
            P(None, "rep"),
        ),
        check_vma=False,
    )
```

profile of v0, /device:TPU:1, one launch (start us, length us, event | category | flops | bytes accessed | tf_op | source)
XLA Modules:
  0.0 479.5 jit_solution(9664069411142004350)
XLA Ops:
  8.0 0.0 reduce-scatter.2.cloned.1.call-start
  8.1 0.7 reduce-scatter.2.cloned.1.call-update
  8.8 0.0 all-gather.4.cloned.1.call-start
  8.8 0.5 all-gather.4.cloned.1.call-update
  9.4 0.0 all-gather.6.cloned.1.call-start
  9.4 44.3 %reduce-scatter.2.cloned.1.call-done = bf16[1,2,16,1024]{3,2,1,0:T(8,128)(2,1)} async-done(((bf16[1,2,16,8192]{3,2,1,0:T(8,128)(2,1)}), bf16[1,2,16,1024]{3,2,1,0:T(8,128)(2,1)}) %reduce-scatter.2.cloned.1.call-update) | async-done | bytes 65552 | tf_op jit(solution)/shard_map/reduce_scatter | solution.py:10
  53.7 49.1 %all-gather.4.cloned.1.call-done = bf16[2,1024,1024]{2,1,0:T(8,128)(2,1)} async-done(((bf16[2,16,1024]{2,1,0:T(8,128)(2,1)}), bf16[2,1024,1024]{2,1,0:T(8,128)(2,1)}) %all-gather.4.cloned.1.call-update) | async-done | bytes 4194320 | tf_op jit(solution)/shard_map/all_gather | solution.py:15
  102.8 3.5 convolution_convert_fusion.1
  106.3 0.4 copy.19
  106.7 1.1 reshape.33
  107.8 6.4 %all-to-all-start = ((bf16[64,2,256]{2,1,0:T(2,128)(2,1)}), bf16[64,2,256]{2,1,0:T(2,128)(2,1)S(1)}, u32[]{:S(2)}, u32[]{:S(2)}) async-start(bf16[64,2,256]{2,1,0:T(2,128)(2,1)} %reshape.33), calls=%async_computation.1 | async-start | bytes 131072 | tf_op jit(solution)/shard_map/all_to_all | solution.py:19
  114.3 0.0 all-gather.8.cloned.1.call-start
  114.3 0.1 broadcast_bitcast_fusion.2
  114.4 0.1 broadcast_bitcast_fusion.3
  114.5 9.9 %all-to-all-done = bf16[64,2,256]{2,1,0:T(2,128)(2,1)S(1)} async-done(((bf16[64,2,256]{2,1,0:T(2,128)(2,1)}), bf16[64,2,256]{2,1,0:T(2,128)(2,1)S(1)}, u32[]{:S(2)}, u32[]{:S(2)}) %all-to-all-start) | async-done | bytes 65568 | tf_op jit(solution)/shard_map/all_to_all | solution.py:19
  124.3 0.4 reshape.34
  124.7 0.2 copy.37
  124.9 0.8 all_to_all.16
  125.7 63.5 %all-gather.6.cloned.1.call-done = bf16[2,1024,1024]{2,1,0:T(8,128)(2,1)} async-done(((bf16[2,16,1024]{2,1,0:T(8,128)(2,1)}), bf16[2,1024,1024]{2,1,0:T(8,128)(2,1)}) %all-gather.6.cloned.1.call-update) | async-done | bytes 4194320 | tf_op jit(solution)/shard_map/all_gather | solution.py:24
  189.2 3.1 fusion.4
  192.2 0.4 copy-done.1
  192.6 1.8 convolution_convert_fusion
  194.5 0.1 bitcast_reduce_fusion
  194.6 0.1 bitcast_reduce_fusion.1
  194.6 124.0 %pmax.7 = f32[2,8]{1,0:T(2,128)S(1)} all-reduce(f32[2,8]{1,0:T(2,128)S(1)} %bitcast_reduce_fusion), channel_id=1, replica_groups=mesh['rep'=8,'fsdp'=64] {'fsdp'}, use_global_device_ids=true, to_apply=%region_6.7 | all-reduce | flops 16 | bytes 128 | tf_op jit(solution)/shard_map/pmax | solution.py:48
  318.6 126.3 %pmin.7 = f32[2,8]{1,0:T(2,128)S(1)} all-reduce(f32[2,8]{1,0:T(2,128)S(1)} %bitcast_reduce_fusion.1), channel_id=1, replica_groups=mesh['rep'=8,'fsdp'=64] {'fsdp'}, use_global_device_ids=true, to_apply=%region_3.0 | all-reduce | flops 16 | bytes 128 | tf_op jit(solution)/shard_map/pmin | solution.py:47
  445.0 0.1 broadcast_bitcast_fusion
  445.1 0.1 broadcast_bitcast_fusion.1
  445.2 0.7 multiply_divide_fusion
  445.8 3.5 subtract_convert_fusion
  449.4 21.8 %all_gather.15 = bf16[2,16,8192]{2,1,0:T(8,128)(2,1)S(1)} all-gather(bf16[2,16,1024]{2,1,0:T(8,128)(2,1)S(1)} %get-tuple-element.10), channel_id=1, replica_groups=mesh['rep'=8,'fsdp'=64] {'rep'}, dimensions={2}, use_global_device_ids=true | all-gather | bytes 589824 | tf_op jit(solution)/shard_map/all_gather | solution.py:53
  471.1 0.8 copy.41
  (27 shorter events, 0.1 us)
Async XLA Ops:
  8.0 106.4 %copy-start = (f32[2,8]{1,0:T(2,128)S(1)}, f32[2,8]{1,0:T(2,128)}, u32[]{:S(2)}) copy-start(f32[2,8]{1,0:T(2,128)} %param.14) | copy-start | bytes 196
  8.0 98.3 %copy-start.3 = (bf16[2,16,1024]{2,1,0:T(8,128)(2,1)S(1)}, bf16[2,16,1024]{2,1,0:T(8,128)(2,1)}, u32[]{:S(2)}) copy-start(bf16[2,16,1024]{2,1,0:T(8,128)(2,1)} %param.10) | copy-start | bytes 196612
  8.0 106.3 %copy-start.9 = (f32[2,8]{1,0:T(2,128)S(1)}, f32[2,8]{1,0:T(2,128)}, u32[]{:S(2)}) copy-start(f32[2,8]{1,0:T(2,128)} %param.15) | copy-start | bytes 196
  8.0 45.7 %reduce-scatter.2.cloned.1.call-start = ((), (), s32[]{:S(2)}) async-start(), calls=%async_computation.2 | async-start | bytes 589824 | tf_op jit(solution)/shard_map/reduce_scatter | solution.py:10
  8.8 180.4 %copy-start.4 = (s32[2,16,1024]{2,1,0:T(8,128)S(1)}, s32[2,16,1024]{2,1,0:T(8,128)}, u32[]{:S(2)}) copy-start(s32[2,16,1024]{2,1,0:T(8,128)} %param.13) | copy-start | bytes 393220
  8.8 180.4 %copy-start.5 = (f32[2,16,1024]{2,1,0:T(8,128)S(1)}, f32[2,16,1024]{2,1,0:T(8,128)}, u32[]{:S(2)}) copy-start(f32[2,16,1024]{2,1,0:T(8,128)} %param.12) | copy-start | bytes 393220
  8.8 94.0 %all-gather.4.cloned.1.call-start = ((), (), s32[]{:S(2)}) async-start(), calls=%async_computation.3 | async-start | bytes 4259840 | tf_op jit(solution)/shard_map/all_gather | solution.py:15
  9.4 179.8 %all-gather.6.cloned.1.call-start = ((), (), s32[]{:S(2)}) async-start(), calls=%async_computation.4 | async-start | bytes 4259840 | tf_op jit(solution)/shard_map/all_gather | solution.py:24
  107.8 16.5 %all-to-all-start = ((bf16[64,2,256]{2,1,0:T(2,128)(2,1)}), bf16[64,2,256]{2,1,0:T(2,128)(2,1)S(1)}, u32[]{:S(2)}, u32[]{:S(2)}) async-start(bf16[64,2,256]{2,1,0:T(2,128)(2,1)} %reshape.33), calls=%async_computation.1 | async-start | bytes 131072 | tf_op jit(solution)/shard_map/all_to_all | solution.py:19
  114.3 331.6 %all-gather.8.cloned.1.call-start = ((), (), s32[]{:S(2)}) async-start(), calls=%async_computation.5 | async-start | bytes 4259840 | tf_op jit(solution)/shard_map/all_gather | solution.py:42
  189.2 3.4 copy-start.1
  189.2 256.7 %copy-start.6 = (bf16[2,16,1024]{2,1,0:T(8,128)(2,1)S(1)}, bf16[2,16,1024]{2,1,0:T(8,128)(2,1)}, u32[]{:S(2)}) copy-start(bf16[2,16,1024]{2,1,0:T(8,128)(2,1)} %param.9) | copy-start | bytes 196612
  192.2 257.1 %copy-start.2 = (f32[2,16,1024]{2,1,0:T(8,128)}, f32[2,16,1024]{2,1,0:T(8,128)S(1)}, u32[]{:S(2)}) copy-start(f32[2,16,1024]{2,1,0:T(8,128)S(1)} %get-tuple-element.21) | copy-start | bytes 393220
  445.0 26.9 %copy-start.7 = (f32[2,8]{1,0:T(2,128)}, f32[2,8]{1,0:T(2,128)S(1)}, u32[]{:S(2)}) copy-start(f32[2,8]{1,0:T(2,128)S(1)} %pmin.7) | copy-start | bytes 196
  445.0 26.9 %copy-start.8 = (f32[2,8]{1,0:T(2,128)}, f32[2,8]{1,0:T(2,128)S(1)}, u32[]{:S(2)}) copy-start(f32[2,8]{1,0:T(2,128)S(1)} %sub.24) | copy-start | bytes 196
Sparse Core Ops, SparseCore 0:
  11.7 41.9 reduce-scatter.1
Sparse Core Ops, SparseCore 1:
  12.7 90.1 all-gather.3
  107.2 81.9 all-gather.5
  194.5 82.0 all-gather.7
where the time goes:
time: 483 us; the launch traced here: 480 us
  blocking collectives  272 us (56%)
  waiting for transfers between devices  168 us (35%)
  between operations  15.8 us (3%)
  matrix products  11.9 us (2%)
  starting transfers between devices  6.58 us (1%)
    pmin x1, blocking collectives, on_device(): low_new = lax.pmin(local_low, 'fsdp')  126 us
    pmax x1, blocking collectives, on_device(): highest = lax.pmax(local_high, 'fsdp')  124 us
    all_gather x1, waiting for transfers between devices, on_device(): lax.all_gather(projected, 'fsdp', axis=1, tiled=True)  63.5 us
    all_gather x1, waiting for transfers between devices, on_device(): panels = lax.all_gather(right_basis, 'fsdp', axis=1, tiled=True)  49.1 us
    reduce_scatter x1, waiting for transfers between devices, on_device(): lax.psum_scatter(grads.astype(jnp.float32).astype(jnp.bfloat16), 'rep', s...  44.3 us
    all_gather x1, blocking collectives, on_device(): params_new = lax.all_gather(stepped, 'rep', axis=2, tiled=True)  21.8 us
    all_to_all x1, waiting for transfers between devices, on_device(): lax.all_to_all(left_basis, 'fsdp', split_axis=2, concat_axis=1, tiled=True)  9.86 us
  transfers between devices with their start and end apart: 5, of which 4 were waited for; matrix products, arithmetic and copies ran while one was open for 1% of the time, Pallas kernels for 0%

commit v1 on v0

v1 whole, which is shorter than its diff:
```python
import jax
import jax.numpy as jnp
from jax import lax
from jax.sharding import Mesh, PartitionSpec as P

QGROUP = 128
F = ("y", "x", "core")
ZQ = ("rep", "x", "core")
Q = ("x", "core")


def exchange(blocks, axes):
    return lax.all_to_all(blocks, axes, split_axis=0, concat_axis=0, tiled=True)


def pieces(values):
    first = lax.reduce_precision(values, 8, 7)
    rest = values - first
    second = lax.reduce_precision(rest, 8, 7)
    third = rest - second
    return jnp.stack([first, second, third]).astype(jnp.bfloat16)


def on_device(grads, params, left_basis, right_basis, moment, codes, level_low, level_span):
    bf16, f32 = jnp.bfloat16, jnp.float32
    both = jnp.broadcast_to(right_basis[None, None], (4, 2, 2, 16, 1024))
    lefts = jnp.broadcast_to(left_basis[None, :, None], (4, 2, 1, 16, 1024))
    bases = exchange(jnp.concatenate([both, lefts], axis=2).reshape(8, 3, 16, 1024), Q)
    right_y = bases[:, :2].transpose(1, 0, 2, 3).reshape(2, 128, 1024)
    left_y = bases[:, 2].reshape(128, 1024)
    right = lax.all_gather(right_y, "y", axis=1, tiled=True)

    sent = grads[0].reshape(2, 16, 8, 4, 256).transpose(2, 3, 0, 1, 4).reshape(64, 16, 256)
    got = exchange(sent, ZQ).reshape(8, 128, 256)
    grad16 = jnp.sum(got.astype(f32), axis=0).astype(bf16)
    part = jnp.einsum("ki,kj->ij", left_y, grad16, preferred_element_type=f32).astype(bf16)
    got = exchange(part.reshape(64, 16, 256), F).reshape(8, 4, 2, 16, 256)
    turned = jnp.sum(got.astype(f32), axis=0).transpose(1, 2, 0, 3).reshape(2, 16, 1024).astype(bf16)

    doubled = jnp.concatenate([params, jnp.zeros_like(params)], axis=0)
    params_all = lax.all_gather(doubled, "rep", axis=0)[:, :2]

    rotated = jnp.einsum("lik,lkj->lij", turned, right, preferred_element_type=f32)
    moment_new = 0.9 * moment + 0.1 * rotated
    grouped = rotated.reshape(2, 16, 8, QGROUP)
    code_grouped = codes.reshape(2, 16, 8, QGROUP).astype(f32)
    second = level_low[:, None, :, None] + code_grouped / 15.0 * level_span[:, None, :, None]
    second_new = 0.95 * second + 0.05 * grouped * grouped
    flat = second_new.reshape(2, 16, 1024)
    scaled = (moment_new / (jnp.sqrt(flat) + 1e-08)).astype(bf16)
    returned = jnp.einsum("lik,ljk->lij", scaled, right, preferred_element_type=f32).astype(bf16)

    ends = jnp.stack([jnp.min(second_new, axis=(1, 3)), jnp.max(second_new, axis=(1, 3))])
    row = jnp.pad(pieces(ends).reshape(1, 96), ((0, 7), (0, 32)))
    block = returned.reshape(2, 16, 4, 2, 128).transpose(2, 0, 3, 1, 4).reshape(4, 2, 32, 128)
    block = jnp.concatenate([block, jnp.broadcast_to(row, (4, 2, 8, 128))], axis=2)
    got = exchange(jnp.broadcast_to(block[None], (8, 4, 2, 40, 128)).reshape(64, 40, 128), F)
    back = got[:, :32].reshape(64, 2, 16, 128).transpose(0, 2, 1, 3).reshape(1024, 256)
    ends = got[:, 32, :96].astype(f32).reshape(64, 3, 2, 2, 8)
    ends = (ends[:, 0] + ends[:, 1]) + ends[:, 2]
    low_new = jnp.min(ends[:, 0], axis=0)
    span_new = jnp.max(ends[:, 1], axis=0) - low_new

    moved = jnp.einsum("ki,ij->kj", left_y, back, preferred_element_type=f32).astype(bf16)
    moved = jnp.broadcast_to(moved.reshape(1, 8, 16, 256), (8, 8, 16, 256)).reshape(64, 16, 256)
    got = exchange(moved, ZQ).reshape(8, 4, 2, 16, 256)

    levels = 15.0 * (second_new - low_new[:, None, :, None]) / span_new[:, None, :, None]
    levels = levels.reshape(2, 16, 1024)
    mine = lax.dynamic_index_in_dim(got, lax.axis_index("rep"), 0, keepdims=False)
    update = mine.transpose(1, 2, 0, 3).reshape(2, 16, 1024).astype(f32)
    every = got.transpose(2, 3, 0, 1, 4).reshape(2, 16, 8192).astype(f32)
    old = params_all.transpose(1, 2, 0, 3).reshape(2, 16, 8192).astype(f32)
    params_new = (old * (1.0 - 0.05 * 0.1) - 0.05 * every).astype(bf16)
    return (params_new, moment_new, update, levels, low_new, span_new)


def solution(mesh):
    fine = Mesh(mesh.devices.reshape(8, 8, 4, 2), ("rep", "y", "x", "core"))
    return jax.shard_map(
        on_device,
        mesh=fine,
        in_specs=(
            P("rep", None, F, None),
            P(None, F, "rep"),
            P(None, F, None),
            P(None, ("rep",) + F, None),
            P(None, F, "rep"),
            P(None, F, "rep"),
            P(None, "rep"),
            P(None, "rep"),
        ),
        out_specs=(
            P(None, F, None),
            P(None, F, "rep"),
            P(None, F, "rep"),
            P(None, F, "rep"),
            P(None, "rep"),
            P(None, "rep"),
        ),
        check_vma=False,
    )
```

time: 483 us -> 183 us (0.38)
  blocking collectives: 272 us -> 21.5 us
  waiting for transfers between devices: 168 us -> 85.7 us
  starting transfers between devices: 6.58 us -> 39.2 us
  local copies, waits for them, and re-layouts: 4.32 us -> 10.8 us
    pmin x1 -> x0, blocking collectives: 126 us -> none  [on_device(): low_new = lax.pmin(local_low, 'fsdp')]
    pmax x1 -> x0, blocking collectives: 124 us -> none  [on_device(): highest = lax.pmax(local_high, 'fsdp')]
    all_gather x3 -> x2, waiting for transfers between devices: 113 us -> 29.1 us  [the longest x1 24 us: on_device(): params_all = lax.all_gather(doubled, 'rep', axis=0)[:, :2]]
    all_to_all x1 -> x4, waiting for transfers between devices: 9.86 us -> 56.5 us  [exchange(): return lax.all_to_all(blocks, axes, split_axis=0, concat_axis=0, tiled=True)]
    reduce_scatter x1 -> x0, waiting for transfers between devices: 44.3 us -> none  [on_device(): lax.psum_scatter(grads.astype(jnp.float32).astype(jnp.bfloat16), 'rep', s...]
    all_to_all x1 -> x4, starting transfers between devices: 6.42 us -> 39.2 us  [exchange(): return lax.all_to_all(blocks, axes, split_axis=0, concat_axis=0, tiled=True)]
    all_gather x1 -> x0, blocking collectives: 21.8 us -> none  [on_device(): params_new = lax.all_gather(stepped, 'rep', axis=2, tiled=True)]
    all_to_all x0 -> x1, blocking collectives: none -> 21.5 us  [exchange(): return lax.all_to_all(blocks, axes, split_axis=0, concat_axis=0, tiled=True)]
  transfers between devices with their start and end apart: 5 -> 6, of which waited for: 4 -> 5; matrix products, arithmetic and copies ran while one was open for 1% -> 8% of each run, Pallas kernels for 0% -> 0%
where the time goes in v1:
time: 183 us; the launch traced here: 182 us
  waiting for transfers between devices  85.7 us (47%)
  starting transfers between devices  39.2 us (21%)
  blocking collectives  21.5 us (12%)
  between operations  14.4 us (8%)
  local copies, waits for them, and re-layouts  10.8 us (6%)
  matrix products  7.63 us (4%)
  other arithmetic  2.68 us (1%)
    all_to_all x4, waiting for transfers between devices, exchange(): return lax.all_to_all(blocks, axes, split_axis=0, concat_axis=0, tiled=True)  56.5 us
    all_to_all x4, starting transfers between devices, exchange(): return lax.all_to_all(blocks, axes, split_axis=0, concat_axis=0, tiled=True)  39.2 us
    all_gather x1, waiting for transfers between devices, on_device(): params_all = lax.all_gather(doubled, 'rep', axis=0)[:, :2]  24 us
    all_to_all x1, blocking collectives, exchange(): return lax.all_to_all(blocks, axes, split_axis=0, concat_axis=0, tiled=True)  21.5 us
    all_gather x1, waiting for transfers between devices, on_device(): right = lax.all_gather(right_y, 'y', axis=1, tiled=True)  5.07 us
  transfers between devices with their start and end apart: 6, of which 5 were waited for; matrix products, arithmetic and copies ran while one was open for 8% of the time, Pallas kernels for 0%

profile of v1, /device:TPU:1, one launch (start us, length us, event | category | flops | bytes accessed | tf_op | source)
XLA Modules:
  0.0 181.9 jit_solution(2144387039888588092)
XLA Ops:
  7.2 0.9 broadcast_in_dim.12
  8.2 0.9 broadcast_in_dim.13
  9.1 21.5 %all_to_all.25 = bf16[8,3,16,1024]{3,2,1,0:T(8,128)(2,1)S(1)} all-to-all(bf16[8,3,16,1024]{3,2,1,0:T(8,128)(2,1)S(1)} %bitcast.80), channel_id=1, replica_groups=mesh['rep'=8,'y'=8,'x'=4,'core'=2] {'x','core'}, dimensions={0} | all-to-all | bytes 1572864 | tf_op jit(solution)/shard_map/all_to_all | solution.py:13
  30.7 0.9 copy.66
  31.6 0.4 reshape_squeeze.7
  32.0 1.1 copy.64
  33.1 8.8 %all-to-all-start.1 = ((bf16[64,16,256]{2,1,0:T(8,128)(2,1)}), bf16[64,16,256]{2,1,0:T(8,128)(2,1)S(1)}, u32[]{:S(2)}, u32[]{:S(2)}) async-start(bf16[64,16,256]{2,1,0:T(8,128)(2,1)} %bitcast.5), calls=%async_computation.1 | async-start | bytes 1048576 | tf_op jit(solution)/shard_map/all_to_all | solution.py:13
  41.9 17.7 %all-to-all-done.1 = bf16[64,16,256]{2,1,0:T(8,128)(2,1)S(1)} async-done(((bf16[64,16,256]{2,1,0:T(8,128)(2,1)}), bf16[64,16,256]{2,1,0:T(8,128)(2,1)S(1)}, u32[]{:S(2)}, u32[]{:S(2)}) %all-to-all-start.1) | async-done | bytes 524320 | tf_op jit(solution)/shard_map/all_to_all | solution.py:13
  59.7 1.1 convolution_convert_fusion
  60.8 10.5 %all-to-all-start.2 = ((bf16[64,16,256]{2,1,0:T(8,128)(2,1)}), bf16[64,16,256]{2,1,0:T(8,128)(2,1)S(1)}, u32[]{:S(2)}, u32[]{:S(2)}) async-start(bf16[64,16,256]{2,1,0:T(8,128)(2,1)} %bitcast.7), calls=%async_computation.2 | async-start | bytes 1048576 | tf_op jit(solution)/shard_map/all_to_all | solution.py:13
  71.4 0.7 concatenate.33
  72.2 22.2 %all-to-all-done.2 = bf16[64,16,256]{2,1,0:T(8,128)(2,1)S(1)} async-done(((bf16[64,16,256]{2,1,0:T(8,128)(2,1)}), bf16[64,16,256]{2,1,0:T(8,128)(2,1)S(1)}, u32[]{:S(2)}, u32[]{:S(2)}) %all-to-all-start.2) | async-done | bytes 524320 | tf_op jit(solution)/shard_map/all_to_all | solution.py:13
  94.5 5.1 %all-gather.4.cloned.1.call-done = bf16[2,1024,1024]{2,1,0:T(8,128)(2,1)} async-done(((bf16[2,128,1024]{2,1,0:T(8,128)(2,1)}), bf16[2,1024,1024]{2,1,0:T(8,128)(2,1)}) %all-gather.4.cloned.1.call-update) | async-done | bytes 4194320 | tf_op jit(solution)/shard_map/all_gather | solution.py:31
  99.6 2.9 %fusion.7 = (f32[2,1024]{1,0:T(2,128)S(1)}, f32[2,1024]{1,0:T(2,128)S(1)}, f32[2,16,1024]{2,1,0:T(8,128)S(1)}, f32[2,16,1024]{2,1,0:T(8,128)S(1)}) fusion(f32[2,1024]{1,0:T(2,128)S(1)} %get-tuple-element.15, s32[2,16,1024]{2,1,0:T(8,128)S(1)} %copy-done.3, f32[2,1024]{1,0:T(2,128)S(1)} %get-tuple-element.16, f32[2,16,1024]{2,1,0:T(8,128)S(1)} %copy-done.4, ...), kind=kOutput, calls=%fused_computation.44 | convolution fusion | flops 67497984 | bytes 4816896 | tf_op jit(solution)/shard_map/lik,lkj->lij/dot_general | solution.py:43
  102.8 3.4 %convolution_convert_fusion.2 = bf16[2,16,1024]{2,1,0:T(8,128)(2,1)S(1)} fusion(bf16[2,1024,1024]{2,1,0:T(8,128)(2,1)} %all-gather.4.cloned.1.call-done, f32[2,16,1024]{2,1,0:T(8,128)S(1)} %get-tuple-element.11, f32[2,16,1024]{2,1,0:T(8,128)S(1)} %get-tuple-element.10), kind=kOutput, calls=%fused_computation.2 | convolution fusion | flops 67239936 | bytes 4521984 | tf_op jit(solution)/shard_map/lik,ljk->lij/dot_general | solution.py:51
  106.3 0.9 broadcast_in_dim.15
  107.2 8.1 %all-to-all-start.3 = ((bf16[64,40,128]{2,1,0:T(8,128)(2,1)}), bf16[64,40,128]{2,1,0:T(8,128)(2,1)S(1)}, u32[]{:S(2)}, u32[]{:S(2)}) async-start(bf16[64,40,128]{2,1,0:T(8,128)(2,1)} %bitcast.16), calls=%async_computation.3 | async-start | bytes 1310720 | tf_op jit(solution)/shard_map/all_to_all | solution.py:13
  115.4 24.0 %all-gather.6.cloned.1.call-done = bf16[32,16,1024]{2,1,0:T(8,128)(2,1)} async-done(((bf16[4,16,1024]{2,1,0:T(8,128)(2,1)}), bf16[32,16,1024]{2,1,0:T(8,128)(2,1)}) %all-gather.6.cloned.1.call-update) | async-done | bytes 1048592 | tf_op jit(solution)/shard_map/all_gather | solution.py:41
  139.4 1.1 slice.40
  140.5 0.4 multiply_bitcast_fusion.1
  140.9 0.2 mul.90
  141.2 0.4 copy.68
  141.6 0.2 convolution_convert_fusion.1
  141.8 0.8 broadcast_in_dim.17
  142.7 11.7 %all-to-all-start.4 = ((bf16[64,16,256]{2,1,0:T(8,128)(2,1)}), bf16[64,16,256]{2,1,0:T(8,128)(2,1)S(1)}, u32[]{:S(2)}, u32[]{:S(2)}) async-start(bf16[64,16,256]{2,1,0:T(8,128)(2,1)} %bitcast.20), calls=%async_computation.4 | async-start | bytes 1048576 | tf_op jit(solution)/shard_map/all_to_all | solution.py:13
  154.8 0.7 multiply_divide_fusion
  155.5 16.6 %all-to-all-done.4 = bf16[64,16,256]{2,1,0:T(8,128)(2,1)S(1)} async-done(((bf16[64,16,256]{2,1,0:T(8,128)(2,1)}), bf16[64,16,256]{2,1,0:T(8,128)(2,1)S(1)}, u32[]{:S(2)}, u32[]{:S(2)}) %all-to-all-start.4) | async-done | bytes 524320 | tf_op jit(solution)/shard_map/all_to_all | solution.py:13
  172.1 0.1 multiply_bitcast_fusion
  172.3 0.7 copy.76
  173.0 0.7 copy.69
  173.7 0.5 mul.109
  174.2 0.9 subtract_convert_fusion
  (55 shorter events, 1.4 us)
Async XLA Ops:
  7.2 65.0 %copy-start = (f32[2,8]{1,0:T(2,128)S(1)}, f32[2,8]{1,0:T(2,128)}, u32[]{:S(2)}) copy-start(f32[2,8]{1,0:T(2,128)} %param.14) | copy-start | bytes 196
  7.2 24.4 %copy-start.2 = (bf16[1,2,16,8192]{3,2,1,0:T(8,128)(2,1)S(1)}, bf16[1,2,16,8192]{3,2,1,0:T(8,128)(2,1)}, u32[]{:S(2)}) copy-start(bf16[1,2,16,8192]{3,2,1,0:T(8,128)(2,1)} %param.8) | copy-start | bytes 1572868
  7.2 92.4 %all-gather.4.cloned.1.call-start = ((), (), s32[]{:S(2)}) async-start(), calls=%async_computation.5 | async-start | bytes 4718592 | tf_op jit(solution)/shard_map/all_gather | solution.py:31
  30.6 40.7 %copy-start.5 = (bf16[2,16,1024]{2,1,0:T(8,128)(2,1)S(1)}, bf16[2,16,1024]{2,1,0:T(8,128)(2,1)}, u32[]{:S(2)}) copy-start(bf16[2,16,1024]{2,1,0:T(8,128)(2,1)} %param.9) | copy-start | bytes 196612
  30.7 41.4 %copy-start.8 = (f32[2,8]{1,0:T(2,128)S(1)}, f32[2,8]{1,0:T(2,128)}, u32[]{:S(2)}) copy-start(f32[2,8]{1,0:T(2,128)} %param.15) | copy-start | bytes 196
  30.7 68.9 %copy-start.3 = (s32[2,16,1024]{2,1,0:T(8,128)S(1)}, s32[2,16,1024]{2,1,0:T(8,128)}, u32[]{:S(2)}) copy-start(s32[2,16,1024]{2,1,0:T(8,128)} %param.13) | copy-start | bytes 393220
  30.7 68.9 %copy-start.4 = (f32[2,16,1024]{2,1,0:T(8,128)S(1)}, f32[2,16,1024]{2,1,0:T(8,128)}, u32[]{:S(2)}) copy-start(f32[2,16,1024]{2,1,0:T(8,128)} %param.12) | copy-start | bytes 393220
  33.1 26.5 %all-to-all-start.1 = ((bf16[64,16,256]{2,1,0:T(8,128)(2,1)}), bf16[64,16,256]{2,1,0:T(8,128)(2,1)S(1)}, u32[]{:S(2)}, u32[]{:S(2)}) async-start(bf16[64,16,256]{2,1,0:T(8,128)(2,1)} %bitcast.5), calls=%async_computation.1 | async-start | bytes 1048576 | tf_op jit(solution)/shard_map/all_to_all | solution.py:13
  60.8 33.6 %all-to-all-start.2 = ((bf16[64,16,256]{2,1,0:T(8,128)(2,1)}), bf16[64,16,256]{2,1,0:T(8,128)(2,1)S(1)}, u32[]{:S(2)}, u32[]{:S(2)}) async-start(bf16[64,16,256]{2,1,0:T(8,128)(2,1)} %bitcast.7), calls=%async_computation.2 | async-start | bytes 1048576 | tf_op jit(solution)/shard_map/all_to_all | solution.py:13
  71.3 68.1 %all-gather.6.cloned.1.call-start = ((), (), s32[]{:S(2)}) async-start(), calls=%async_computation.6 | async-start | bytes 1179648 | tf_op jit(solution)/shard_map/all_gather | solution.py:41
  102.5 38.4 %copy-start.1 = (f32[2,16,1024]{2,1,0:T(8,128)}, f32[2,16,1024]{2,1,0:T(8,128)S(1)}, u32[]{:S(2)}) copy-start(f32[2,16,1024]{2,1,0:T(8,128)S(1)} %get-tuple-element.11) | copy-start | bytes 393220
  107.2 33.9 %all-to-all-start.3 = ((bf16[64,40,128]{2,1,0:T(8,128)(2,1)}), bf16[64,40,128]{2,1,0:T(8,128)(2,1)S(1)}, u32[]{:S(2)}, u32[]{:S(2)}) async-start(bf16[64,40,128]{2,1,0:T(8,128)(2,1)} %bitcast.16), calls=%async_computation.3 | async-start | bytes 1310720 | tf_op jit(solution)/shard_map/all_to_all | solution.py:13
  142.7 29.5 %all-to-all-start.4 = ((bf16[64,16,256]{2,1,0:T(8,128)(2,1)}), bf16[64,16,256]{2,1,0:T(8,128)(2,1)S(1)}, u32[]{:S(2)}, u32[]{:S(2)}) async-start(bf16[64,16,256]{2,1,0:T(8,128)(2,1)} %bitcast.20), calls=%async_computation.4 | async-start | bytes 1048576 | tf_op jit(solution)/shard_map/all_to_all | solution.py:13
  154.7 20.4 %copy-start.6 = (f32[2,8]{1,0:T(2,128)}, f32[2,8]{1,0:T(2,128)S(1)}, u32[]{:S(2)}) copy-start(f32[2,8]{1,0:T(2,128)S(1)} %get-tuple-element.8) | copy-start | bytes 196
  154.7 20.4 %copy-start.7 = (f32[2,8]{1,0:T(2,128)}, f32[2,8]{1,0:T(2,128)S(1)}, u32[]{:S(2)}) copy-start(f32[2,8]{1,0:T(2,128)S(1)} %sub.54) | copy-start | bytes 196
Sparse Core Ops, SparseCore 0:
  31.7 67.8 all-gather.3
  102.3 37.0 all-gather.5

commit v2 on v1

v2 whole, which is shorter than its diff:
```python
import jax
import jax.numpy as jnp
from jax import lax
from jax.sharding import Mesh, PartitionSpec as P

QGROUP = 128
F = ("y", "x", "core")
ZQ = ("rep", "x", "core")
Q = ("x", "core")
YX = ("y", "x")


def exchange(blocks, axes):
    return lax.all_to_all(blocks, axes, split_axis=0, concat_axis=0, tiled=True)


def shift(block, axis, size, by):
    return lax.ppermute(block, axis, [(i, (i + by) % size) for i in range(size)])


def around(block, axis):
    up, down = [block], [block]
    for _ in range(3):
        up.append(shift(up[-1], axis, 8, 1))
        down.append(shift(down[-1], axis, 8, -1))
    up.append(shift(up[-1], axis, 8, 1))
    return up + down[:0:-1]


def pieces(values):
    first = lax.reduce_precision(values, 8, 7)
    rest = values - first
    second = lax.reduce_precision(rest, 8, 7)
    third = rest - second
    return jnp.stack([first, second, third]).astype(jnp.bfloat16)


def on_device(grads, params, left_basis, right_basis, moment, codes, level_low, level_span):
    bf16, f32 = jnp.bfloat16, jnp.float32
    core = lax.axis_index("core")
    y = lax.axis_index("y")
    pick = lambda values, at: lax.dynamic_index_in_dim(values, at, 0, keepdims=False)

    def own_layer(own, other):
        return jnp.where(core == 0, jnp.concatenate([own, other], -2), jnp.concatenate([other, own], -2))

    bases = jnp.stack([right_basis, left_basis], axis=1)
    bases = jnp.broadcast_to(bases[None], (4, 2, 2, 16, 1024)).reshape(8, 2, 16, 1024)
    bases = exchange(bases, Q)
    right_y = bases[:, 0].reshape(128, 1024)
    left_y = bases[:, 1].reshape(128, 1024)

    sent = grads[0].reshape(2, 16, 8, 4, 256).transpose(2, 3, 0, 1, 4).reshape(64, 16, 256)
    got = exchange(sent, ZQ).reshape(8, 128, 256)
    grad16 = jnp.sum(got.astype(f32), axis=0).astype(bf16)
    part = jnp.einsum("ki,kj->ij", left_y, grad16, preferred_element_type=f32).astype(bf16)

    right = jnp.concatenate(around(right_y, "y"), axis=0)
    state = jnp.stack([moment, codes.astype(f32)], axis=1)
    state = own_layer(pick(state, core), shift(pick(state, 1 - core), "core", 2, 1))

    got = exchange(part.reshape(32, 32, 256), YX).reshape(8, 4, 32, 256)
    turned = jnp.sum(got.astype(f32), axis=0).transpose(1, 0, 2).reshape(32, 8, 128).astype(bf16)
    order = jnp.mod(y - jnp.arange(8), 8)
    turned = jnp.take(turned, order, axis=1).reshape(32, 1024)

    rotated = jnp.einsum("ik,kj->ij", turned, right, preferred_element_type=f32)
    low, span = pick(level_low, core), pick(level_span, core)

    def second_of(code_values, rotated, low, span):
        second = low[..., None, :, None] + code_values / 15.0 * span[..., None, :, None]
        return 0.95 * second + 0.05 * rotated * rotated

    second_new = second_of(state[1].reshape(32, 8, QGROUP), rotated.reshape(32, 8, QGROUP), low, span)
    moment_mid = 0.9 * state[0] + 0.1 * rotated
    scaled = (moment_mid / (jnp.sqrt(second_new.reshape(32, 1024)) + 1e-08)).astype(bf16)
    returned = jnp.einsum("ik,jk->ij", scaled, right, preferred_element_type=f32).astype(bf16)
    returned = jnp.take(returned.reshape(32, 8, 128), order, axis=1)

    ends = jnp.stack([jnp.min(second_new, axis=(0, 2)), jnp.max(second_new, axis=(0, 2))])
    row = jnp.pad(pieces(ends).reshape(1, 48), ((0, 7), (0, 80)))
    block = returned.reshape(32, 4, 2, 128).transpose(1, 2, 0, 3).reshape(4, 64, 128)
    block = jnp.concatenate([block, jnp.broadcast_to(row, (4, 8, 128))], axis=1)
    got = exchange(jnp.broadcast_to(block[None], (8, 4, 72, 128)).reshape(32, 72, 128), YX)
    back = got[:, :64].reshape(32, 2, 32, 128).transpose(0, 2, 1, 3).reshape(1024, 256)
    ends = got[:, 64, :48].astype(f32).reshape(32, 3, 2, 8)
    ends = (ends[:, 0] + ends[:, 1]) + ends[:, 2]
    ends = jnp.stack([jnp.min(ends[:, 0], axis=0), jnp.max(ends[:, 1], axis=0)])

    moved = jnp.einsum("ki,ij->kj", left_y, back, preferred_element_type=f32).astype(bf16)
    moved = jnp.broadcast_to(moved.reshape(1, 8, 16, 256), (8, 8, 16, 256)).reshape(64, 16, 256)
    got = exchange(moved, ZQ).reshape(8, 4, 2, 16, 256)

    rotated = rotated.reshape(2, 16, 1024)
    here, there = pick(rotated, core), shift(pick(rotated, 1 - core), "core", 2, 1)
    both = lambda here, there: jnp.where(core == 0, jnp.stack([here, there]), jnp.stack([there, here]))
    rotated = both(here, there)
    ends = both(ends, shift(ends, "core", 2, 1))
    low_new = ends[:, 0]
    span_new = ends[:, 1] - low_new
    moment_new = 0.9 * moment + 0.1 * rotated
    second_new = second_of(
        codes.astype(f32).reshape(2, 16, 8, QGROUP), rotated.reshape(2, 16, 8, QGROUP), level_low, level_span
    )
    levels = 15.0 * (second_new - low_new[:, None, :, None]) / span_new[:, None, :, None]
    levels = levels.reshape(2, 16, 1024)

    rep = lax.axis_index("rep")
    update = pick(got, rep).transpose(1, 2, 0, 3).reshape(2, 16, 1024).astype(f32)
    every = got.transpose(2, 3, 0, 1, 4).reshape(2, 16, 8192).astype(f32)
    olds = jnp.take(jnp.stack(around(params, "rep")), jnp.mod(rep - jnp.arange(8), 8), axis=0)
    old = olds.transpose(1, 2, 0, 3).reshape(2, 16, 8192).astype(f32)
    params_new = (old * (1.0 - 0.05 * 0.1) - 0.05 * every).astype(bf16)
    return (params_new, moment_new, update, levels, low_new, span_new)


def solution(mesh):
    fine = Mesh(mesh.devices.reshape(8, 8, 4, 2), ("rep", "y", "x", "core"))
    return jax.shard_map(
        on_device,
        mesh=fine,
        in_specs=(
            P("rep", None, F, None),
            P(None, F, "rep"),
            P(None, F, None),
            P(None, ("rep",) + F, None),
            P(None, F, "rep"),
            P(None, F, "rep"),
            P(None, "rep"),
            P(None, "rep"),
        ),
        out_specs=(
            P(None, F, None),
            P(None, F, "rep"),
            P(None, F, "rep"),
            P(None, F, "rep"),
            P(None, "rep"),
            P(None, "rep"),
        ),
        check_vma=False,
    )
```

time: 183 us -> 174 us (0.951)
  starting transfers between devices: 39.2 us -> 96.8 us
  waiting for transfers between devices: 85.7 us -> 37.9 us
  blocking collectives: 21.5 us -> 0 us
  local copies, waits for them, and re-layouts: 10.8 us -> 25.4 us
  between operations: 14.4 us -> 1.38 us
  other arithmetic: 2.68 us -> 8.54 us
  matrix products: 7.63 us -> 2.63 us
    ppermute x0 -> x17, starting transfers between devices: none -> 59.3 us  [shift(): lax.ppermute(block, axis, [(i, (i + by) % size) for i in range(size)])]
    all_to_all x4 -> x5, waiting for transfers between devices: 56.5 us -> 25.3 us  [exchange(): return lax.all_to_all(blocks, axes, split_axis=0, concat_axis=0, tiled=True)]
    all_gather x2 -> x0, waiting for transfers between devices: 29.1 us -> none  [the longest x1 24 us: on_device(): params_all = lax.all_gather(doubled, 'rep', axis=0)[:, :2]]
    all_to_all x1 -> x0, blocking collectives: 21.5 us -> none  [exchange(): return lax.all_to_all(blocks, axes, split_axis=0, concat_axis=0, tiled=True)]
    ppermute x0 -> x17, waiting for transfers between devices: none -> 12.6 us  [shift(): lax.ppermute(block, axis, [(i, (i + by) % size) for i in range(size)])]
    unnamed x24 -> x50, local copies, waits for them, and re-layouts: 0.35 us -> 12.9 us
    dot_general x2, matrix products: 6.28 us -> 1.26 us  [the longest x1 0.72 us: on_device(): jnp.einsum('ik,jk->ij', scaled, right, preferred_element_type=f32)]
    gather x0 -> x3, local copies, waits for them, and re-layouts: none -> 3.11 us  [the longest x1 1.74 us: on_device(): jnp.take(jnp.stack(around(params, 'rep')), jnp.mod(rep - jnp.arange(8), 8...]
  transfers between devices with their start and end apart: 6 -> 22, of which waited for: 5 -> 6; matrix products, arithmetic and copies ran while one was open for 8% -> 17% of each run, Pallas kernels for 0% -> 0%
where the time goes in v2:
time: 174 us; the launch traced here: 173 us
  starting transfers between devices  96.8 us (56%)
  waiting for transfers between devices  37.9 us (22%)
  local copies, waits for them, and re-layouts  25.4 us (15%)
  other arithmetic  8.54 us (5%)
  matrix products  2.63 us (2%)
    ppermute x17, starting transfers between devices, shift(): lax.ppermute(block, axis, [(i, (i + by) % size) for i in range(size)])  59.3 us
    all_to_all x5, starting transfers between devices, exchange(): return lax.all_to_all(blocks, axes, split_axis=0, concat_axis=0, tiled=True)  37.5 us
    all_to_all x5, waiting for transfers between devices, exchange(): return lax.all_to_all(blocks, axes, split_axis=0, concat_axis=0, tiled=True)  25.3 us
    unnamed x50, local copies, waits for them, and re-layouts  12.9 us
    ppermute x17, waiting for transfers between devices, shift(): lax.ppermute(block, axis, [(i, (i + by) % size) for i in range(size)])  12.6 us
  transfers between devices with their start and end apart: 22, of which 6 were waited for; matrix products, arithmetic and copies ran while one was open for 17% of the time, Pallas kernels for 0%

profile of v2, /device:TPU:1, one launch (start us, length us, event | category | flops | bytes accessed | tf_op | source)
XLA Modules:
  0.0 172.6 jit_solution(10007404332668190429)
XLA Ops:
  0.7 5.0 %collective-permute-start = (bf16[2,16,1024]{2,1,0:T(8,128)(2,1)}, bf16[2,16,1024]{2,1,0:T(8,128)(2,1)S(1)}, u32[]{:S(2)}, u32[]{:S(2)}) collective-permute-start(bf16[2,16,1024]{2,1,0:T(8,128)(2,1)} %param.11), channel_id=1, source_target_pairs={{0,64},{64,128},{128,192},{192,256},{256,320},{320,384},{384,448},... | collective-permute-start | bytes 196616 | tf_op jit(solution)/shard_map/ppermute | solution.py:18
  5.6 8.6 %collective-permute-start.4 = (bf16[2,16,1024]{2,1,0:T(8,128)(2,1)}, bf16[2,16,1024]{2,1,0:T(8,128)(2,1)S(1)}, u32[]{:S(2)}, u32[]{:S(2)}) collective-permute-start(bf16[2,16,1024]{2,1,0:T(8,128)(2,1)} %param.11), channel_id=1, source_target_pairs={{0,448},{64,0},{128,64},{192,128},{256,192},{320,256},{384,320},{4... | collective-permute-start | bytes 196616 | tf_op jit(solution)/shard_map/ppermute | solution.py:18
  16.1 2.9 %collective-permute-start.7 = (f32[2,16,1024]{2,1,0:T(8,128)S(1)}, f32[2,16,1024]{2,1,0:T(8,128)S(1)}, u32[]{:S(2)}, u32[]{:S(2)}) collective-permute-start(f32[2,16,1024]{2,1,0:T(8,128)S(1)} %get-tuple-element.14), channel_id=1, source_target_pairs={{0,1},{1,0},{2,3},{3,2},{4,5},{5,4},{6,7},{7,6},{8,9},{9,8},{10,11... | collective-permute-start | bytes 393224 | tf_op jit(solution)/shard_map/ppermute | solution.py:18
  20.7 4.4 %all-to-all-start = ((bf16[8,2,16,1024]{3,2,1,0:T(8,128)(2,1)}), bf16[8,2,16,1024]{3,2,1,0:T(8,128)(2,1)S(1)}, u32[]{:S(2)}, u32[]{:S(2)}) async-start(bf16[8,2,16,1024]{3,2,1,0:T(8,128)(2,1)} %bitcast.12), calls=%async_computation | async-start | bytes 1048576 | tf_op jit(solution)/shard_map/all_to_all | solution.py:14
  29.4 5.2 %all-to-all-done = bf16[8,2,16,1024]{3,2,1,0:T(8,128)(2,1)S(1)} async-done(((bf16[8,2,16,1024]{3,2,1,0:T(8,128)(2,1)}), bf16[8,2,16,1024]{3,2,1,0:T(8,128)(2,1)S(1)}, u32[]{:S(2)}, u32[]{:S(2)}) %all-to-all-start) | async-done | bytes 524320 | tf_op jit(solution)/shard_map/all_to_all | solution.py:14
  34.6 6.5 %all-to-all-start.1 = ((bf16[64,16,256]{2,1,0:T(8,128)(2,1)}), bf16[64,16,256]{2,1,0:T(8,128)(2,1)S(1)}, u32[]{:S(2)}, u32[]{:S(2)}) async-start(bf16[64,16,256]{2,1,0:T(8,128)(2,1)} %bitcast.20), calls=%async_computation.1 | async-start | bytes 1048576 | tf_op jit(solution)/shard_map/all_to_all | solution.py:14
  41.7 3.2 %collective-permute-start.8 = (bf16[128,1024]{1,0:T(8,128)(2,1)S(1)}, bf16[128,1024]{1,0:T(8,128)(2,1)S(1)}, u32[]{:S(2)}, u32[]{:S(2)}) collective-permute-start(bf16[128,1024]{1,0:T(8,128)(2,1)S(1)} %bitcast.179), channel_id=1, source_target_pairs={{0,8},{8,16},{16,24},{24,32},{32,40},{40,48},{48,56},{56,0},{1,9},... | collective-permute-start | bytes 786440 | tf_op jit(solution)/shard_map/ppermute | solution.py:18
  45.4 3.3 %collective-permute-start.1 = (bf16[2,16,1024]{2,1,0:T(8,128)(2,1)S(1)}, bf16[2,16,1024]{2,1,0:T(8,128)(2,1)S(1)}, u32[]{:S(2)}, u32[]{:S(2)}) collective-permute-start(bf16[2,16,1024]{2,1,0:T(8,128)(2,1)S(1)} %collective-permute-done), channel_id=1, source_target_pairs={{0,64},{64,128},{128,192},{192,256},{256,320},{320,384},{384,448},... | collective-permute-start | bytes 196616 | tf_op jit(solution)/shard_map/ppermute | solution.py:18
  48.8 3.4 %collective-permute-start.5 = (bf16[2,16,1024]{2,1,0:T(8,128)(2,1)S(1)}, bf16[2,16,1024]{2,1,0:T(8,128)(2,1)}, u32[]{:S(2)}, u32[]{:S(2)}) collective-permute-start(bf16[2,16,1024]{2,1,0:T(8,128)(2,1)S(1)} %collective-permute-done.4), channel_id=1, source_target_pairs={{0,448},{64,0},{128,64},{192,128},{256,192},{320,256},{384,320},{4... | collective-permute-start | bytes 196616 | tf_op jit(solution)/shard_map/ppermute | solution.py:18
  52.8 4.1 %collective-permute-done.1 = bf16[2,16,1024]{2,1,0:T(8,128)(2,1)S(1)} collective-permute-done((bf16[2,16,1024]{2,1,0:T(8,128)(2,1)S(1)}, bf16[2,16,1024]{2,1,0:T(8,128)(2,1)S(1)}, u32[]{:S(2)}, u32[]{:S(2)}) %collective-permute-start.1) | collective-permute-done | bytes 65568 | tf_op jit(solution)/shard_map/ppermute | solution.py:18
  56.9 1.9 %collective-permute-start.2 = (bf16[2,16,1024]{2,1,0:T(8,128)(2,1)S(1)}, bf16[2,16,1024]{2,1,0:T(8,128)(2,1)}, u32[]{:S(2)}, u32[]{:S(2)}) collective-permute-start(bf16[2,16,1024]{2,1,0:T(8,128)(2,1)S(1)} %collective-permute-done.1), channel_id=1, source_target_pairs={{0,64},{64,128},{128,192},{192,256},{256,320},{320,384},{384,448},... | collective-permute-start | bytes 196616 | tf_op jit(solution)/shard_map/ppermute | solution.py:18
  58.8 4.6 %collective-permute-start.6 = (bf16[2,16,1024]{2,1,0:T(8,128)(2,1)}, bf16[2,16,1024]{2,1,0:T(8,128)(2,1)}, u32[]{:S(2)}, u32[]{:S(2)}) collective-permute-start(bf16[2,16,1024]{2,1,0:T(8,128)(2,1)} %collective-permute-done.5), channel_id=1, source_target_pairs={{0,448},{64,0},{128,64},{192,128},{256,192},{320,256},{384,320},{4... | collective-permute-start | bytes 196616 | tf_op jit(solution)/shard_map/ppermute | solution.py:18
  63.4 5.1 %collective-permute-start.12 = (bf16[128,1024]{1,0:T(8,128)(2,1)S(1)}, bf16[128,1024]{1,0:T(8,128)(2,1)}, u32[]{:S(2)}, u32[]{:S(2)}) collective-permute-start(bf16[128,1024]{1,0:T(8,128)(2,1)S(1)} %bitcast.180), channel_id=1, source_target_pairs={{0,56},{8,0},{16,8},{24,16},{32,24},{40,32},{48,40},{56,48},{1,57}... | collective-permute-start | bytes 786440 | tf_op jit(solution)/shard_map/ppermute | solution.py:18
  68.5 1.9 %collective-permute-start.9 = (bf16[128,1024]{1,0:T(8,128)(2,1)S(1)}, bf16[128,1024]{1,0:T(8,128)(2,1)}, u32[]{:S(2)}, u32[]{:S(2)}) collective-permute-start(bf16[128,1024]{1,0:T(8,128)(2,1)S(1)} %collective-permute-done.8), channel_id=1, source_target_pairs={{0,8},{8,16},{16,24},{24,32},{32,40},{40,48},{48,56},{56,0},{1,9},... | collective-permute-start | bytes 786440 | tf_op jit(solution)/shard_map/ppermute | solution.py:18
  71.1 1.9 %collective-permute-start.3 = (bf16[2,16,1024]{2,1,0:T(8,128)(2,1)}, bf16[2,16,1024]{2,1,0:T(8,128)(2,1)}, u32[]{:S(2)}, u32[]{:S(2)}) collective-permute-start(bf16[2,16,1024]{2,1,0:T(8,128)(2,1)} %collective-permute-done.2), channel_id=1, source_target_pairs={{0,64},{64,128},{128,192},{192,256},{256,320},{320,384},{384,448},... | collective-permute-start | bytes 196616 | tf_op jit(solution)/shard_map/ppermute | solution.py:18
  73.1 4.8 %collective-permute-start.13 = (bf16[128,1024]{1,0:T(8,128)(2,1)}, bf16[128,1024]{1,0:T(8,128)(2,1)}, u32[]{:S(2)}, u32[]{:S(2)}) collective-permute-start(bf16[128,1024]{1,0:T(8,128)(2,1)} %collective-permute-done.12), channel_id=1, source_target_pairs={{0,56},{8,0},{16,8},{24,16},{32,24},{40,32},{48,40},{56,48},{1,57}... | collective-permute-start | bytes 786440 | tf_op jit(solution)/shard_map/ppermute | solution.py:18
  77.9 1.9 %collective-permute-start.10 = (bf16[128,1024]{1,0:T(8,128)(2,1)}, bf16[128,1024]{1,0:T(8,128)(2,1)}, u32[]{:S(2)}, u32[]{:S(2)}) collective-permute-start(bf16[128,1024]{1,0:T(8,128)(2,1)} %collective-permute-done.9), channel_id=1, source_target_pairs={{0,8},{8,16},{16,24},{24,32},{32,40},{40,48},{48,56},{56,0},{1,9},... | collective-permute-start | bytes 786440 | tf_op jit(solution)/shard_map/ppermute | solution.py:18
  81.1 6.5 %all-to-all-start.2 = ((bf16[32,32,256]{2,1,0:T(8,128)(2,1)}), bf16[32,32,256]{2,1,0:T(8,128)(2,1)S(1)}, u32[]{:S(2)}, u32[]{:S(2)}) async-start(bf16[32,32,256]{2,1,0:T(8,128)(2,1)} %bitcast.22), calls=%async_computation.2 | async-start | bytes 1048576 | tf_op jit(solution)/shard_map/all_to_all | solution.py:14
  87.5 1.5 bitcast_dynamic-update-slice_fusion.4
  89.0 3.1 %collective-permute-start.11 = (bf16[128,1024]{1,0:T(8,128)(2,1)}, bf16[128,1024]{1,0:T(8,128)(2,1)S(1)}, u32[]{:S(2)}, u32[]{:S(2)}) collective-permute-start(bf16[128,1024]{1,0:T(8,128)(2,1)} %collective-permute-done.10), channel_id=1, source_target_pairs={{0,8},{8,16},{16,24},{24,32},{32,40},{40,48},{48,56},{56,0},{1,9},... | collective-permute-start | bytes 786440 | tf_op jit(solution)/shard_map/ppermute | solution.py:18
  93.2 3.4 %collective-permute-start.14 = (bf16[128,1024]{1,0:T(8,128)(2,1)}, bf16[128,1024]{1,0:T(8,128)(2,1)S(1)}, u32[]{:S(2)}, u32[]{:S(2)}) collective-permute-start(bf16[128,1024]{1,0:T(8,128)(2,1)} %collective-permute-done.13), channel_id=1, source_target_pairs={{0,56},{8,0},{16,8},{24,16},{32,24},{40,32},{48,40},{56,48},{1,57}... | collective-permute-start | bytes 786440 | tf_op jit(solution)/shard_map/ppermute | solution.py:18
  98.5 7.5 %collective-permute-done.11 = bf16[128,1024]{1,0:T(8,128)(2,1)S(1)} collective-permute-done((bf16[128,1024]{1,0:T(8,128)(2,1)}, bf16[128,1024]{1,0:T(8,128)(2,1)S(1)}, u32[]{:S(2)}, u32[]{:S(2)}) %collective-permute-start.11) | collective-permute-done | bytes 262176 | tf_op jit(solution)/shard_map/ppermute | solution.py:18
  112.3 7.5 %all-to-all-start.3 = ((bf16[32,72,128]{2,1,0:T(8,128)(2,1)}), bf16[32,72,128]{2,1,0:T(8,128)(2,1)S(1)}, u32[]{:S(2)}, u32[]{:S(2)}) async-start(bf16[32,72,128]{2,1,0:T(8,128)(2,1)} %bitcast.41), calls=%async_computation.3 | async-start | bytes 1179648 | tf_op jit(solution)/shard_map/all_to_all | solution.py:14
  119.9 1.5 bitcast_dynamic-update-slice_fusion.3
  121.4 1.5 bitcast_dynamic-update-slice_fusion.2
  122.8 1.5 bitcast_dynamic-update-slice_fusion.1
  124.9 1.7 %gather_fusion = bf16[8,2,16,1024]{3,2,1,0:T(8,128)(2,1)S(1)} fusion(bf16[8,2,16,1024]{3,2,1,0:T(8,128)(2,1)} %bitcast_dynamic-update-slice_fusion, s32[1024]{0:T(1024)} %pad_clamp_fusion.1), kind=kCustom, calls=%fused_computation.2 | custom fusion | bytes 1048608 | tf_op jit(solution)/shard_map/jit(_take)/gather | solution.py:111
  127.0 8.7 %all-to-all-done.3 = bf16[32,72,128]{2,1,0:T(8,128)(2,1)S(1)} async-done(((bf16[32,72,128]{2,1,0:T(8,128)(2,1)}), bf16[32,72,128]{2,1,0:T(8,128)(2,1)S(1)}, u32[]{:S(2)}, u32[]{:S(2)}) %all-to-all-start.3) | async-done | bytes 589856 | tf_op jit(solution)/shard_map/all_to_all | solution.py:14
  137.7 12.6 %all-to-all-start.4 = ((bf16[64,16,256]{2,1,0:T(8,128)(2,1)}), bf16[64,16,256]{2,1,0:T(8,128)(2,1)S(1)}, u32[]{:S(2)}, u32[]{:S(2)}) async-start(bf16[64,16,256]{2,1,0:T(8,128)(2,1)} %bitcast.45), calls=%async_computation.4 | async-start | bytes 1048576 | tf_op jit(solution)/shard_map/all_to_all | solution.py:14
  150.3 2.4 %collective-permute-start.16 = (f32[2,8]{1,0:T(2,128)S(1)}, f32[2,8]{1,0:T(2,128)S(1)}, u32[]{:S(2)}, u32[]{:S(2)}) collective-permute-start(f32[2,8]{1,0:T(2,128)S(1)} %get-tuple-element.22), channel_id=1, source_target_pairs={{0,1},{1,0},{2,3},{3,2},{4,5},{5,4},{6,7},{7,6},{8,9},{9,8},{10,11... | collective-permute-start | bytes 200 | tf_op jit(solution)/shard_map/ppermute | solution.py:18
  152.7 2.0 %collective-permute-start.15 = (f32[16,1024]{1,0:T(8,128)S(1)}, f32[16,1024]{1,0:T(8,128)S(1)}, u32[]{:S(2)}, u32[]{:S(2)}) collective-permute-start(f32[16,1024]{1,0:T(8,128)S(1)} %get-tuple-element.17), channel_id=1, source_target_pairs={{0,1},{1,0},{2,3},{3,2},{4,5},{5,4},{6,7},{7,6},{8,9},{9,8},{10,11... | collective-permute-start | bytes 196616 | tf_op jit(solution)/shard_map/ppermute | solution.py:18
  156.6 11.4 %all-to-all-done.4 = bf16[64,16,256]{2,1,0:T(8,128)(2,1)S(1)} async-done(((bf16[64,16,256]{2,1,0:T(8,128)(2,1)}), bf16[64,16,256]{2,1,0:T(8,128)(2,1)S(1)}, u32[]{:S(2)}, u32[]{:S(2)}) %all-to-all-start.4) | async-done | bytes 524320 | tf_op jit(solution)/shard_map/all_to_all | solution.py:14
  (129 shorter events, 29.9 us)
Async XLA Ops:
  0.6 24.5 %copy-start.12 = (f32[2,8]{1,0:T(2,128)S(1)}, f32[2,8]{1,0:T(2,128)}, u32[]{:S(2)}) copy-start(f32[2,8]{1,0:T(2,128)} %param.17) | copy-start | bytes 196
  0.6 24.5 %copy-start.11 = (f32[2,8]{1,0:T(2,128)S(1)}, f32[2,8]{1,0:T(2,128)}, u32[]{:S(2)}) copy-start(f32[2,8]{1,0:T(2,128)} %param.16) | copy-start | bytes 196
  0.7 26.0 %copy-start.1 = (bf16[1,2,16,8192]{3,2,1,0:T(8,128)(2,1)S(1)}, bf16[1,2,16,8192]{3,2,1,0:T(8,128)(2,1)}, u32[]{:S(2)}) copy-start(bf16[1,2,16,8192]{3,2,1,0:T(8,128)(2,1)} %param.10) | copy-start | bytes 1572868
  0.7 44.8 %collective-permute-start = (bf16[2,16,1024]{2,1,0:T(8,128)(2,1)}, bf16[2,16,1024]{2,1,0:T(8,128)(2,1)S(1)}, u32[]{:S(2)}, u32[]{:S(2)}) collective-permute-start(bf16[2,16,1024]{2,1,0:T(8,128)(2,1)} %param.11), channel_id=1, source_target_pairs={{0,64},{64,128},{128,192},{192,256},{256,320},{320,384},{384,448},... | collective-permute-start | bytes 196616 | tf_op jit(solution)/shard_map/ppermute | solution.py:18
  5.6 43.1 %collective-permute-start.4 = (bf16[2,16,1024]{2,1,0:T(8,128)(2,1)}, bf16[2,16,1024]{2,1,0:T(8,128)(2,1)S(1)}, u32[]{:S(2)}, u32[]{:S(2)}) collective-permute-start(bf16[2,16,1024]{2,1,0:T(8,128)(2,1)} %param.11), channel_id=1, source_target_pairs={{0,448},{64,0},{128,64},{192,128},{256,192},{320,256},{384,320},{4... | collective-permute-start | bytes 196616 | tf_op jit(solution)/shard_map/ppermute | solution.py:18
  16.1 55.0 %collective-permute-start.7 = (f32[2,16,1024]{2,1,0:T(8,128)S(1)}, f32[2,16,1024]{2,1,0:T(8,128)S(1)}, u32[]{:S(2)}, u32[]{:S(2)}) collective-permute-start(f32[2,16,1024]{2,1,0:T(8,128)S(1)} %get-tuple-element.14), channel_id=1, source_target_pairs={{0,1},{1,0},{2,3},{3,2},{4,5},{5,4},{6,7},{7,6},{8,9},{9,8},{10,11... | collective-permute-start | bytes 393224 | tf_op jit(solution)/shard_map/ppermute | solution.py:18
  20.7 13.9 %all-to-all-start = ((bf16[8,2,16,1024]{3,2,1,0:T(8,128)(2,1)}), bf16[8,2,16,1024]{3,2,1,0:T(8,128)(2,1)S(1)}, u32[]{:S(2)}, u32[]{:S(2)}) async-start(bf16[8,2,16,1024]{3,2,1,0:T(8,128)(2,1)} %bitcast.12), calls=%async_computation | async-start | bytes 1048576 | tf_op jit(solution)/shard_map/all_to_all | solution.py:14
  34.6 45.2 %all-to-all-start.1 = ((bf16[64,16,256]{2,1,0:T(8,128)(2,1)}), bf16[64,16,256]{2,1,0:T(8,128)(2,1)S(1)}, u32[]{:S(2)}, u32[]{:S(2)}) async-start(bf16[64,16,256]{2,1,0:T(8,128)(2,1)} %bitcast.20), calls=%async_computation.1 | async-start | bytes 1048576 | tf_op jit(solution)/shard_map/all_to_all | solution.py:14
  41.7 26.8 %collective-permute-start.8 = (bf16[128,1024]{1,0:T(8,128)(2,1)S(1)}, bf16[128,1024]{1,0:T(8,128)(2,1)S(1)}, u32[]{:S(2)}, u32[]{:S(2)}) collective-permute-start(bf16[128,1024]{1,0:T(8,128)(2,1)S(1)} %bitcast.179), channel_id=1, source_target_pairs={{0,8},{8,16},{16,24},{24,32},{32,40},{40,48},{48,56},{56,0},{1,9},... | collective-permute-start | bytes 786440 | tf_op jit(solution)/shard_map/ppermute | solution.py:18
  45.4 11.4 %collective-permute-start.1 = (bf16[2,16,1024]{2,1,0:T(8,128)(2,1)S(1)}, bf16[2,16,1024]{2,1,0:T(8,128)(2,1)S(1)}, u32[]{:S(2)}, u32[]{:S(2)}) collective-permute-start(bf16[2,16,1024]{2,1,0:T(8,128)(2,1)S(1)} %collective-permute-done), channel_id=1, source_target_pairs={{0,64},{64,128},{128,192},{192,256},{256,320},{320,384},{384,448},... | collective-permute-start | bytes 196616 | tf_op jit(solution)/shard_map/ppermute | solution.py:18
  48.7 38.8 %copy-start.6 = (bf16[2,16,1024]{2,1,0:T(8,128)(2,1)}, bf16[2,16,1024]{2,1,0:T(8,128)(2,1)S(1)}, u32[]{:S(2)}) copy-start(bf16[2,16,1024]{2,1,0:T(8,128)(2,1)S(1)} %collective-permute-done.4) | copy-start | bytes 196612
  48.8 10.0 %collective-permute-start.5 = (bf16[2,16,1024]{2,1,0:T(8,128)(2,1)S(1)}, bf16[2,16,1024]{2,1,0:T(8,128)(2,1)}, u32[]{:S(2)}, u32[]{:S(2)}) collective-permute-start(bf16[2,16,1024]{2,1,0:T(8,128)(2,1)S(1)} %collective-permute-done.4), channel_id=1, source_target_pairs={{0,448},{64,0},{128,64},{192,128},{256,192},{320,256},{384,320},{4... | collective-permute-start | bytes 196616 | tf_op jit(solution)/shard_map/ppermute | solution.py:18
  56.9 14.2 %collective-permute-start.2 = (bf16[2,16,1024]{2,1,0:T(8,128)(2,1)S(1)}, bf16[2,16,1024]{2,1,0:T(8,128)(2,1)}, u32[]{:S(2)}, u32[]{:S(2)}) collective-permute-start(bf16[2,16,1024]{2,1,0:T(8,128)(2,1)S(1)} %collective-permute-done.1), channel_id=1, source_target_pairs={{0,64},{64,128},{128,192},{192,256},{256,320},{320,384},{384,448},... | collective-permute-start | bytes 196616 | tf_op jit(solution)/shard_map/ppermute | solution.py:18
  58.8 62.5 %collective-permute-start.6 = (bf16[2,16,1024]{2,1,0:T(8,128)(2,1)}, bf16[2,16,1024]{2,1,0:T(8,128)(2,1)}, u32[]{:S(2)}, u32[]{:S(2)}) collective-permute-start(bf16[2,16,1024]{2,1,0:T(8,128)(2,1)} %collective-permute-done.5), channel_id=1, source_target_pairs={{0,448},{64,0},{128,64},{192,128},{256,192},{320,256},{384,320},{4... | collective-permute-start | bytes 196616 | tf_op jit(solution)/shard_map/ppermute | solution.py:18
  63.4 9.7 %collective-permute-start.12 = (bf16[128,1024]{1,0:T(8,128)(2,1)S(1)}, bf16[128,1024]{1,0:T(8,128)(2,1)}, u32[]{:S(2)}, u32[]{:S(2)}) collective-permute-start(bf16[128,1024]{1,0:T(8,128)(2,1)S(1)} %bitcast.180), channel_id=1, source_target_pairs={{0,56},{8,0},{16,8},{24,16},{32,24},{40,32},{48,40},{56,48},{1,57}... | collective-permute-start | bytes 786440 | tf_op jit(solution)/shard_map/ppermute | solution.py:18
  68.5 19.0 %copy-start.4 = (bf16[128,1024]{1,0:T(8,128)(2,1)}, bf16[128,1024]{1,0:T(8,128)(2,1)S(1)}, u32[]{:S(2)}) copy-start(bf16[128,1024]{1,0:T(8,128)(2,1)S(1)} %collective-permute-done.8) | copy-start | bytes 786436
  68.5 9.4 %collective-permute-start.9 = (bf16[128,1024]{1,0:T(8,128)(2,1)S(1)}, bf16[128,1024]{1,0:T(8,128)(2,1)}, u32[]{:S(2)}, u32[]{:S(2)}) collective-permute-start(bf16[128,1024]{1,0:T(8,128)(2,1)S(1)} %collective-permute-done.8), channel_id=1, source_target_pairs={{0,8},{8,16},{16,24},{24,32},{32,40},{40,48},{48,56},{56,0},{1,9},... | collective-permute-start | bytes 786440 | tf_op jit(solution)/shard_map/ppermute | solution.py:18
  71.1 48.7 %collective-permute-start.3 = (bf16[2,16,1024]{2,1,0:T(8,128)(2,1)}, bf16[2,16,1024]{2,1,0:T(8,128)(2,1)}, u32[]{:S(2)}, u32[]{:S(2)}) collective-permute-start(bf16[2,16,1024]{2,1,0:T(8,128)(2,1)} %collective-permute-done.2), channel_id=1, source_target_pairs={{0,64},{64,128},{128,192},{192,256},{256,320},{320,384},{384,448},... | collective-permute-start | bytes 196616 | tf_op jit(solution)/shard_map/ppermute | solution.py:18
  73.1 20.1 %collective-permute-start.13 = (bf16[128,1024]{1,0:T(8,128)(2,1)}, bf16[128,1024]{1,0:T(8,128)(2,1)}, u32[]{:S(2)}, u32[]{:S(2)}) collective-permute-start(bf16[128,1024]{1,0:T(8,128)(2,1)} %collective-permute-done.12), channel_id=1, source_target_pairs={{0,56},{8,0},{16,8},{24,16},{32,24},{40,32},{48,40},{56,48},{1,57}... | collective-permute-start | bytes 786440 | tf_op jit(solution)/shard_map/ppermute | solution.py:18
  77.9 11.1 %collective-permute-start.10 = (bf16[128,1024]{1,0:T(8,128)(2,1)}, bf16[128,1024]{1,0:T(8,128)(2,1)}, u32[]{:S(2)}, u32[]{:S(2)}) collective-permute-start(bf16[128,1024]{1,0:T(8,128)(2,1)} %collective-permute-done.9), channel_id=1, source_target_pairs={{0,8},{8,16},{16,24},{24,32},{32,40},{40,48},{48,56},{56,0},{1,9},... | collective-permute-start | bytes 786440 | tf_op jit(solution)/shard_map/ppermute | solution.py:18
  81.1 27.0 %all-to-all-start.2 = ((bf16[32,32,256]{2,1,0:T(8,128)(2,1)}), bf16[32,32,256]{2,1,0:T(8,128)(2,1)S(1)}, u32[]{:S(2)}, u32[]{:S(2)}) async-start(bf16[32,32,256]{2,1,0:T(8,128)(2,1)} %bitcast.22), calls=%async_computation.2 | async-start | bytes 1048576 | tf_op jit(solution)/shard_map/all_to_all | solution.py:14
  89.0 17.0 %collective-permute-start.11 = (bf16[128,1024]{1,0:T(8,128)(2,1)}, bf16[128,1024]{1,0:T(8,128)(2,1)S(1)}, u32[]{:S(2)}, u32[]{:S(2)}) collective-permute-start(bf16[128,1024]{1,0:T(8,128)(2,1)} %collective-permute-done.10), channel_id=1, source_target_pairs={{0,8},{8,16},{16,24},{24,32},{32,40},{40,48},{48,56},{56,0},{1,9},... | collective-permute-start | bytes 786440 | tf_op jit(solution)/shard_map/ppermute | solution.py:18
  93.2 15.8 %copy-start.13 = (pred[8]{0:T(512)(128)(4,1)S(1)}, pred[8]{0:T(512)(128)(4,1)}, u32[]{:S(2)}) copy-start(pred[8]{0:T(512)(128)(4,1)} %compare_and_fusion) | copy-start | bytes 28
  93.2 12.9 %collective-permute-start.14 = (bf16[128,1024]{1,0:T(8,128)(2,1)}, bf16[128,1024]{1,0:T(8,128)(2,1)S(1)}, u32[]{:S(2)}, u32[]{:S(2)}) collective-permute-start(bf16[128,1024]{1,0:T(8,128)(2,1)} %collective-permute-done.13), channel_id=1, source_target_pairs={{0,56},{8,0},{16,8},{24,16},{32,24},{40,32},{48,40},{56,48},{1,57}... | collective-permute-start | bytes 786440 | tf_op jit(solution)/shard_map/ppermute | solution.py:18
  110.2 16.5 %copy-start.14 = (pred[8]{0:T(512)(128)(4,1)S(1)}, pred[8]{0:T(512)(128)(4,1)}, u32[]{:S(2)}) copy-start(pred[8]{0:T(512)(128)(4,1)} %compare_and_fusion.1) | copy-start | bytes 28
  112.3 23.4 %all-to-all-start.3 = ((bf16[32,72,128]{2,1,0:T(8,128)(2,1)}), bf16[32,72,128]{2,1,0:T(8,128)(2,1)S(1)}, u32[]{:S(2)}, u32[]{:S(2)}) async-start(bf16[32,72,128]{2,1,0:T(8,128)(2,1)} %bitcast.41), calls=%async_computation.3 | async-start | bytes 1179648 | tf_op jit(solution)/shard_map/all_to_all | solution.py:14
  136.0 19.8 %copy-start.2 = (s32[2,16,1024]{2,1,0:T(8,128)S(1)}, s32[2,16,1024]{2,1,0:T(8,128)}, u32[]{:S(2)}) copy-start(s32[2,16,1024]{2,1,0:T(8,128)} %param.15) | copy-start | bytes 393220
  136.1 19.8 %copy-start.3 = (f32[2,16,1024]{2,1,0:T(8,128)S(1)}, f32[2,16,1024]{2,1,0:T(8,128)}, u32[]{:S(2)}) copy-start(f32[2,16,1024]{2,1,0:T(8,128)} %param.14) | copy-start | bytes 393220
  136.1 19.8 %copy-start.8 = (f32[2,1024]{1,0:T(2,128)S(1)}, f32[2,1024]{1,0:T(2,128)}, u32[]{:S(2)}) copy-start(f32[2,1024]{1,0:T(2,128)} %get-tuple-element.30) | copy-start | bytes 24580
  137.7 30.3 %all-to-all-start.4 = ((bf16[64,16,256]{2,1,0:T(8,128)(2,1)}), bf16[64,16,256]{2,1,0:T(8,128)(2,1)S(1)}, u32[]{:S(2)}, u32[]{:S(2)}) async-start(bf16[64,16,256]{2,1,0:T(8,128)(2,1)} %bitcast.45), calls=%async_computation.4 | async-start | bytes 1048576 | tf_op jit(solution)/shard_map/all_to_all | solution.py:14
  150.3 4.3 %collective-permute-start.16 = (f32[2,8]{1,0:T(2,128)S(1)}, f32[2,8]{1,0:T(2,128)S(1)}, u32[]{:S(2)}, u32[]{:S(2)}) collective-permute-start(f32[2,8]{1,0:T(2,128)S(1)} %get-tuple-element.22), channel_id=1, source_target_pairs={{0,1},{1,0},{2,3},{3,2},{4,5},{5,4},{6,7},{7,6},{8,9},{9,8},{10,11... | collective-permute-start | bytes 200 | tf_op jit(solution)/shard_map/ppermute | solution.py:18
  152.7 3.1 %collective-permute-start.15 = (f32[16,1024]{1,0:T(8,128)S(1)}, f32[16,1024]{1,0:T(8,128)S(1)}, u32[]{:S(2)}, u32[]{:S(2)}) collective-permute-start(f32[16,1024]{1,0:T(8,128)S(1)} %get-tuple-element.17), channel_id=1, source_target_pairs={{0,1},{1,0},{2,3},{3,2},{4,5},{5,4},{6,7},{7,6},{8,9},{9,8},{10,11... | collective-permute-start | bytes 196616 | tf_op jit(solution)/shard_map/ppermute | solution.py:18
  (5 other events, 54.4 us)

commit v3 on v1

v3 whole, which is shorter than its diff:
```python
import jax
import jax.numpy as jnp
from jax import lax
from jax.experimental import pallas as pl
from jax.experimental.pallas import tpu as pltpu
from jax.sharding import Mesh, PartitionSpec as P

QGROUP = 128
F = ("y", "x", "core")
ZQ = ("rep", "x", "core")
Q = ("x", "core")
YX = ("y", "x")
BF16, F32 = jnp.bfloat16, jnp.float32
VMEM = pl.BlockSpec(memory_space=pltpu.VMEM)
SMEM = pl.BlockSpec(memory_space=pltpu.SMEM)
ANY = pl.BlockSpec(memory_space=pl.ANY)


def shape(*dims, of=BF16):
    return jax.ShapeDtypeStruct(dims, of)


def exchange(blocks, axes):
    return lax.all_to_all(blocks, axes, split_axis=0, concat_axis=0, tiled=True)


def shift(block, axis, size, by):
    return lax.ppermute(block, axis, [(i, (i + by) % size) for i in range(size)])


def bases_kernel(right, left, out):
    for panel in range(4):
        out[panel, :, 0] = right[...]
        out[panel, :, 1] = left[...]


def bases_out(right, left):
    return pl.pallas_call(
        bases_kernel, out_shape=shape(4, 2, 2, 16, 1024), in_specs=[VMEM, VMEM], out_specs=VMEM
    )(right, left)


def panels_kernel(grads, out):
    for panel in range(32):
        out[panel] = grads[:, :, panel * 256 : panel * 256 + 256]


def panels(grads):
    return pl.pallas_call(
        panels_kernel, out_shape=shape(32, 2, 16, 256), in_specs=[VMEM], out_specs=VMEM
    )(grads)


def left_kernel(grads, left, out):
    total = grads[0].astype(F32)
    for replica in range(1, 8):
        total += grads[replica].astype(F32)
    part = lax.dot_general(
        left[...], total.astype(BF16), (((0,), (0,)), ((), ())), preferred_element_type=F32
    )
    out[...] = part.astype(BF16)


def left_part(grads, left):
    return pl.pallas_call(
        left_kernel, out_shape=shape(1024, 256), in_specs=[VMEM, VMEM], out_specs=VMEM
    )(grads, left)


def middle_kernel(
    got, own, far, up, down, more, moment, codes, state, low, span, out, mine, others, right, rotated, scaled, sems
):
    core, at = lax.axis_index("core"), lax.axis_index("y")
    ring = [own, up.at[0], more.at[0], down.at[1], far, up.at[1], more.at[1], down.at[0]]
    copies = []
    for back, block in enumerate(ring):
        place = lax.rem(at + 8 - back, 8)
        copies.append(pltpu.make_async_copy(block, right.at[place], sems.at[back]))
    for copy in copies:
        copy.start()
    turned = []
    for panel in range(4):
        total = got[0, panel].astype(F32)
        for part in range(1, 8):
            total += got[part, panel].astype(F32)
        turned.append(total.astype(BF16))
    turned = jnp.concatenate(turned, axis=1)
    for copy in copies:
        copy.wait()
    basis = right[...].reshape(1024, 1024)
    rotated[...] = jnp.dot(turned, basis, preferred_element_type=F32)
    here = pl.ds(pl.multiple_of(core * 16, 16), 16)
    there = pl.ds(pl.multiple_of((1 - core) * 16, 16), 16)
    mine[...] = rotated[here, :]
    others[...] = rotated[there, :]
    lows, highs = [], []
    for group in range(8):
        lanes = slice(group * 128, group * 128 + 128)
        base, width = low[core, group], span[core, group]
        ends = []
        for rows, mean, code in (
            (here, moment[core, :, lanes], codes[core, :, lanes].astype(F32)),
            (there, state[0, :, lanes], state[1, :, lanes]),
        ):
            turn = rotated[rows, lanes]
            second = 0.95 * (base + code / 15.0 * width) + 0.05 * turn * turn
            mean = 0.9 * mean + 0.1 * turn
            scaled[rows, lanes] = mean / (jnp.sqrt(second) + 1e-08)
            ends.append(second)
        lows.append(jnp.min(jnp.minimum(*ends), axis=0, keepdims=True))
        highs.append(jnp.max(jnp.maximum(*ends), axis=0, keepdims=True))
    returned = lax.dot_general(
        scaled[...].astype(BF16), basis, (((1,), (1,)), ((), ())), preferred_element_type=F32
    ).astype(BF16)
    ends = jnp.concatenate(
        [
            jnp.min(jnp.concatenate(lows, axis=0), axis=1, keepdims=True),
            jnp.max(jnp.concatenate(highs, axis=0), axis=1, keepdims=True),
        ],
        axis=0,
    )
    first = ends.astype(BF16).astype(F32)
    second = (ends - first).astype(BF16).astype(F32)
    third = ends - first - second
    lane = lax.broadcasted_iota(jnp.int32, (16, 128), 1)
    tile = jnp.where(lane == 0, first, jnp.where(lane == 1, second, jnp.where(lane == 2, third, 0.0)))
    tile = tile.astype(BF16)
    for panel in range(4):
        start = panel * 256
        for copy in range(8):
            out[copy, panel, 0:32] = returned[:, start : start + 128]
            out[copy, panel, 32:64] = returned[:, start + 128 : start + 256]
            out[copy, panel, 64:80] = tile


def middle(got, own, far, up, down, more, moment, codes, state, low, span):
    return pl.pallas_call(
        middle_kernel,
        out_shape=(shape(8, 4, 80, 128), shape(16, 1024, of=F32), shape(16, 1024, of=F32)),
        in_specs=[VMEM] + [ANY] * 5 + [VMEM] * 3 + [SMEM] * 2,
        out_specs=(VMEM, VMEM, VMEM),
        scratch_shapes=[
            pltpu.VMEM((8, 128, 1024), BF16),
            pltpu.VMEM((32, 1024), F32),
            pltpu.VMEM((32, 1024), F32),
            pltpu.SemaphoreType.DMA((8,)),
        ],
        compiler_params=pltpu.CompilerParams(vmem_limit_bytes=32 * 1024 * 1024),
    )(got, own, far, up, down, more, moment, codes, state, low, span)


def update_kernel(got, left, out, ends):
    halves = [
        jnp.dot(left[...], got[:, at : at + 32, :].reshape(1024, 128), preferred_element_type=F32)
        for at in (0, 32)
    ]
    moved = jnp.concatenate(halves, axis=1).astype(BF16).reshape(8, 16, 256)
    for copy in range(8):
        out[copy] = moved
    values = jnp.sum(got[:, 64:80, :].astype(F32), axis=2, keepdims=True)
    ends[0] = jnp.broadcast_to(jnp.min(values[:, 0:8], axis=0), (8, 128))
    ends[1] = jnp.broadcast_to(jnp.max(values[:, 8:16], axis=0), (8, 128))


def update_part(got, left):
    return pl.pallas_call(
        update_kernel,
        out_shape=(shape(8, 8, 16, 256), shape(2, 8, 128, of=F32)),
        in_specs=[VMEM, VMEM],
        out_specs=(VMEM, VMEM),
    )(got, left)


def step_kernel(got, olds, params_new, update):
    rep = lax.axis_index("rep")
    for panel in range(4):
        lanes = slice(panel * 256, panel * 256 + 256)
        update[:, :, lanes] = got[rep, panel].astype(F32)
        for block in range(8):
            change = got[block, panel].astype(F32)
            old = olds[block, :, :, lanes].astype(F32)
            new = old * (1.0 - 0.05 * 0.1) - 0.05 * change
            start = block * 1024 + panel * 256
            params_new[:, :, start : start + 256] = new.astype(BF16)


def step(got, olds):
    return pl.pallas_call(
        step_kernel,
        out_shape=(shape(2, 16, 8192), shape(2, 16, 1024, of=F32)),
        in_specs=[VMEM, VMEM],
        out_specs=(VMEM, VMEM),
    )(got, olds)


def on_device(grads, params, left_basis, right_basis, moment, codes, level_low, level_span):
    core, rep = lax.axis_index("core"), lax.axis_index("rep")
    pick = lambda values, at: lax.dynamic_index_in_dim(values, at, 0, keepdims=False)
    both = lambda here, there: jnp.where(core == 0, jnp.stack([here, there]), jnp.stack([there, here]))
    swap = lambda values: shift(values, "core", 2, 1)

    def wait(value, after):
        return lax.optimization_barrier((value, after))[0]

    bases = exchange(bases_out(right_basis, left_basis).reshape(8, 2, 16, 1024), Q)
    right_y = bases[:, 0].reshape(128, 1024)
    left_y = bases[:, 1].reshape(128, 1024)

    sent = panels(grads[0])
    got = exchange(sent.reshape(64, 16, 256), ZQ)
    part = left_part(got.reshape(8, 128, 256), left_y)

    far = shift(right_y, "y", 8, 4)
    pair = jnp.stack([right_y, far])
    up, down = shift(pair, "y", 8, 1), shift(pair, "y", 8, -1)
    more = shift(up, "y", 8, 1)

    state = jnp.stack([pick(moment, 1 - core), pick(codes, 1 - core).astype(F32)])
    state = swap(wait(state, part))

    got = exchange(part.reshape(32, 32, 256), YX).reshape(8, 4, 32, 256)
    block, mine, others = middle(
        got, right_y, far, up, down, more, moment, codes, state, level_low, level_span
    )
    got = exchange(block.reshape(32, 80, 128), YX)
    moved, ends = update_part(got, left_y)
    got = exchange(moved.reshape(64, 16, 256), ZQ).reshape(8, 4, 2, 16, 256)

    rotated = both(mine, swap(others))
    ends = ends[:, :, 0]
    ends = both(ends, swap(ends))
    low_new = ends[:, 0]
    span_new = ends[:, 1] - low_new
    moment_new = 0.9 * moment + 0.1 * rotated
    grouped = rotated.reshape(2, 16, 8, QGROUP)
    code_grouped = codes.reshape(2, 16, 8, QGROUP).astype(F32)
    second = level_low[:, None, :, None] + code_grouped / 15.0 * level_span[:, None, :, None]
    second_new = 0.95 * second + 0.05 * grouped * grouped
    levels = 15.0 * (second_new - low_new[:, None, :, None]) / span_new[:, None, :, None]
    levels = levels.reshape(2, 16, 1024)

    olds = params[None]
    for bit, start, end in ((1, sent, part), (2, part, block), (4, block, moved)):
        other = lax.ppermute(wait(olds, start), "rep", [(i, i ^ bit) for i in range(8)])
        olds, other = wait((olds, other), end)
        olds = jnp.where(rep & bit == 0, jnp.concatenate([olds, other]), jnp.concatenate([other, olds]))
    params_new, update = step(got, olds)
    return (params_new, moment_new, update, levels, low_new, span_new)


def solution(mesh):
    fine = Mesh(mesh.devices.reshape(8, 8, 4, 2), ("rep", "y", "x", "core"))
    return jax.shard_map(
        on_device,
        mesh=fine,
        in_specs=(
            P("rep", None, F, None),
            P(None, F, "rep"),
            P(None, F, None),
            P(None, ("rep",) + F, None),
            P(None, F, "rep"),
            P(None, F, "rep"),
            P(None, "rep"),
            P(None, "rep"),
        ),
        out_specs=(
            P(None, F, None),
            P(None, F, "rep"),
            P(None, F, "rep"),
            P(None, F, "rep"),
            P(None, "rep"),
            P(None, "rep"),
        ),
        check_vma=False,
    )
```

time: 183 us -> 158 us (0.86)
  starting transfers between devices: 39.2 us -> 87.4 us
  waiting for transfers between devices: 85.7 us -> 48.5 us
  blocking collectives: 21.5 us -> 0 us
  between operations: 14.4 us -> 0.97 us
  Pallas kernels: 0 us -> 13.1 us
  matrix products: 7.63 us -> 0 us
  local copies, waits for them, and re-layouts: 10.8 us -> 4.64 us
    ppermute x0 -> x10, starting transfers between devices: none -> 46.5 us  [the longest x7 32.3 us: shift(): lax.ppermute(block, axis, [(i, (i + by) % size) for i in range(size)])]
    all_to_all x4 -> x5, waiting for transfers between devices: 56.5 us -> 20 us  [exchange(): return lax.all_to_all(blocks, axes, split_axis=0, concat_axis=0, tiled=True)]
    all_gather x2 -> x0, waiting for transfers between devices: 29.1 us -> none  [the longest x1 24 us: on_device(): params_all = lax.all_gather(doubled, 'rep', axis=0)[:, :2]]
    ppermute x0 -> x10, waiting for transfers between devices: none -> 28.5 us  [the longest x7 22.4 us: shift(): lax.ppermute(block, axis, [(i, (i + by) % size) for i in range(size)])]
    all_to_all x1 -> x0, blocking collectives: 21.5 us -> none  [exchange(): return lax.all_to_all(blocks, axes, split_axis=0, concat_axis=0, tiled=True)]
    pallas_call x0 -> x6, Pallas kernels: none -> 13.1 us  [the longest x1 2.87 us: middle(): pl.pallas_call(middle_kernel, out_shape=(shape(8, 4, 80, 128), shape(16,...]
    dot_general x4 -> x0, matrix products: 7.63 us -> none  [the longest x1 3.38 us: on_device(): jnp.einsum('lik,ljk->lij', scaled, right, preferred_element_type=f32)]
    broadcast_in_dim x5 -> x0, local copies, waits for them, and re-layouts: 3.57 us -> none  [the longest x1 0.94 us: on_device(): both = jnp.broadcast_to(right_basis[None, None], (4, 2, 2, 16, 1024))]
  transfers between devices with their start and end apart: 6 -> 15, of which waited for: 5 -> 8; matrix products, arithmetic and copies ran while one was open for 8% -> 2% of each run, Pallas kernels for 0% -> 4%
where the time goes in v3:
time: 158 us; the launch traced here: 157 us
  starting transfers between devices  87.4 us (55%)
  waiting for transfers between devices  48.5 us (31%)
  Pallas kernels  13.1 us (8%)
  local copies, waits for them, and re-layouts  4.64 us (3%)
  other arithmetic  2.61 us (2%)
    all_to_all x5, starting transfers between devices, exchange(): return lax.all_to_all(blocks, axes, split_axis=0, concat_axis=0, tiled=True)  40.8 us
    ppermute x7, starting transfers between devices, shift(): lax.ppermute(block, axis, [(i, (i + by) % size) for i in range(size)])  32.3 us
    ppermute x7, waiting for transfers between devices, shift(): lax.ppermute(block, axis, [(i, (i + by) % size) for i in range(size)])  22.4 us
    all_to_all x5, waiting for transfers between devices, exchange(): return lax.all_to_all(blocks, axes, split_axis=0, concat_axis=0, tiled=True)  20 us
    ppermute x3, starting transfers between devices, on_device(): lax.ppermute(wait(olds, start), 'rep', [(i, i ^ bit) for i in range(8)])  14.2 us
    ppermute x3, waiting for transfers between devices, on_device(): lax.ppermute(wait(olds, start), 'rep', [(i, i ^ bit) for i in range(8)])  6.11 us
    unnamed x28, local copies, waits for them, and re-layouts  3.77 us
  transfers between devices with their start and end apart: 15, of which 8 were waited for; matrix products, arithmetic and copies ran while one was open for 2% of the time, Pallas kernels for 4%

profile of v3, /device:TPU:1, one launch (start us, length us, event | category | flops | bytes accessed | tf_op | source)
XLA Modules:
  0.0 157.1 jit_solution(6900218102924759422)
XLA Ops:
  0.6 1.7 %shard_map.128 = bf16[4,2,2,16,1024]{4,3,2,1,0:T(8,128)(2,1)} custom-call(bf16[2,16,1024]{2,1,0:T(8,128)(2,1)} %right.1, bf16[2,16,1024]{2,1,0:T(8,128)(2,1)} %left.1), custom_call_target="tpu_custom_call" | custom-call | tf_op jit(solution)/shard_map/pallas_call | solution.py:38
  2.3 10.3 %all-to-all-start.1 = ((bf16[8,2,16,1024]{3,2,1,0:T(8,128)(2,1)}), bf16[8,2,16,1024]{3,2,1,0:T(8,128)(2,1)S(1)}, u32[]{:S(2)}, u32[]{:S(2)}) async-start(bf16[8,2,16,1024]{3,2,1,0:T(8,128)(2,1)} %bitcast.46), calls=%async_computation.1 | async-start | bytes 1048576 | tf_op jit(solution)/shard_map/all_to_all | solution.py:24
  12.6 1.9 %shard_map.127 = bf16[32,2,16,256]{3,2,1,0:T(8,128)(2,1)} custom-call(bf16[2,16,8192]{2,1,0:T(8,128)(2,1)} %bitcast.51), custom_call_target="tpu_custom_call" | custom-call | tf_op jit(solution)/shard_map/pallas_call | solution.py:49
  14.5 7.6 %all-to-all-done.1 = bf16[8,2,16,1024]{3,2,1,0:T(8,128)(2,1)S(1)} async-done(((bf16[8,2,16,1024]{3,2,1,0:T(8,128)(2,1)}), bf16[8,2,16,1024]{3,2,1,0:T(8,128)(2,1)S(1)}, u32[]{:S(2)}, u32[]{:S(2)}) %all-to-all-start.1) | async-done | bytes 524320 | tf_op jit(solution)/shard_map/all_to_all | solution.py:24
  22.1 7.9 %all-to-all-start = ((bf16[64,16,256]{2,1,0:T(8,128)(2,1)}), bf16[64,16,256]{2,1,0:T(8,128)(2,1)S(1)}, u32[]{:S(2)}, u32[]{:S(2)}) async-start(bf16[64,16,256]{2,1,0:T(8,128)(2,1)} %bitcast.50), calls=%async_computation | async-start | bytes 1048576 | tf_op jit(solution)/shard_map/all_to_all | solution.py:24
  30.7 7.4 %collective-permute-start = (bf16[128,1024]{1,0:T(8,128)(2,1)S(1)}, bf16[128,1024]{1,0:T(8,128)(2,1)S(1)}, u32[]{:S(2)}, u32[]{:S(2)}) collective-permute-start(bf16[128,1024]{1,0:T(8,128)(2,1)S(1)} %bitcast.38), channel_id=1, source_target_pairs={{0,32},{8,40},{16,48},{24,56},{32,0},{40,8},{48,16},{56,24},{1,33}... | collective-permute-start | bytes 786440 | tf_op jit(solution)/shard_map/ppermute | solution.py:28
  38.2 7.8 %collective-permute-done.far = bf16[128,1024]{1,0:T(8,128)(2,1)S(1)} collective-permute-done((bf16[128,1024]{1,0:T(8,128)(2,1)S(1)}, bf16[128,1024]{1,0:T(8,128)(2,1)S(1)}, u32[]{:S(2)}, u32[]{:S(2)}) %collective-permute-start) | collective-permute-done | bytes 262176 | tf_op jit(solution)/shard_map/ppermute | solution.py:28
  46.0 0.9 pad_maximum_fusion
  46.8 6.3 %collective-permute-start.1 = (bf16[2,128,1024]{2,1,0:T(8,128)(2,1)}, bf16[2,128,1024]{2,1,0:T(8,128)(2,1)S(1)}, u32[]{:S(2)}, u32[]{:S(2)}) collective-permute-start(bf16[2,128,1024]{2,1,0:T(8,128)(2,1)} %pad_maximum_fusion), channel_id=1, source_target_pairs={{0,8},{8,16},{16,24},{24,32},{32,40},{40,48},{48,56},{56,0},{1,9},... | collective-permute-start | bytes 1572872 | tf_op jit(solution)/shard_map/ppermute | solution.py:28
  54.0 2.2 %shard_map.129 = bf16[1024,256]{1,0:T(8,128)(2,1)} custom-call(bf16[8,128,256]{2,1,0:T(8,128)(2,1)} %bitcast.49, bf16[128,1024]{1,0:T(8,128)(2,1)} %bitcast.44), custom_call_target="tpu_custom_call" | custom-call | tf_op jit(solution)/shard_map/pallas_call | solution.py:65
  56.2 9.7 %all-to-all-start.2 = ((bf16[32,32,256]{2,1,0:T(8,128)(2,1)}), bf16[32,32,256]{2,1,0:T(8,128)(2,1)S(1)}, u32[]{:S(2)}, u32[]{:S(2)}) async-start(bf16[32,32,256]{2,1,0:T(8,128)(2,1)} %bitcast.48), calls=%async_computation.2 | async-start | bytes 1048576 | tf_op jit(solution)/shard_map/all_to_all | solution.py:24
  66.0 4.6 %collective-permute-start.2 = (bf16[2,128,1024]{2,1,0:T(8,128)(2,1)}, bf16[2,128,1024]{2,1,0:T(8,128)(2,1)S(1)}, u32[]{:S(2)}, u32[]{:S(2)}) collective-permute-start(bf16[2,128,1024]{2,1,0:T(8,128)(2,1)} %pad_maximum_fusion), channel_id=1, source_target_pairs={{0,56},{8,0},{16,8},{24,16},{32,24},{40,32},{48,40},{56,48},{1,57}... | collective-permute-start | bytes 1572872 | tf_op jit(solution)/shard_map/ppermute | solution.py:28
  70.5 1.9 %collective-permute-start.3 = (bf16[2,128,1024]{2,1,0:T(8,128)(2,1)S(1)}, bf16[2,128,1024]{2,1,0:T(8,128)(2,1)S(1)}, u32[]{:S(2)}, u32[]{:S(2)}) collective-permute-start(bf16[2,128,1024]{2,1,0:T(8,128)(2,1)S(1)} %collective-permute-done.1.up), channel_id=1, source_target_pairs={{0,8},{8,16},{16,24},{24,32},{32,40},{40,48},{48,56},{56,0},{1,9},... | collective-permute-start | bytes 1572872 | tf_op jit(solution)/shard_map/ppermute | solution.py:28
  72.6 4.0 %collective-permute-start.4 = (f32[2,16,1024]{2,1,0:T(8,128)S(1)}, f32[2,16,1024]{2,1,0:T(8,128)S(1)}, u32[]{:S(2)}, u32[]{:S(2)}) collective-permute-start(f32[2,16,1024]{2,1,0:T(8,128)S(1)} %pad_maximum_fusion.1), channel_id=1, source_target_pairs={{0,1},{1,0},{2,3},{3,2},{4,5},{5,4},{6,7},{7,6},{8,9},{9,8},{10,11... | collective-permute-start | bytes 393224 | tf_op jit(solution)/shard_map/ppermute | solution.py:28
  76.6 1.0 collective-permute-done.4.state
  77.5 12.1 %collective-permute-done.2.down = bf16[2,128,1024]{2,1,0:T(8,128)(2,1)S(1)} collective-permute-done((bf16[2,128,1024]{2,1,0:T(8,128)(2,1)}, bf16[2,128,1024]{2,1,0:T(8,128)(2,1)S(1)}, u32[]{:S(2)}, u32[]{:S(2)}) %collective-permute-start.2) | collective-permute-done | bytes 524320 | tf_op jit(solution)/shard_map/ppermute | solution.py:28
  89.7 1.5 collective-permute-done.3.more
  91.1 2.9 %shard_map.130 = (bf16[8,4,80,128]{3,2,1,0:T(8,128)(2,1)}, f32[16,1024]{1,0:T(8,128)S(1)}, f32[16,1024]{1,0:T(8,128)S(1)}) custom-call(bf16[8,4,32,256]{3,2,1,0:T(8,128)(2,1)S(1)} %bitcast.41, bf16[128,1024]{1,0:T(8,128)(2,1)S(1)} %bitcast.40, bf16[128,1024]{1,0:T(8,128)(2,1)S(1)} %collective-permute-done.far, ...), custom_call_target="tpu_custom_call" | custom-call | tf_op jit(solution)/shard_map/pallas_call | solution.py:137
  94.0 7.5 %all-to-all-start.3 = ((bf16[32,80,128]{2,1,0:T(8,128)(2,1)}), bf16[32,80,128]{2,1,0:T(8,128)(2,1)S(1)}, u32[]{:S(2)}, u32[]{:S(2)}) async-start(bf16[32,80,128]{2,1,0:T(8,128)(2,1)} %bitcast.10), calls=%async_computation.3 | async-start | bytes 1310720 | tf_op jit(solution)/shard_map/all_to_all | solution.py:24
  101.5 3.1 %collective-permute-start.5 = (bf16[1,2,16,1024]{3,2,1,0:T(8,128)(2,1)S(1)}, bf16[1,2,16,1024]{3,2,1,0:T(8,128)(2,1)S(1)}, u32[]{:S(2)}, u32[]{:S(2)}) collective-permute-start(bf16[1,2,16,1024]{3,2,1,0:T(8,128)(2,1)S(1)} %bitcast.54), channel_id=1, source_target_pairs={{0,64},{64,0},{128,192},{192,128},{256,320},{320,256},{384,448},{4... | collective-permute-start | bytes 196616 | tf_op jit(solution)/shard_map/ppermute | solution.py:244
  104.6 1.9 %collective-permute-done.5 = bf16[1,2,16,1024]{3,2,1,0:T(8,128)(2,1)S(1)} collective-permute-done((bf16[1,2,16,1024]{3,2,1,0:T(8,128)(2,1)S(1)}, bf16[1,2,16,1024]{3,2,1,0:T(8,128)(2,1)S(1)}, u32[]{:S(2)}, u32[]{:S(2)}) %collective-permute-start.5) | collective-permute-done | bytes 65568 | tf_op jit(solution)/shard_map/ppermute | solution.py:244
  106.6 4.0 %collective-permute-start.6 = (bf16[2,2,16,1024]{3,2,1,0:T(8,128)(2,1)S(1)}, bf16[2,2,16,1024]{3,2,1,0:T(8,128)(2,1)S(1)}, u32[]{:S(2)}, u32[]{:S(2)}) collective-permute-start(bf16[2,2,16,1024]{3,2,1,0:T(8,128)(2,1)S(1)} %maximum_select_fusion.2), channel_id=1, source_target_pairs={{0,128},{64,192},{128,0},{192,64},{256,384},{320,448},{384,256},{4... | collective-permute-start | bytes 393224 | tf_op jit(solution)/shard_map/ppermute | solution.py:244
  110.6 4.2 %collective-permute-done.6 = bf16[2,2,16,1024]{3,2,1,0:T(8,128)(2,1)S(1)} collective-permute-done((bf16[2,2,16,1024]{3,2,1,0:T(8,128)(2,1)S(1)}, bf16[2,2,16,1024]{3,2,1,0:T(8,128)(2,1)S(1)}, u32[]{:S(2)}, u32[]{:S(2)}) %collective-permute-start.6) | collective-permute-done | bytes 131104 | tf_op jit(solution)/shard_map/ppermute | solution.py:244
  114.9 7.1 %collective-permute-start.7 = (bf16[4,2,16,1024]{3,2,1,0:T(8,128)(2,1)S(1)}, bf16[4,2,16,1024]{3,2,1,0:T(8,128)(2,1)S(1)}, u32[]{:S(2)}, u32[]{:S(2)}) collective-permute-start(bf16[4,2,16,1024]{3,2,1,0:T(8,128)(2,1)S(1)} %maximum_select_fusion.1), channel_id=1, source_target_pairs={{0,256},{64,320},{128,384},{192,448},{256,0},{320,64},{384,128},{4... | collective-permute-start | bytes 786440 | tf_op jit(solution)/shard_map/ppermute | solution.py:244
  122.1 5.7 %collective-permute-start.8 = (f32[16,1024]{1,0:T(8,128)S(1)}, f32[16,1024]{1,0:T(8,128)S(1)}, u32[]{:S(2)}, u32[]{:S(2)}) collective-permute-start(f32[16,1024]{1,0:T(8,128)S(1)} %get-tuple-element.37), channel_id=1, source_target_pairs={{0,1},{1,0},{2,3},{3,2},{4,5},{5,4},{6,7},{7,6},{8,9},{9,8},{10,11... | collective-permute-start | bytes 196616 | tf_op jit(solution)/shard_map/ppermute | solution.py:28
  127.8 0.8 copy-done.4
  128.7 2.2 %shard_map.131 = (bf16[8,8,16,256]{3,2,1,0:T(8,128)(2,1)}, f32[2,8,128]{2,1,0:T(8,128)}) custom-call(bf16[32,80,128]{2,1,0:T(8,128)(2,1)} %copy-done.4, bf16[128,1024]{1,0:T(8,128)(2,1)} %bitcast.45), custom_call_target="tpu_custom_call" | custom-call | tf_op jit(solution)/shard_map/pallas_call | solution.py:166
  130.9 5.5 %all-to-all-start.4 = ((bf16[64,16,256]{2,1,0:T(8,128)(2,1)}), bf16[64,16,256]{2,1,0:T(8,128)(2,1)S(1)}, u32[]{:S(2)}, u32[]{:S(2)}) async-start(bf16[64,16,256]{2,1,0:T(8,128)(2,1)} %bitcast.52), calls=%async_computation.4 | async-start | bytes 1048576 | tf_op jit(solution)/shard_map/all_to_all | solution.py:24
  136.5 2.4 %collective-permute-start.9 = (f32[2,8]{1,0:T(2,128)S(1)}, f32[2,8]{1,0:T(2,128)S(1)}, u32[]{:S(2)}, u32[]{:S(2)}) collective-permute-start(f32[2,8]{1,0:T(2,128)S(1)} %slice_reduce_fusion), channel_id=1, source_target_pairs={{0,1},{1,0},{2,3},{3,2},{4,5},{5,4},{6,7},{7,6},{8,9},{9,8},{10,11... | collective-permute-start | bytes 200 | tf_op jit(solution)/shard_map/ppermute | solution.py:28
  138.9 0.9 maximum_select_fusion.olds
  141.8 12.3 %all-to-all-done.4 = bf16[64,16,256]{2,1,0:T(8,128)(2,1)S(1)} async-done(((bf16[64,16,256]{2,1,0:T(8,128)(2,1)}), bf16[64,16,256]{2,1,0:T(8,128)(2,1)S(1)}, u32[]{:S(2)}, u32[]{:S(2)}) %all-to-all-start.4) | async-done | bytes 524320 | tf_op jit(solution)/shard_map/all_to_all | solution.py:24
  154.9 2.2 %shard_map.132 = (bf16[2,16,8192]{2,1,0:T(8,128)(2,1)}, f32[2,16,1024]{2,1,0:T(8,128)}) custom-call(bf16[8,4,2,16,256]{4,3,2,1,0:T(8,128)(2,1)} %bitcast.47, bf16[8,2,16,1024]{3,2,1,0:T(8,128)(2,1)} %maximum_select_fusion.olds), custom_call_target="tpu_custom_call" | custom-call | tf_op jit(solution)/shard_map/pallas_call | solution.py:188
  (47 shorter events, 4.7 us)
Async XLA Ops:
  2.3 19.8 %all-to-all-start.1 = ((bf16[8,2,16,1024]{3,2,1,0:T(8,128)(2,1)}), bf16[8,2,16,1024]{3,2,1,0:T(8,128)(2,1)S(1)}, u32[]{:S(2)}, u32[]{:S(2)}) async-start(bf16[8,2,16,1024]{3,2,1,0:T(8,128)(2,1)} %bitcast.46), calls=%async_computation.1 | async-start | bytes 1048576 | tf_op jit(solution)/shard_map/all_to_all | solution.py:24
  22.1 31.1 %all-to-all-start = ((bf16[64,16,256]{2,1,0:T(8,128)(2,1)}), bf16[64,16,256]{2,1,0:T(8,128)(2,1)S(1)}, u32[]{:S(2)}, u32[]{:S(2)}) async-start(bf16[64,16,256]{2,1,0:T(8,128)(2,1)} %bitcast.50), calls=%async_computation | async-start | bytes 1048576 | tf_op jit(solution)/shard_map/all_to_all | solution.py:24
  30.7 15.3 %collective-permute-start = (bf16[128,1024]{1,0:T(8,128)(2,1)S(1)}, bf16[128,1024]{1,0:T(8,128)(2,1)S(1)}, u32[]{:S(2)}, u32[]{:S(2)}) collective-permute-start(bf16[128,1024]{1,0:T(8,128)(2,1)S(1)} %bitcast.38), channel_id=1, source_target_pairs={{0,32},{8,40},{16,48},{24,56},{32,0},{40,8},{48,16},{56,24},{1,33}... | collective-permute-start | bytes 786440 | tf_op jit(solution)/shard_map/ppermute | solution.py:28
  46.8 23.7 %collective-permute-start.1 = (bf16[2,128,1024]{2,1,0:T(8,128)(2,1)}, bf16[2,128,1024]{2,1,0:T(8,128)(2,1)S(1)}, u32[]{:S(2)}, u32[]{:S(2)}) collective-permute-start(bf16[2,128,1024]{2,1,0:T(8,128)(2,1)} %pad_maximum_fusion), channel_id=1, source_target_pairs={{0,8},{8,16},{16,24},{24,32},{32,40},{40,48},{48,56},{56,0},{1,9},... | collective-permute-start | bytes 1572872 | tf_op jit(solution)/shard_map/ppermute | solution.py:28
  53.2 0.8 copy-start.6
  56.2 16.2 %copy-start = (f32[2,16,1024]{2,1,0:T(8,128)S(1)}, f32[2,16,1024]{2,1,0:T(8,128)}, u32[]{:S(2)}) copy-start(f32[2,16,1024]{2,1,0:T(8,128)} %moment.1) | copy-start | bytes 393220
  56.2 34.9 %all-to-all-start.2 = ((bf16[32,32,256]{2,1,0:T(8,128)(2,1)}), bf16[32,32,256]{2,1,0:T(8,128)(2,1)S(1)}, u32[]{:S(2)}, u32[]{:S(2)}) async-start(bf16[32,32,256]{2,1,0:T(8,128)(2,1)} %bitcast.48), calls=%async_computation.2 | async-start | bytes 1048576 | tf_op jit(solution)/shard_map/all_to_all | solution.py:24
  66.0 6.5 %copy-start.1 = (s32[2,16,1024]{2,1,0:T(8,128)S(1)}, s32[2,16,1024]{2,1,0:T(8,128)}, u32[]{:S(2)}) copy-start(s32[2,16,1024]{2,1,0:T(8,128)} %codes.1) | copy-start | bytes 393220
  66.0 23.7 %collective-permute-start.2 = (bf16[2,128,1024]{2,1,0:T(8,128)(2,1)}, bf16[2,128,1024]{2,1,0:T(8,128)(2,1)S(1)}, u32[]{:S(2)}, u32[]{:S(2)}) collective-permute-start(bf16[2,128,1024]{2,1,0:T(8,128)(2,1)} %pad_maximum_fusion), channel_id=1, source_target_pairs={{0,56},{8,0},{16,8},{24,16},{32,24},{40,32},{48,40},{56,48},{1,57}... | collective-permute-start | bytes 1572872 | tf_op jit(solution)/shard_map/ppermute | solution.py:28
  70.5 20.6 %collective-permute-start.3 = (bf16[2,128,1024]{2,1,0:T(8,128)(2,1)S(1)}, bf16[2,128,1024]{2,1,0:T(8,128)(2,1)S(1)}, u32[]{:S(2)}, u32[]{:S(2)}) collective-permute-start(bf16[2,128,1024]{2,1,0:T(8,128)(2,1)S(1)} %collective-permute-done.1.up), channel_id=1, source_target_pairs={{0,8},{8,16},{16,24},{24,32},{32,40},{40,48},{48,56},{56,0},{1,9},... | collective-permute-start | bytes 1572872 | tf_op jit(solution)/shard_map/ppermute | solution.py:28
  72.5 18.6 %copy-start.3 = (f32[2,8]{1,0:T(2,128)S(1)}, f32[2,8]{1,0:T(2,128)}, u32[]{:S(2)}) copy-start(f32[2,8]{1,0:T(2,128)} %span.1) | copy-start | bytes 196
  72.6 18.6 %copy-start.2 = (f32[2,8]{1,0:T(2,128)S(1)}, f32[2,8]{1,0:T(2,128)}, u32[]{:S(2)}) copy-start(f32[2,8]{1,0:T(2,128)} %low.1) | copy-start | bytes 196
  72.6 5.0 %collective-permute-start.4 = (f32[2,16,1024]{2,1,0:T(8,128)S(1)}, f32[2,16,1024]{2,1,0:T(8,128)S(1)}, u32[]{:S(2)}, u32[]{:S(2)}) collective-permute-start(f32[2,16,1024]{2,1,0:T(8,128)S(1)} %pad_maximum_fusion.1), channel_id=1, source_target_pairs={{0,1},{1,0},{2,3},{3,2},{4,5},{5,4},{6,7},{7,6},{8,9},{9,8},{10,11... | collective-permute-start | bytes 393224 | tf_op jit(solution)/shard_map/ppermute | solution.py:28
  94.0 7.5 %copy-start.7 = (bf16[2,16,1024]{2,1,0:T(8,128)(2,1)S(1)}, bf16[2,16,1024]{2,1,0:T(8,128)(2,1)}, u32[]{:S(2)}) copy-start(bf16[2,16,1024]{2,1,0:T(8,128)(2,1)} %param.9) | copy-start | bytes 196612
  94.0 33.8 %all-to-all-start.3 = ((bf16[32,80,128]{2,1,0:T(8,128)(2,1)}), bf16[32,80,128]{2,1,0:T(8,128)(2,1)S(1)}, u32[]{:S(2)}, u32[]{:S(2)}) async-start(bf16[32,80,128]{2,1,0:T(8,128)(2,1)} %bitcast.10), calls=%async_computation.3 | async-start | bytes 1310720 | tf_op jit(solution)/shard_map/all_to_all | solution.py:24
  101.5 5.0 %collective-permute-start.5 = (bf16[1,2,16,1024]{3,2,1,0:T(8,128)(2,1)S(1)}, bf16[1,2,16,1024]{3,2,1,0:T(8,128)(2,1)S(1)}, u32[]{:S(2)}, u32[]{:S(2)}) collective-permute-start(bf16[1,2,16,1024]{3,2,1,0:T(8,128)(2,1)S(1)} %bitcast.54), channel_id=1, source_target_pairs={{0,64},{64,0},{128,192},{192,128},{256,320},{320,256},{384,448},{4... | collective-permute-start | bytes 196616 | tf_op jit(solution)/shard_map/ppermute | solution.py:244
  106.6 8.3 %collective-permute-start.6 = (bf16[2,2,16,1024]{3,2,1,0:T(8,128)(2,1)S(1)}, bf16[2,2,16,1024]{3,2,1,0:T(8,128)(2,1)S(1)}, u32[]{:S(2)}, u32[]{:S(2)}) collective-permute-start(bf16[2,2,16,1024]{3,2,1,0:T(8,128)(2,1)S(1)} %maximum_select_fusion.2), channel_id=1, source_target_pairs={{0,128},{64,192},{128,0},{192,64},{256,384},{320,448},{384,256},{4... | collective-permute-start | bytes 393224 | tf_op jit(solution)/shard_map/ppermute | solution.py:244
  114.9 24.0 %collective-permute-start.7 = (bf16[4,2,16,1024]{3,2,1,0:T(8,128)(2,1)S(1)}, bf16[4,2,16,1024]{3,2,1,0:T(8,128)(2,1)S(1)}, u32[]{:S(2)}, u32[]{:S(2)}) collective-permute-start(bf16[4,2,16,1024]{3,2,1,0:T(8,128)(2,1)S(1)} %maximum_select_fusion.1), channel_id=1, source_target_pairs={{0,256},{64,320},{128,384},{192,448},{256,0},{320,64},{384,128},{4... | collective-permute-start | bytes 786440 | tf_op jit(solution)/shard_map/ppermute | solution.py:244
  122.1 18.9 %collective-permute-start.8 = (f32[16,1024]{1,0:T(8,128)S(1)}, f32[16,1024]{1,0:T(8,128)S(1)}, u32[]{:S(2)}, u32[]{:S(2)}) collective-permute-start(f32[16,1024]{1,0:T(8,128)S(1)} %get-tuple-element.37), channel_id=1, source_target_pairs={{0,1},{1,0},{2,3},{3,2},{4,5},{5,4},{6,7},{7,6},{8,9},{9,8},{10,11... | collective-permute-start | bytes 196616 | tf_op jit(solution)/shard_map/ppermute | solution.py:28
  127.8 0.8 copy-start.4
  130.9 5.5 %copy-start.9 = (f32[2,8,128]{2,1,0:T(8,128)S(1)}, f32[2,8,128]{2,1,0:T(8,128)}, u32[]{:S(2)}) copy-start(f32[2,8,128]{2,1,0:T(8,128)} %get-tuple-element.39) | copy-start | bytes 24580
  130.9 23.3 %all-to-all-start.4 = ((bf16[64,16,256]{2,1,0:T(8,128)(2,1)}), bf16[64,16,256]{2,1,0:T(8,128)(2,1)S(1)}, u32[]{:S(2)}, u32[]{:S(2)}) async-start(bf16[64,16,256]{2,1,0:T(8,128)(2,1)} %bitcast.52), calls=%async_computation.4 | async-start | bytes 1048576 | tf_op jit(solution)/shard_map/all_to_all | solution.py:24
  136.5 3.3 %collective-permute-start.9 = (f32[2,8]{1,0:T(2,128)S(1)}, f32[2,8]{1,0:T(2,128)S(1)}, u32[]{:S(2)}, u32[]{:S(2)}) collective-permute-start(f32[2,8]{1,0:T(2,128)S(1)} %slice_reduce_fusion), channel_id=1, source_target_pairs={{0,1},{1,0},{2,3},{3,2},{4,5},{5,4},{6,7},{7,6},{8,9},{9,8},{10,11... | collective-permute-start | bytes 200 | tf_op jit(solution)/shard_map/ppermute | solution.py:28
  139.8 0.6 copy-start.8
  140.4 0.6 copy-start.10
  154.1 0.8 copy-start.5

commit v4 on v1

v4 whole, which is shorter than its diff:
```python
import jax
import jax.numpy as jnp
from jax import lax
from jax.experimental import pallas as pl
from jax.experimental.pallas import tpu as pltpu
from jax.sharding import Mesh, PartitionSpec as P

F = ("y", "x", "core")
ZQ = ("rep", "x", "core")
Q = ("x", "core")
BF16, F32 = jnp.bfloat16, jnp.float32
VMEM = pl.BlockSpec(memory_space=pltpu.VMEM)
SMEM = pl.BlockSpec(memory_space=pltpu.SMEM)
ANY = pl.BlockSpec(memory_space=pl.ANY)
PARAMS = pltpu.CompilerParams(vmem_limit_bytes=32 * 1024 * 1024)


def shape(*dims, of=BF16):
    return jax.ShapeDtypeStruct(dims, of)


def exchange(blocks, axes):
    return lax.all_to_all(blocks, axes, split_axis=0, concat_axis=0, tiled=True)


def shift(block, axis, size, by):
    return lax.ppermute(block, axis, [(i, (i + by) % size) for i in range(size)])


def pull(refs, places, sems):
    copies = [
        pltpu.make_async_copy(ref, place, sems.at[i])
        for i, (ref, place) in enumerate(zip(refs, places))
    ]
    for copy in copies:
        copy.start()

    def wait():
        for copy in copies:
            copy.wait()

    return wait


def quarters(tiles, lane):
    turned = []
    for to in range(4):
        new = None
        for part in range(4):
            tile = tiles[part]
            by = (32 * (part - to)) % 128
            tile = pltpu.roll(tile, by, 1) if by else tile
            new = tile if new is None else jnp.where(lane >= 32 * part, tile, new)
        turned.append(new)
    return turned


def panels_kernel(grads, left, out):
    lane = lax.broadcasted_iota(jnp.int32, (32, 128), 1)
    eighth = pl.ds(pl.multiple_of(lax.axis_index("rep") * 128, 128), 128)
    basis = left[:, :, eighth]
    for block in range(8):
        for half in range(2):
            start = block * 1024 + half * 512
            tiles = [
                grads[:, :, start + 128 * i : start + 128 * i + 128].astype(F32).reshape(32, 128)
                for i in range(4)
            ]
            for x, tile in enumerate(quarters(tiles, lane)):
                out[block, x, :, :, half * 128 : half * 128 + 128] = tile.astype(BF16).reshape(2, 16, 128)
        for x in range(4):
            out[block, x, :, :, 256:384] = basis


def panels(grads, left):
    return pl.pallas_call(
        panels_kernel, out_shape=shape(8, 4, 2, 16, 384), in_specs=[VMEM, VMEM], out_specs=VMEM
    )(grads, left)


def left_kernel(grads, out, left, held, sems):
    wait = pull([grads], [held], sems)
    wait()
    total = held[0, :, 0:256].astype(F32)
    for replica in range(1, 8):
        total += held[replica, :, 0:256].astype(F32)
    for replica in range(8):
        left[:, replica * 128 : replica * 128 + 128] = held[replica, :, 256:384]
    part = lax.dot_general(
        left[...], total.astype(BF16), (((0,), (0,)), ((), ())), preferred_element_type=F32
    )
    out[...] = part.astype(BF16)


def left_part(grads):
    return pl.pallas_call(
        left_kernel,
        out_shape=(shape(1024, 256), shape(128, 1024)),
        in_specs=[ANY],
        out_specs=(VMEM, VMEM),
        scratch_shapes=[pltpu.VMEM((8, 128, 384), BF16), pltpu.SemaphoreType.DMA((1,))],
        compiler_params=PARAMS,
    )(grads)


def right_kernel(got, own, far, up, down, more, out, right_out, held, right, sems):
    at = lax.axis_index("y")
    ring = [own, up.at[0], more.at[0], down.at[1], far, up.at[1], more.at[1], down.at[0]]
    places = [right.at[lax.rem(at + 8 - back, 8)] for back in range(8)]
    wait = pull([got] + ring, [held] + places, sems)
    wait()
    total = held[0].astype(F32)
    for part in range(1, 8):
        total += held[part].astype(F32)
    basis = right[...].reshape(256, 1024)
    out[...] = jnp.dot(total.astype(BF16), basis, preferred_element_type=F32).astype(BF16)
    right_out[...] = basis


def right_part(got, pieces):
    return pl.pallas_call(
        right_kernel,
        out_shape=(shape(128, 1024), shape(256, 1024)),
        in_specs=[ANY] * 6,
        out_specs=(VMEM, VMEM),
        scratch_shapes=[
            pltpu.VMEM((8, 128, 256), BF16),
            pltpu.VMEM((8, 32, 1024), BF16),
            pltpu.SemaphoreType.DMA((9,)),
        ],
        compiler_params=PARAMS,
    )(got, *pieces)


def ends_tile(ends):
    first = ends.astype(BF16).astype(F32)
    second = (ends - first).astype(BF16).astype(F32)
    third = ends - first - second
    lane = lax.broadcasted_iota(jnp.int32, (16, 128), 1)
    tile = jnp.where(lane == 0, first, jnp.where(lane == 1, second, jnp.where(lane == 2, third, 0.0)))
    return tile.astype(BF16)


def ends_of(tiles):
    values = jnp.sum(tiles.astype(F32), axis=2, keepdims=True)
    return jnp.min(values[:, 0:8], axis=0), jnp.max(values[:, 8:16], axis=0)


def moments_kernel(got, moment, codes, low, span, out, moment_new, second_new, held, sems):
    wait = pull([got], [held], sems)
    wait()
    for layer in range(2):
        lows, highs = [], []
        for group in range(8):
            lanes = slice(group * 128, group * 128 + 128)
            turn = held[0, layer, :, lanes].astype(F32)
            for part in range(1, 4):
                turn += held[part, layer, :, lanes].astype(F32)
            mean = 0.9 * moment[layer, :, lanes] + 0.1 * turn
            code = codes[layer, :, lanes].astype(F32)
            second = low[layer, group] + code / 15.0 * span[layer, group]
            second = 0.95 * second + 0.05 * turn * turn
            moment_new[layer, :, lanes] = mean
            second_new[layer, :, lanes] = second
            scaled = (mean / (jnp.sqrt(second) + 1e-08)).astype(BF16)
            for copy in range(4):
                out[copy, layer, group * 16 : group * 16 + 16] = scaled
            lows.append(jnp.min(second, axis=0, keepdims=True))
            highs.append(jnp.max(second, axis=0, keepdims=True))
        lows = jnp.min(jnp.concatenate(lows, axis=0), axis=1, keepdims=True)
        highs = jnp.max(jnp.concatenate(highs, axis=0), axis=1, keepdims=True)
        tile = ends_tile(jnp.concatenate([lows, highs], axis=0))
        for copy in range(4):
            for to in range(2):
                out[copy, to, 128 + layer * 16 : 144 + layer * 16] = tile


def moments(got, moment, codes, low, span):
    return pl.pallas_call(
        moments_kernel,
        out_shape=(
            shape(4, 2, 160, 128),
            shape(2, 16, 1024, of=F32),
            shape(2, 16, 1024, of=F32),
        ),
        in_specs=[ANY, VMEM, VMEM, SMEM, SMEM],
        out_specs=(VMEM, VMEM, VMEM),
        scratch_shapes=[pltpu.VMEM((4, 2, 16, 1024), BF16), pltpu.SemaphoreType.DMA((1,))],
        compiler_params=PARAMS,
    )(got, moment, codes, low, span)


def back_kernel(got, right, out, held, sems):
    wait = pull([got], [held], sems)
    wait()
    rows = [held[:, at * 16 : at * 16 + 16, :].reshape(128, 128) for at in range(8)]
    returned = lax.dot_general(
        jnp.concatenate(rows, axis=1), right[...], (((1,), (1,)), ((), ())), preferred_element_type=F32
    ).astype(BF16)
    tiles = [
        ends_tile(jnp.concatenate(ends_of(held[:, at : at + 16, :]), axis=0)) for at in (128, 144)
    ]
    for copy in range(8):
        out[copy, 0:128] = returned[:, 0:128]
        out[copy, 128:256] = returned[:, 128:256]
        out[copy, 256:272] = tiles[0]
        out[copy, 272:288] = tiles[1]


def back_part(got, right):
    return pl.pallas_call(
        back_kernel,
        out_shape=shape(8, 288, 128),
        in_specs=[ANY, VMEM],
        out_specs=VMEM,
        scratch_shapes=[pltpu.VMEM((8, 160, 128), BF16), pltpu.SemaphoreType.DMA((1,))],
        compiler_params=PARAMS,
    )(got, right)


def update_kernel(got, left, out, ends, held, sems):
    wait = pull([got], [held], sems)
    wait()
    halves = [
        jnp.dot(left[...], held[:, at : at + 128, :].reshape(1024, 128), preferred_element_type=F32)
        for at in (0, 128)
    ]
    moved = jnp.concatenate(halves, axis=1).astype(BF16).reshape(8, 16, 256)
    for copy in range(8):
        out[copy] = moved
    for layer in range(2):
        low, high = ends_of(held[:, 256 + 16 * layer : 272 + 16 * layer, :])
        ends[0, layer] = jnp.broadcast_to(low, (8, 128))
        ends[1, layer] = jnp.broadcast_to(high, (8, 128))


def update_part(got, left):
    return pl.pallas_call(
        update_kernel,
        out_shape=(shape(8, 8, 16, 256), shape(2, 2, 8, 128, of=F32)),
        in_specs=[ANY, VMEM],
        out_specs=(VMEM, VMEM),
        scratch_shapes=[pltpu.VMEM((8, 288, 128), BF16), pltpu.SemaphoreType.DMA((1,))],
        compiler_params=PARAMS,
    )(got, left)


def step_kernel(got, olds, params_new, update, held, sems):
    rep = lax.axis_index("rep")
    lane = lax.broadcasted_iota(jnp.int32, (32, 128), 1)
    wait = pull([got], [held], sems)
    wait()

    def change_of(block, half):
        lanes = slice(half * 128, half * 128 + 128)
        tiles = [held[block, x, :, :, lanes].astype(F32).reshape(32, 128) for x in range(4)]
        return [tile.reshape(2, 16, 128) for tile in quarters(tiles, lane)]

    for half in range(2):
        for part, change in enumerate(change_of(rep, half)):
            start = half * 512 + part * 128
            update[:, :, start : start + 128] = change
        for block in range(8):
            for part, change in enumerate(change_of(block, half)):
                start = half * 512 + part * 128
                old = olds[jnp.bitwise_xor(rep, block), :, :, start : start + 128].astype(F32)
                new = old * (1.0 - 0.05 * 0.1) - 0.05 * change
                start += block * 1024
                params_new[:, :, start : start + 128] = new.astype(BF16)


def step(got, olds):
    return pl.pallas_call(
        step_kernel,
        out_shape=(shape(2, 16, 8192), shape(2, 16, 1024, of=F32)),
        in_specs=[ANY, VMEM],
        out_specs=(VMEM, VMEM),
        scratch_shapes=[pltpu.VMEM((8, 4, 2, 16, 256), BF16), pltpu.SemaphoreType.DMA((1,))],
        compiler_params=PARAMS,
    )(got, olds)


def on_device(grads, params, left_basis, right_basis, moment, codes, level_low, level_span):
    core = lax.axis_index("core")
    pick = lambda values, at: lax.dynamic_index_in_dim(values, at, 0, keepdims=False)
    both = lambda here, there: jnp.where(core == 0, jnp.stack([here, there]), jnp.stack([there, here]))
    swap = lambda values: shift(values, "core", 2, 1)
    tie = lax.optimization_barrier

    right = both(pick(right_basis, core), swap(pick(right_basis, 1 - core))).reshape(32, 1024)
    far = shift(right, "y", 8, 4)
    pair = jnp.stack([right, far])
    up, down = shift(pair, "y", 8, 1), shift(pair, "y", 8, -1)

    sent = panels(grads[0], left_basis)
    got = exchange(sent.reshape(64, 16, 384), ZQ)
    got, up, down = tie((got, up, down))
    part, left_y = left_part(got.reshape(8, 128, 384))
    more = shift(up, "y", 8, 1)

    flip = lambda values, axis, size, bit: lax.ppermute(values, axis, [(i, i ^ bit) for i in range(size)])

    def joined(olds, other, bit):
        return jnp.stack([olds, other], 1).reshape(8 // bit, 2, 16, 1024)

    olds = params[None]

    got = exchange(part.reshape(8, 128, 256), "y")
    turned, right_x = right_part(got, (right, far, up, down, more))
    turned, other = tie((turned, flip(tie((olds, part))[0], "rep", 8, 4)))
    olds = joined(olds, other, 4)
    got = exchange(turned.reshape(8, 16, 1024), Q).reshape(4, 2, 16, 1024)
    block, moment_new, second_new = moments(got, moment, codes, level_low, level_span)
    got = exchange(block.reshape(8, 160, 128), Q)
    block = back_part(got, right_x)
    got = exchange(block, "y")
    moved, ends = update_part(got, left_y)
    moved, other = tie((moved, flip(tie((olds, block))[0], "rep", 8, 2)))
    olds = joined(olds, other, 2)
    olds = joined(olds, flip(olds, "rep", 8, 1), 1)
    got = exchange(moved.reshape(64, 16, 256), ZQ).reshape(8, 4, 2, 16, 256)

    low_new = ends[0, :, :, 0]
    span_new = ends[1, :, :, 0] - low_new
    grouped = second_new.reshape(2, 16, 8, 128)
    levels = 15.0 * (grouped - low_new[:, None, :, None]) / span_new[:, None, :, None]
    levels = levels.reshape(2, 16, 1024)
    params_new, update = step(got, olds)
    return (params_new, moment_new, update, levels, low_new, span_new)


def solution(mesh):
    fine = Mesh(mesh.devices.reshape(8, 8, 4, 2), ("rep", "y", "x", "core"))
    return jax.shard_map(
        on_device,
        mesh=fine,
        in_specs=(
            P("rep", None, F, None),
            P(None, F, "rep"),
            P(None, F, None),
            P(None, ("rep",) + F, None),
            P(None, F, "rep"),
            P(None, F, "rep"),
            P(None, "rep"),
            P(None, "rep"),
        ),
        out_specs=(
            P(None, F, None),
            P(None, F, "rep"),
            P(None, F, "rep"),
            P(None, F, "rep"),
            P(None, "rep"),
            P(None, "rep"),
        ),
        check_vma=False,
    )
```

time: 183 us -> 149 us (0.81)
  waiting for transfers between devices: 85.7 us -> 42.3 us
  starting transfers between devices: 39.2 us -> 66.6 us
  between operations: 14.4 us -> 0.93 us
  Pallas kernels: 0 us -> 10.1 us
  local copies, waits for them, and re-layouts: 10.8 us -> 1.48 us
  matrix products: 7.63 us -> 0 us
  blocking collectives: 21.5 us -> 25.9 us
  other arithmetic: 2.68 us -> 0.81 us
    all_to_all x4, waiting for transfers between devices: 56.5 us -> 15.2 us  [exchange(): return lax.all_to_all(blocks, axes, split_axis=0, concat_axis=0, tiled=True)]
    ppermute x0 -> x8, starting transfers between devices: none -> 36.1 us  [the longest x5 21.6 us: shift(): lax.ppermute(block, axis, [(i, (i + by) % size) for i in range(size)])]
    all_gather x2 -> x0, waiting for transfers between devices: 29.1 us -> none  [the longest x1 24 us: on_device(): params_all = lax.all_gather(doubled, 'rep', axis=0)[:, :2]]
    ppermute x0 -> x8, waiting for transfers between devices: none -> 27.1 us  [the longest x3 14.1 us: on_device(): lax.ppermute(values, axis, [(i, i ^ bit) for i in range(size)])]
    pallas_call x0 -> x7, Pallas kernels: none -> 10.1 us  [the longest x1 2.43 us: panels(): pl.pallas_call(panels_kernel, out_shape=shape(8, 4, 2, 16, 384), in_specs...]
    all_to_all x4, starting transfers between devices: 39.2 us -> 30.6 us  [exchange(): return lax.all_to_all(blocks, axes, split_axis=0, concat_axis=0, tiled=True)]
    dot_general x4 -> x0, matrix products: 7.63 us -> none  [the longest x1 3.38 us: on_device(): jnp.einsum('lik,ljk->lij', scaled, right, preferred_element_type=f32)]
    all_to_all x1 -> x2, blocking collectives: 21.5 us -> 25.9 us  [exchange(): return lax.all_to_all(blocks, axes, split_axis=0, concat_axis=0, tiled=True)]
  transfers between devices with their start and end apart: 6 -> 12, of which waited for: 5 -> 6; matrix products, arithmetic and copies ran while one was open for 8% -> 1% of each run, Pallas kernels for 0% -> 2%
where the time goes in v4:
time: 149 us; the launch traced here: 148 us
  starting transfers between devices  66.6 us (45%)
  waiting for transfers between devices  42.3 us (28%)
  blocking collectives  25.9 us (17%)
  Pallas kernels  10.1 us (7%)
    all_to_all x4, starting transfers between devices, exchange(): return lax.all_to_all(blocks, axes, split_axis=0, concat_axis=0, tiled=True)  30.6 us
    all_to_all x2, blocking collectives, exchange(): return lax.all_to_all(blocks, axes, split_axis=0, concat_axis=0, tiled=True)  25.9 us
    ppermute x5, starting transfers between devices, shift(): lax.ppermute(block, axis, [(i, (i + by) % size) for i in range(size)])  21.6 us
    all_to_all x4, waiting for transfers between devices, exchange(): return lax.all_to_all(blocks, axes, split_axis=0, concat_axis=0, tiled=True)  15.2 us
    ppermute x3, starting transfers between devices, on_device(): lax.ppermute(values, axis, [(i, i ^ bit) for i in range(size)])  14.5 us
    ppermute x3, waiting for transfers between devices, on_device(): lax.ppermute(values, axis, [(i, i ^ bit) for i in range(size)])  14.1 us
    ppermute x5, waiting for transfers between devices, shift(): lax.ppermute(block, axis, [(i, (i + by) % size) for i in range(size)])  13 us
  transfers between devices with their start and end apart: 12, of which 6 were waited for; matrix products, arithmetic and copies ran while one was open for 1% of the time, Pallas kernels for 2%

profile of v4, /device:TPU:1, one launch (start us, length us, event | category | flops | bytes accessed | tf_op | source)
XLA Modules:
  0.0 148.2 jit_solution(7774484964289198298)
XLA Ops:
  0.6 2.4 %shard_map.127 = bf16[8,4,2,16,384]{4,3,2,1,0:T(8,128)(2,1)} custom-call(bf16[2,16,8192]{2,1,0:T(8,128)(2,1)} %bitcast.50, bf16[2,16,1024]{2,1,0:T(8,128)(2,1)} %left.1), custom_call_target="tpu_custom_call" | custom-call | tf_op jit(solution)/shard_map/pallas_call | solution.py:76
  3.1 15.0 %all-to-all-start = ((bf16[64,16,384]{2,1,0:T(8,128)(2,1)}), bf16[64,16,384]{2,1,0:T(8,128)(2,1)S(1)}, u32[]{:S(2)}, u32[]{:S(2)}) async-start(bf16[64,16,384]{2,1,0:T(8,128)(2,1)} %bitcast.47), calls=%async_computation | async-start | bytes 1572864 | tf_op jit(solution)/shard_map/all_to_all | solution.py:23
  18.1 2.4 %collective-permute-start = (bf16[16,1024]{1,0:T(8,128)(2,1)S(1)}, bf16[16,1024]{1,0:T(8,128)(2,1)S(1)}, u32[]{:S(2)}, u32[]{:S(2)}) collective-permute-start(bf16[16,1024]{1,0:T(8,128)(2,1)S(1)} %get-tuple-element.51), channel_id=1, source_target_pairs={{0,1},{1,0},{2,3},{3,2},{4,5},{5,4},{6,7},{7,6},{8,9},{9,8},{10,11... | collective-permute-start | bytes 98312 | tf_op jit(solution)/shard_map/ppermute | solution.py:27
  20.4 0.8 collective-permute-done
  21.3 7.5 %collective-permute-start.1 = (bf16[32,1024]{1,0:T(8,128)(2,1)S(1)}, bf16[32,1024]{1,0:T(8,128)(2,1)S(1)}, u32[]{:S(2)}, u32[]{:S(2)}) collective-permute-start(bf16[32,1024]{1,0:T(8,128)(2,1)S(1)} %bitcast.41), channel_id=1, source_target_pairs={{0,32},{8,40},{16,48},{24,56},{32,0},{40,8},{48,16},{56,24},{1,33}... | collective-permute-start | bytes 196616 | tf_op jit(solution)/shard_map/ppermute | solution.py:27
  28.8 2.1 %collective-permute-done.1.far = bf16[32,1024]{1,0:T(8,128)(2,1)S(1)} collective-permute-done((bf16[32,1024]{1,0:T(8,128)(2,1)S(1)}, bf16[32,1024]{1,0:T(8,128)(2,1)S(1)}, u32[]{:S(2)}, u32[]{:S(2)}) %collective-permute-start.1) | collective-permute-done | bytes 65568 | tf_op jit(solution)/shard_map/ppermute | solution.py:27
  30.8 6.6 %collective-permute-start.3 = (bf16[2,32,1024]{2,1,0:T(8,128)(2,1)S(1)}, bf16[2,32,1024]{2,1,0:T(8,128)(2,1)S(1)}, u32[]{:S(2)}, u32[]{:S(2)}) collective-permute-start(bf16[2,32,1024]{2,1,0:T(8,128)(2,1)S(1)} %pad_maximum_fusion.2), channel_id=1, source_target_pairs={{0,56},{8,0},{16,8},{24,16},{32,24},{40,32},{48,40},{56,48},{1,57}... | collective-permute-start | bytes 393224 | tf_op jit(solution)/shard_map/ppermute | solution.py:27
  37.4 1.9 %collective-permute-start.2 = (bf16[2,32,1024]{2,1,0:T(8,128)(2,1)S(1)}, bf16[2,32,1024]{2,1,0:T(8,128)(2,1)S(1)}, u32[]{:S(2)}, u32[]{:S(2)}) collective-permute-start(bf16[2,32,1024]{2,1,0:T(8,128)(2,1)S(1)} %pad_maximum_fusion.2), channel_id=1, source_target_pairs={{0,8},{8,16},{16,24},{24,32},{32,40},{40,48},{48,56},{56,0},{1,9},... | collective-permute-start | bytes 393224 | tf_op jit(solution)/shard_map/ppermute | solution.py:27
  39.4 5.0 %collective-permute-done.2.up = bf16[2,32,1024]{2,1,0:T(8,128)(2,1)S(1)} collective-permute-done((bf16[2,32,1024]{2,1,0:T(8,128)(2,1)S(1)}, bf16[2,32,1024]{2,1,0:T(8,128)(2,1)S(1)}, u32[]{:S(2)}, u32[]{:S(2)}) %collective-permute-start.2) | collective-permute-done | bytes 131104 | tf_op jit(solution)/shard_map/ppermute | solution.py:27
  44.3 1.2 shard_map.128
  45.6 3.6 %all-to-all-start.1 = ((bf16[8,128,256]{2,1,0:T(8,128)(2,1)}), bf16[8,128,256]{2,1,0:T(8,128)(2,1)S(1)}, u32[]{:S(2)}, u32[]{:S(2)}) async-start(bf16[8,128,256]{2,1,0:T(8,128)(2,1)} %bitcast.8), calls=%async_computation.1 | async-start | bytes 1048576 | tf_op jit(solution)/shard_map/all_to_all | solution.py:23
  49.2 3.3 %collective-permute-start.4 = (bf16[2,32,1024]{2,1,0:T(8,128)(2,1)S(1)}, bf16[2,32,1024]{2,1,0:T(8,128)(2,1)S(1)}, u32[]{:S(2)}, u32[]{:S(2)}) collective-permute-start(bf16[2,32,1024]{2,1,0:T(8,128)(2,1)S(1)} %collective-permute-done.2.up), channel_id=1, source_target_pairs={{0,8},{8,16},{16,24},{24,32},{32,40},{40,48},{48,56},{56,0},{1,9},... | collective-permute-start | bytes 393224 | tf_op jit(solution)/shard_map/ppermute | solution.py:27
  52.5 7.2 %collective-permute-start.5 = (bf16[1,2,16,1024]{3,2,1,0:T(8,128)(2,1)S(1)}, bf16[1,2,16,1024]{3,2,1,0:T(8,128)(2,1)S(1)}, u32[]{:S(2)}, u32[]{:S(2)}) collective-permute-start(bf16[1,2,16,1024]{3,2,1,0:T(8,128)(2,1)S(1)} %bitcast.53), channel_id=1, source_target_pairs={{0,256},{64,320},{128,384},{192,448},{256,0},{320,64},{384,128},{4... | collective-permute-start | bytes 196616 | tf_op jit(solution)/shard_map/ppermute | solution.py:301
  59.7 5.1 %collective-permute-done.4.more = bf16[2,32,1024]{2,1,0:T(8,128)(2,1)S(1)} collective-permute-done((bf16[2,32,1024]{2,1,0:T(8,128)(2,1)S(1)}, bf16[2,32,1024]{2,1,0:T(8,128)(2,1)S(1)}, u32[]{:S(2)}, u32[]{:S(2)}) %collective-permute-start.4) | collective-permute-done | bytes 131104 | tf_op jit(solution)/shard_map/ppermute | solution.py:27
  64.8 1.1 shard_map.129
  66.0 15.0 %all_to_all.30 = bf16[8,16,1024]{2,1,0:T(8,128)(2,1)S(1)} all-to-all(bf16[8,16,1024]{2,1,0:T(8,128)(2,1)S(1)} %bitcast.45), channel_id=1, replica_groups=mesh['rep'=8,'y'=8,'x'=4,'core'=2] {'x','core'}, dimensions={0} | all-to-all | bytes 524288 | tf_op jit(solution)/shard_map/all_to_all | solution.py:23
  81.0 0.7 copy-done.2
  81.6 1.5 %shard_map.130 = (bf16[4,2,160,128]{3,2,1,0:T(8,128)(2,1)S(1)}, f32[2,16,1024]{2,1,0:T(8,128)}, f32[2,16,1024]{2,1,0:T(8,128)S(1)}) custom-call(bf16[4,2,16,1024]{3,2,1,0:T(8,128)(2,1)S(1)} %bitcast.40, f32[2,16,1024]{2,1,0:T(8,128)S(1)} %copy-done, s32[2,16,1024]{2,1,0:T(8,128)S(1)} %copy-done.1, f32[2,8]{1,0:T(2,128)S(1)} %copy-done.2, f32[2,8]{1,0:T(2,128)S(1)} %copy-done.3), custom_call_target="tpu_custom_call" | custom-call | tf_op jit(solution)/shard_map/pallas_call | solution.py:179
  83.1 10.9 %all_to_all.31.got = bf16[8,160,128]{2,1,0:T(8,128)(2,1)S(1)} all-to-all(bf16[8,160,128]{2,1,0:T(8,128)(2,1)S(1)} %bitcast.44), channel_id=1, replica_groups=mesh['rep'=8,'y'=8,'x'=4,'core'=2] {'x','core'}, dimensions={0} | all-to-all | bytes 655360 | tf_op jit(solution)/shard_map/all_to_all | solution.py:23
  94.0 1.3 shard_map.131
  95.3 3.5 %all-to-all-start.4 = ((bf16[8,288,128]{2,1,0:T(8,128)(2,1)}), bf16[8,288,128]{2,1,0:T(8,128)(2,1)S(1)}, u32[]{:S(2)}, u32[]{:S(2)}) async-start(bf16[8,288,128]{2,1,0:T(8,128)(2,1)} %shard_map.131), calls=%async_computation.4 | async-start | bytes 1179648 | tf_op jit(solution)/shard_map/all_to_all | solution.py:23
  98.9 4.0 %collective-permute-start.6 = (bf16[2,2,16,1024]{3,2,1,0:T(8,128)(2,1)S(1)}, bf16[2,2,16,1024]{3,2,1,0:T(8,128)(2,1)S(1)}, u32[]{:S(2)}, u32[]{:S(2)}) collective-permute-start(bf16[2,2,16,1024]{3,2,1,0:T(8,128)(2,1)S(1)} %get-tuple-element.38), channel_id=1, source_target_pairs={{0,128},{64,192},{128,0},{192,64},{256,384},{320,448},{384,256},{4... | collective-permute-start | bytes 393224 | tf_op jit(solution)/shard_map/ppermute | solution.py:301
  102.9 15.2 %all-to-all-done.4.got = bf16[8,288,128]{2,1,0:T(8,128)(2,1)S(1)} async-done(((bf16[8,288,128]{2,1,0:T(8,128)(2,1)}), bf16[8,288,128]{2,1,0:T(8,128)(2,1)S(1)}, u32[]{:S(2)}, u32[]{:S(2)}) %all-to-all-start.4) | async-done | bytes 589856 | tf_op jit(solution)/shard_map/all_to_all | solution.py:23
  118.1 1.2 shard_map.132
  119.4 8.4 %all-to-all-start.5 = ((bf16[64,16,256]{2,1,0:T(8,128)(2,1)}), bf16[64,16,256]{2,1,0:T(8,128)(2,1)S(1)}, u32[]{:S(2)}, u32[]{:S(2)}) async-start(bf16[64,16,256]{2,1,0:T(8,128)(2,1)} %bitcast.16), calls=%async_computation.5 | async-start | bytes 1048576 | tf_op jit(solution)/shard_map/all_to_all | solution.py:23
  127.8 0.1 slice_reduce_fusion.1
  127.9 3.3 %collective-permute-start.7 = (bf16[4,2,16,1024]{3,2,1,0:T(8,128)(2,1)S(1)}, bf16[4,2,16,1024]{3,2,1,0:T(8,128)(2,1)S(1)}, u32[]{:S(2)}, u32[]{:S(2)}) collective-permute-start(bf16[4,2,16,1024]{3,2,1,0:T(8,128)(2,1)S(1)} %bitcast.48), channel_id=1, source_target_pairs={{0,64},{64,0},{128,192},{192,128},{256,320},{320,256},{384,448},{4... | collective-permute-start | bytes 786440 | tf_op jit(solution)/shard_map/ppermute | solution.py:301
  131.3 0.1 broadcast_bitcast_fusion.1
  131.3 0.5 copy-done.7
  131.9 0.7 multiply_divide_fusion
  132.6 14.1 %collective-permute-done.7 = bf16[4,2,16,1024]{3,2,1,0:T(8,128)(2,1)S(1)} collective-permute-done((bf16[4,2,16,1024]{3,2,1,0:T(8,128)(2,1)S(1)}, bf16[4,2,16,1024]{3,2,1,0:T(8,128)(2,1)S(1)}, u32[]{:S(2)}, u32[]{:S(2)}) %collective-permute-start.7) | collective-permute-done | bytes 262176 | tf_op jit(solution)/shard_map/ppermute | solution.py:301
  146.8 1.4 shard_map.133
  (30 shorter events, 0.3 us)
Async XLA Ops:
  3.1 15.0 %copy-start.4 = (bf16[2,16,1024]{2,1,0:T(8,128)(2,1)S(1)}, bf16[2,16,1024]{2,1,0:T(8,128)(2,1)}, u32[]{:S(2)}) copy-start(bf16[2,16,1024]{2,1,0:T(8,128)(2,1)} %param.11) | copy-start | bytes 196612
  3.1 41.3 %all-to-all-start = ((bf16[64,16,384]{2,1,0:T(8,128)(2,1)}), bf16[64,16,384]{2,1,0:T(8,128)(2,1)S(1)}, u32[]{:S(2)}, u32[]{:S(2)}) async-start(bf16[64,16,384]{2,1,0:T(8,128)(2,1)} %bitcast.47), calls=%async_computation | async-start | bytes 1572864 | tf_op jit(solution)/shard_map/all_to_all | solution.py:23
  18.1 3.2 %collective-permute-start = (bf16[16,1024]{1,0:T(8,128)(2,1)S(1)}, bf16[16,1024]{1,0:T(8,128)(2,1)S(1)}, u32[]{:S(2)}, u32[]{:S(2)}) collective-permute-start(bf16[16,1024]{1,0:T(8,128)(2,1)S(1)} %get-tuple-element.51), channel_id=1, source_target_pairs={{0,1},{1,0},{2,3},{3,2},{4,5},{5,4},{6,7},{7,6},{8,9},{9,8},{10,11... | collective-permute-start | bytes 98312 | tf_op jit(solution)/shard_map/ppermute | solution.py:27
  21.3 9.5 %collective-permute-start.1 = (bf16[32,1024]{1,0:T(8,128)(2,1)S(1)}, bf16[32,1024]{1,0:T(8,128)(2,1)S(1)}, u32[]{:S(2)}, u32[]{:S(2)}) collective-permute-start(bf16[32,1024]{1,0:T(8,128)(2,1)S(1)} %bitcast.41), channel_id=1, source_target_pairs={{0,32},{8,40},{16,48},{24,56},{32,0},{40,8},{48,16},{56,24},{1,33}... | collective-permute-start | bytes 196616 | tf_op jit(solution)/shard_map/ppermute | solution.py:27
  30.8 8.5 %collective-permute-start.3 = (bf16[2,32,1024]{2,1,0:T(8,128)(2,1)S(1)}, bf16[2,32,1024]{2,1,0:T(8,128)(2,1)S(1)}, u32[]{:S(2)}, u32[]{:S(2)}) collective-permute-start(bf16[2,32,1024]{2,1,0:T(8,128)(2,1)S(1)} %pad_maximum_fusion.2), channel_id=1, source_target_pairs={{0,56},{8,0},{16,8},{24,16},{32,24},{40,32},{48,40},{56,48},{1,57}... | collective-permute-start | bytes 393224 | tf_op jit(solution)/shard_map/ppermute | solution.py:27
  37.4 6.9 %collective-permute-start.2 = (bf16[2,32,1024]{2,1,0:T(8,128)(2,1)S(1)}, bf16[2,32,1024]{2,1,0:T(8,128)(2,1)S(1)}, u32[]{:S(2)}, u32[]{:S(2)}) collective-permute-start(bf16[2,32,1024]{2,1,0:T(8,128)(2,1)S(1)} %pad_maximum_fusion.2), channel_id=1, source_target_pairs={{0,8},{8,16},{16,24},{24,32},{32,40},{40,48},{48,56},{56,0},{1,9},... | collective-permute-start | bytes 393224 | tf_op jit(solution)/shard_map/ppermute | solution.py:27
  45.6 6.9 %copy-start.5 = (bf16[2,16,1024]{2,1,0:T(8,128)(2,1)S(1)}, bf16[2,16,1024]{2,1,0:T(8,128)(2,1)}, u32[]{:S(2)}) copy-start(bf16[2,16,1024]{2,1,0:T(8,128)(2,1)} %param.9) | copy-start | bytes 196612
  45.6 19.2 %all-to-all-start.1 = ((bf16[8,128,256]{2,1,0:T(8,128)(2,1)}), bf16[8,128,256]{2,1,0:T(8,128)(2,1)S(1)}, u32[]{:S(2)}, u32[]{:S(2)}) async-start(bf16[8,128,256]{2,1,0:T(8,128)(2,1)} %bitcast.8), calls=%async_computation.1 | async-start | bytes 1048576 | tf_op jit(solution)/shard_map/all_to_all | solution.py:23
  49.2 15.6 %collective-permute-start.4 = (bf16[2,32,1024]{2,1,0:T(8,128)(2,1)S(1)}, bf16[2,32,1024]{2,1,0:T(8,128)(2,1)S(1)}, u32[]{:S(2)}, u32[]{:S(2)}) collective-permute-start(bf16[2,32,1024]{2,1,0:T(8,128)(2,1)S(1)} %collective-permute-done.2.up), channel_id=1, source_target_pairs={{0,8},{8,16},{16,24},{24,32},{32,40},{40,48},{48,56},{56,0},{1,9},... | collective-permute-start | bytes 393224 | tf_op jit(solution)/shard_map/ppermute | solution.py:27
  52.5 13.4 %collective-permute-start.5 = (bf16[1,2,16,1024]{3,2,1,0:T(8,128)(2,1)S(1)}, bf16[1,2,16,1024]{3,2,1,0:T(8,128)(2,1)S(1)}, u32[]{:S(2)}, u32[]{:S(2)}) collective-permute-start(bf16[1,2,16,1024]{3,2,1,0:T(8,128)(2,1)S(1)} %bitcast.53), channel_id=1, source_target_pairs={{0,256},{64,320},{128,384},{192,448},{256,0},{320,64},{384,128},{4... | collective-permute-start | bytes 196616 | tf_op jit(solution)/shard_map/ppermute | solution.py:301
  65.9 15.0 %copy-start = (f32[2,16,1024]{2,1,0:T(8,128)S(1)}, f32[2,16,1024]{2,1,0:T(8,128)}, u32[]{:S(2)}) copy-start(f32[2,16,1024]{2,1,0:T(8,128)} %moment.1) | copy-start | bytes 393220
  65.9 15.0 %copy-start.1 = (s32[2,16,1024]{2,1,0:T(8,128)S(1)}, s32[2,16,1024]{2,1,0:T(8,128)}, u32[]{:S(2)}) copy-start(s32[2,16,1024]{2,1,0:T(8,128)} %codes.1) | copy-start | bytes 393220
  65.9 15.0 %copy-start.3 = (f32[2,8]{1,0:T(2,128)S(1)}, f32[2,8]{1,0:T(2,128)}, u32[]{:S(2)}) copy-start(f32[2,8]{1,0:T(2,128)} %span.1) | copy-start | bytes 196
  80.9 0.7 copy-start.2
  95.3 22.8 %all-to-all-start.4 = ((bf16[8,288,128]{2,1,0:T(8,128)(2,1)}), bf16[8,288,128]{2,1,0:T(8,128)(2,1)S(1)}, u32[]{:S(2)}, u32[]{:S(2)}) async-start(bf16[8,288,128]{2,1,0:T(8,128)(2,1)} %shard_map.131), calls=%async_computation.4 | async-start | bytes 1179648 | tf_op jit(solution)/shard_map/all_to_all | solution.py:23
  98.9 20.5 %collective-permute-start.6 = (bf16[2,2,16,1024]{3,2,1,0:T(8,128)(2,1)S(1)}, bf16[2,2,16,1024]{3,2,1,0:T(8,128)(2,1)S(1)}, u32[]{:S(2)}, u32[]{:S(2)}) collective-permute-start(bf16[2,2,16,1024]{3,2,1,0:T(8,128)(2,1)S(1)} %get-tuple-element.38), channel_id=1, source_target_pairs={{0,128},{64,192},{128,0},{192,64},{256,384},{320,448},{384,256},{4... | collective-permute-start | bytes 393224 | tf_op jit(solution)/shard_map/ppermute | solution.py:301
  119.4 27.4 %all-to-all-start.5 = ((bf16[64,16,256]{2,1,0:T(8,128)(2,1)}), bf16[64,16,256]{2,1,0:T(8,128)(2,1)S(1)}, u32[]{:S(2)}, u32[]{:S(2)}) async-start(bf16[64,16,256]{2,1,0:T(8,128)(2,1)} %bitcast.16), calls=%async_computation.5 | async-start | bytes 1048576 | tf_op jit(solution)/shard_map/all_to_all | solution.py:23
  127.9 3.3 %copy-start.6 = (f32[2,8]{1,0:T(2,128)}, f32[2,8]{1,0:T(2,128)S(1)}, u32[]{:S(2)}) copy-start(f32[2,8]{1,0:T(2,128)S(1)} %get-tuple-element.46) | copy-start | bytes 196
  127.9 18.7 %collective-permute-start.7 = (bf16[4,2,16,1024]{3,2,1,0:T(8,128)(2,1)S(1)}, bf16[4,2,16,1024]{3,2,1,0:T(8,128)(2,1)S(1)}, u32[]{:S(2)}, u32[]{:S(2)}) collective-permute-start(bf16[4,2,16,1024]{3,2,1,0:T(8,128)(2,1)S(1)} %bitcast.48), channel_id=1, source_target_pairs={{0,64},{64,0},{128,192},{192,128},{256,320},{320,256},{384,448},{4... | collective-permute-start | bytes 786440 | tf_op jit(solution)/shard_map/ppermute | solution.py:301
  131.3 0.6 copy-start.7

commit v5 on v4

v5 whole, which is shorter than its diff:
```python
import jax
import jax.numpy as jnp
from jax import lax
from jax.experimental import pallas as pl
from jax.experimental.pallas import tpu as pltpu
from jax.sharding import Mesh, PartitionSpec as P

F = ("pair", "odd", "x", "core")
A = ("odd", "x")
ZB = ("rep", "pair", "core")
B = ("pair", "core")
BF16, F32 = jnp.bfloat16, jnp.float32
VMEM = pl.BlockSpec(memory_space=pltpu.VMEM)
ANY = pl.BlockSpec(memory_space=pl.ANY)
PARAMS = pltpu.CompilerParams(vmem_limit_bytes=32 * 1024 * 1024)


def shape(*dims, of=BF16):
    return jax.ShapeDtypeStruct(dims, of)


def exchange(blocks, axes):
    return lax.all_to_all(blocks, axes, split_axis=0, concat_axis=0, tiled=True)


def shift(block, axis, size, by):
    return lax.ppermute(block, axis, [(i, (i + by) % size) for i in range(size)])


def pull(refs, places, sems):
    copies = [
        pltpu.make_async_copy(ref, place, sems.at[i])
        for i, (ref, place) in enumerate(zip(refs, places))
    ]
    for copy in copies:
        copy.start()

    def wait():
        for copy in copies:
            copy.wait()

    return wait


def panels_kernel(grads, left, out):
    eighth = pl.ds(pl.multiple_of(lax.axis_index("rep") * 128, 128), 128)
    basis = left[:, :, eighth]
    for panel in range(32):
        out[panel, :, :, 0:256] = grads[:, :, panel * 256 : panel * 256 + 256]
        out[panel, :, :, 256:384] = basis


def panels(grads, left):
    return pl.pallas_call(
        panels_kernel, out_shape=shape(32, 2, 16, 384), in_specs=[VMEM, VMEM], out_specs=VMEM
    )(grads, left)


def left_kernel(grads, out, left, held, sems):
    wait = pull([grads], [held], sems)
    wait()
    total = held[0, :, 0:256].astype(F32)
    for replica in range(1, 8):
        total += held[replica, :, 0:256].astype(F32)
    for replica in range(8):
        left[:, replica * 128 : replica * 128 + 128] = held[replica, :, 256:384]
    part = lax.dot_general(
        left[...], total.astype(BF16), (((0,), (0,)), ((), ())), preferred_element_type=F32
    )
    part = part.astype(BF16)
    for to in range(8):
        for pair in range(4):
            start = pair * 256 + to * 32
            out[to, pair * 32 : pair * 32 + 32] = part[start : start + 32]


def left_part(grads):
    return pl.pallas_call(
        left_kernel,
        out_shape=(shape(8, 128, 256), shape(128, 1024)),
        in_specs=[ANY],
        out_specs=(VMEM, VMEM),
        scratch_shapes=[pltpu.VMEM((8, 128, 384), BF16), pltpu.SemaphoreType.DMA((1,))],
        compiler_params=PARAMS,
    )(grads)


def right_kernel(got, near, away, out, right_out, held, right, sems):
    odd, x = lax.axis_index("odd"), lax.axis_index("x")
    ring, places = [], []
    for bits in range(8):
        block = (near, away)[bits % 2]
        ring.append(block.at[bits // 4, bits // 2 % 2])
        to = jnp.bitwise_xor(odd, bits // 4) * 4 + jnp.bitwise_xor(x, bits % 4)
        places.append(right.at[to])
    wait = pull([got] + ring, [held] + places, sems)
    wait()
    total = held[0].astype(F32)
    for part in range(1, 8):
        total += held[part].astype(F32)
    basis = right[...].reshape(256, 1024)
    out[...] = jnp.dot(total.astype(BF16), basis, preferred_element_type=F32).astype(BF16)
    right_out[...] = basis


def right_part(got, near, away):
    return pl.pallas_call(
        right_kernel,
        out_shape=(shape(128, 1024), shape(256, 1024)),
        in_specs=[ANY] * 3,
        out_specs=(VMEM, VMEM),
        scratch_shapes=[
            pltpu.VMEM((8, 128, 256), BF16),
            pltpu.VMEM((8, 32, 1024), BF16),
            pltpu.SemaphoreType.DMA((9,)),
        ],
        compiler_params=PARAMS,
    )(got, near, away)


def ends_tile(layers):
    lane = lax.broadcasted_iota(jnp.int32, (16, 128), 1)
    tile = jnp.zeros((16, 128), F32)
    for layer, ends in enumerate(layers):
        first = ends.astype(BF16).astype(F32)
        second = (ends - first).astype(BF16).astype(F32)
        third = ends - first - second
        for i, piece in enumerate((first, second, third)):
            tile = jnp.where(lane == layer * 3 + i, piece, tile)
    return tile.astype(BF16)


def ends_of(tiles):
    values = tiles.astype(F32)
    lane = lax.broadcasted_iota(jnp.int32, values.shape, 2)
    layers = []
    for mine in (lane < 3, lane >= 3):
        total = jnp.sum(jnp.where(mine, values, 0.0), axis=2, keepdims=True)
        layers.append((jnp.min(total[:, 0:8], axis=0), jnp.max(total[:, 8:16], axis=0)))
    return layers


def moments_kernel(got, moment, codes, low, span, out, moment_new, second_new, held, sems):
    wait = pull([got], [held], sems)
    wait()
    ends = []
    for layer in range(2):
        lows, highs = [], []
        for group in range(8):
            lanes = slice(group * 128, group * 128 + 128)
            turn = held[0, layer, :, lanes].astype(F32)
            for part in range(1, 4):
                turn += held[part, layer, :, lanes].astype(F32)
            mean = 0.9 * moment[layer, :, lanes] + 0.1 * turn
            code = codes[layer, :, lanes].astype(F32)
            at = (slice(layer, layer + 1), slice(group, group + 1))
            second = low[at] + code / 15.0 * span[at]
            second = 0.95 * second + 0.05 * turn * turn
            moment_new[layer, :, lanes] = mean
            second_new[layer, :, lanes] = second
            scaled = (mean / (jnp.sqrt(second) + 1e-08)).astype(BF16)
            for copy in range(4):
                out[copy, layer, group * 16 : group * 16 + 16] = scaled
            lows.append(jnp.min(second, axis=0, keepdims=True))
            highs.append(jnp.max(second, axis=0, keepdims=True))
        lows = jnp.min(jnp.concatenate(lows, axis=0), axis=1, keepdims=True)
        highs = jnp.max(jnp.concatenate(highs, axis=0), axis=1, keepdims=True)
        ends.append(jnp.concatenate([lows, highs], axis=0))
    tile = ends_tile(ends)
    for copy in range(4):
        for to in range(2):
            out[copy, to, 128:144] = tile


def moments(got, moment, codes, low, span):
    return pl.pallas_call(
        moments_kernel,
        out_shape=(
            shape(4, 2, 144, 128),
            shape(2, 16, 1024, of=F32),
            shape(2, 16, 1024, of=F32),
        ),
        in_specs=[ANY] + [VMEM] * 4,
        out_specs=(VMEM, VMEM, VMEM),
        scratch_shapes=[pltpu.VMEM((4, 2, 16, 1024), BF16), pltpu.SemaphoreType.DMA((1,))],
        compiler_params=PARAMS,
    )(got, moment, codes, low, span)


def back_kernel(got, right, out, held, sems):
    wait = pull([got], [held], sems)
    wait()
    rows = [held[:, at * 16 : at * 16 + 16, :].reshape(128, 128) for at in range(8)]
    returned = lax.dot_general(
        jnp.concatenate(rows, axis=1), right[...], (((1,), (1,)), ((), ())), preferred_element_type=F32
    ).astype(BF16)
    tile = ends_tile([jnp.concatenate(ends, axis=0) for ends in ends_of(held[:, 128:144, :])])
    for copy in range(8):
        out[copy, 0:128] = returned[:, 0:128]
        out[copy, 128:256] = returned[:, 128:256]
        out[copy, 256:272] = tile


def back_part(got, right):
    return pl.pallas_call(
        back_kernel,
        out_shape=shape(8, 272, 128),
        in_specs=[ANY, VMEM],
        out_specs=VMEM,
        scratch_shapes=[pltpu.VMEM((8, 144, 128), BF16), pltpu.SemaphoreType.DMA((1,))],
        compiler_params=PARAMS,
    )(got, right)


def update_kernel(got, left, out, ends, held, back, sems):
    wait = pull([got], [held], sems)
    wait()
    for half in range(2):
        for pair in range(4):
            start = half * 128 + pair * 32
            rows = held[:, start : start + 32, :].reshape(256, 128)
            back[pair * 256 : pair * 256 + 256, half * 128 : half * 128 + 128] = rows
    moved = jnp.dot(left[...], back[...], preferred_element_type=F32).astype(BF16).reshape(8, 16, 256)
    for copy in range(8):
        out[copy] = moved
    for layer, (low, high) in enumerate(ends_of(held[:, 256:272, :])):
        ends[0, layer] = jnp.broadcast_to(low, (8, 128))
        ends[1, layer] = jnp.broadcast_to(high, (8, 128))


def update_part(got, left):
    return pl.pallas_call(
        update_kernel,
        out_shape=(shape(8, 8, 16, 256), shape(2, 2, 8, 128, of=F32)),
        in_specs=[ANY, VMEM],
        out_specs=(VMEM, VMEM),
        scratch_shapes=[
            pltpu.VMEM((8, 272, 128), BF16),
            pltpu.VMEM((1024, 256), BF16),
            pltpu.SemaphoreType.DMA((1,)),
        ],
        compiler_params=PARAMS,
    )(got, left)


def step_kernel(got, olds, params_new, update, held, sems):
    rep = lax.axis_index("rep")
    wait = pull([got], [held], sems)
    wait()
    for panel in range(4):
        lanes = slice(panel * 256, panel * 256 + 256)
        update[:, :, lanes] = held[rep, panel].astype(F32)
        for block in range(8):
            change = held[block, panel].astype(F32)
            old = olds[jnp.bitwise_xor(rep, block), :, :, lanes].astype(F32)
            new = old * (1.0 - 0.05 * 0.1) - 0.05 * change
            start = block * 1024 + panel * 256
            params_new[:, :, start : start + 256] = new.astype(BF16)


def step(got, olds):
    return pl.pallas_call(
        step_kernel,
        out_shape=(shape(2, 16, 8192), shape(2, 16, 1024, of=F32)),
        in_specs=[ANY, VMEM],
        out_specs=(VMEM, VMEM),
        scratch_shapes=[pltpu.VMEM((8, 4, 2, 16, 256), BF16), pltpu.SemaphoreType.DMA((1,))],
        compiler_params=PARAMS,
    )(got, olds)


def on_device(grads, params, left_basis, right_basis, moment, codes, level_low, level_span):
    core = lax.axis_index("core")
    pick = lambda values, at: lax.dynamic_index_in_dim(values, at, 0, keepdims=False)
    both = lambda here, there: jnp.where(core == 0, jnp.stack([here, there]), jnp.stack([there, here]))
    swap = lambda values: shift(values, "core", 2, 1)
    flip = lambda values, axis, size, bit: lax.ppermute(values, axis, [(i, i ^ bit) for i in range(size)])
    tie = lax.optimization_barrier

    right = both(pick(right_basis, core), swap(pick(right_basis, 1 - core))).reshape(1, 32, 1024)
    right = jnp.concatenate([right, flip(right, "x", 4, 2)])[None]
    near = jnp.concatenate([right, flip(right, "odd", 2, 1)])
    away = flip(near, "x", 4, 1)

    sent = panels(grads[0], left_basis)
    got = exchange(sent.reshape(64, 16, 384), ZB)
    got, near = tie((got, near))
    part, left_rows = left_part(got.reshape(8, 128, 384))

    def joined(olds, other, bit):
        return jnp.stack([olds, other], 1).reshape(8 // bit, 2, 16, 1024)

    olds = params[None]

    got = exchange(part, A)
    turned, right_rows = right_part(got, near, away)
    turned, other = tie((turned, flip(tie((olds, part))[0], "rep", 8, 4)))
    olds = joined(olds, other, 4)
    got = exchange(turned.reshape(8, 16, 1024), B).reshape(4, 2, 16, 1024)
    block, moment_new, second_new = moments(got, moment, codes, level_low, level_span)
    got = exchange(block.reshape(8, 144, 128), B)
    block = back_part(got, right_rows)
    got = exchange(block, A)
    moved, ends = update_part(got, left_rows)
    moved, other = tie((moved, flip(tie((olds, block))[0], "rep", 8, 2)))
    olds = joined(olds, other, 2)
    olds = joined(olds, flip(olds, "rep", 8, 1), 1)
    got = exchange(moved.reshape(64, 16, 256), ZB).reshape(8, 4, 2, 16, 256)

    low_new = ends[0, :, :, 0]
    span_new = ends[1, :, :, 0] - low_new
    grouped = second_new.reshape(2, 16, 8, 128)
    levels = 15.0 * (grouped - low_new[:, None, :, None]) / span_new[:, None, :, None]
    levels = levels.reshape(2, 16, 1024)
    params_new, update = step(got, olds)
    return (params_new, moment_new, update, levels, low_new, span_new)


def solution(mesh):
    fine = Mesh(mesh.devices.reshape(8, 4, 2, 4, 2), ("rep",) + F)
    return jax.shard_map(
        on_device,
        mesh=fine,
        in_specs=(
            P("rep", None, F, None),
            P(None, F, "rep"),
            P(None, F, None),
            P(None, ("rep",) + F, None),
            P(None, F, "rep"),
            P(None, F, "rep"),
            P(None, "rep"),
            P(None, "rep"),
        ),
        out_specs=(
            P(None, F, None),
            P(None, F, "rep"),
            P(None, F, "rep"),
            P(None, F, "rep"),
            P(None, "rep"),
            P(None, "rep"),
        ),
        check_vma=False,
    )
```

time: 149 us -> 145 us (0.973)
  starting transfers between devices: 66.6 us -> 54 us
  blocking collectives: 25.9 us -> 32.1 us
  waiting for transfers between devices: 42.3 us -> 45.5 us
    ppermute x5 -> x1, starting transfers between devices: 21.6 us -> 2.36 us  [shift(): lax.ppermute(block, axis, [(i, (i + by) % size) for i in range(size)])]
    ppermute x3 -> x6, waiting for transfers between devices: 14.1 us -> 32.5 us  [on_device(): lax.ppermute(values, axis, [(i, i ^ bit) for i in range(size)])]
    ppermute x5 -> x1, waiting for transfers between devices: 13 us -> 0.83 us  [shift(): lax.ppermute(block, axis, [(i, (i + by) % size) for i in range(size)])]
    all_to_all x2, blocking collectives: 25.9 us -> 32.1 us  [exchange(): return lax.all_to_all(blocks, axes, split_axis=0, concat_axis=0, tiled=True)]
    ppermute x3 -> x6, starting transfers between devices: 14.5 us -> 19 us  [on_device(): lax.ppermute(values, axis, [(i, i ^ bit) for i in range(size)])]
    all_to_all x4, waiting for transfers between devices: 15.2 us -> 12.1 us  [exchange(): return lax.all_to_all(blocks, axes, split_axis=0, concat_axis=0, tiled=True)]
    all_to_all x4, starting transfers between devices: 30.6 us -> 32.6 us  [exchange(): return lax.all_to_all(blocks, axes, split_axis=0, concat_axis=0, tiled=True)]
  transfers between devices with their start and end apart: 12 -> 11, of which waited for: 6 -> 8; matrix products, arithmetic and copies ran while one was open for 1% -> 1% of each run, Pallas kernels for 2% -> 2%
where the time goes in v5:
time: 145 us; the launch traced here: 143 us
  starting transfers between devices  54 us (37%)
  waiting for transfers between devices  45.5 us (31%)
  blocking collectives  32.1 us (22%)
  Pallas kernels  8.62 us (6%)
  local copies, waits for them, and re-layouts  1.48 us (1%)
    all_to_all x4, starting transfers between devices, exchange(): return lax.all_to_all(blocks, axes, split_axis=0, concat_axis=0, tiled=True)  32.6 us
    ppermute x6, waiting for transfers between devices, on_device(): lax.ppermute(values, axis, [(i, i ^ bit) for i in range(size)])  32.5 us
    all_to_all x2, blocking collectives, exchange(): return lax.all_to_all(blocks, axes, split_axis=0, concat_axis=0, tiled=True)  32.1 us
    ppermute x6, starting transfers between devices, on_device(): lax.ppermute(values, axis, [(i, i ^ bit) for i in range(size)])  19 us
    all_to_all x4, waiting for transfers between devices, exchange(): return lax.all_to_all(blocks, axes, split_axis=0, concat_axis=0, tiled=True)  12.1 us
  transfers between devices with their start and end apart: 11, of which 8 were waited for; matrix products, arithmetic and copies ran while one was open for 1% of the time, Pallas kernels for 2%

profile of v5, /device:TPU:1, one launch (start us, length us, event | category | flops | bytes accessed | tf_op | source)
XLA Modules:
  0.0 143.4 jit_solution(7418208711612346309)
XLA Ops:
  0.6 2.0 %shard_map.127 = bf16[32,2,16,384]{3,2,1,0:T(8,128)(2,1)} custom-call(bf16[2,16,8192]{2,1,0:T(8,128)(2,1)} %bitcast.45, bf16[2,16,1024]{2,1,0:T(8,128)(2,1)} %left.1), custom_call_target="tpu_custom_call" | custom-call | tf_op jit(solution)/shard_map/pallas_call | solution.py:54
  2.6 17.8 %all-to-all-start = ((bf16[64,16,384]{2,1,0:T(8,128)(2,1)}), bf16[64,16,384]{2,1,0:T(8,128)(2,1)S(1)}, u32[]{:S(2)}, u32[]{:S(2)}) async-start(bf16[64,16,384]{2,1,0:T(8,128)(2,1)} %bitcast.42), calls=%async_computation | async-start | bytes 1572864 | tf_op jit(solution)/shard_map/all_to_all | solution.py:23
  20.4 2.4 %collective-permute-start = (bf16[16,1024]{1,0:T(8,128)(2,1)S(1)}, bf16[16,1024]{1,0:T(8,128)(2,1)S(1)}, u32[]{:S(2)}, u32[]{:S(2)}) collective-permute-start(bf16[16,1024]{1,0:T(8,128)(2,1)S(1)} %get-tuple-element.49), channel_id=1, source_target_pairs={{0,1},{1,0},{2,3},{3,2},{4,5},{5,4},{6,7},{7,6},{8,9},{9,8},{10,11... | collective-permute-start | bytes 98312 | tf_op jit(solution)/shard_map/ppermute | solution.py:27
  22.8 0.8 collective-permute-done
  23.7 4.7 %collective-permute-start.1 = (bf16[1,32,1024]{2,1,0:T(8,128)(2,1)S(1)}, bf16[1,32,1024]{2,1,0:T(8,128)(2,1)S(1)}, u32[]{:S(2)}, u32[]{:S(2)}) collective-permute-start(bf16[1,32,1024]{2,1,0:T(8,128)(2,1)S(1)} %bitcast.46), channel_id=1, source_target_pairs={{0,4},{2,6},{4,0},{6,2},{1,5},{3,7},{5,1},{7,3},{8,12},{10,14},{12... | collective-permute-start | bytes 196616 | tf_op jit(solution)/shard_map/ppermute | solution.py:277
  28.3 2.1 %collective-permute-done.1 = bf16[1,32,1024]{2,1,0:T(8,128)(2,1)S(1)} collective-permute-done((bf16[1,32,1024]{2,1,0:T(8,128)(2,1)S(1)}, bf16[1,32,1024]{2,1,0:T(8,128)(2,1)S(1)}, u32[]{:S(2)}, u32[]{:S(2)}) %collective-permute-start.1) | collective-permute-done | bytes 65568 | tf_op jit(solution)/shard_map/ppermute | solution.py:277
  30.5 2.3 %collective-permute-start.2 = (bf16[1,2,32,1024]{3,2,1,0:T(8,128)(2,1)S(1)}, bf16[1,2,32,1024]{3,2,1,0:T(8,128)(2,1)S(1)}, u32[]{:S(2)}, u32[]{:S(2)}) collective-permute-start(bf16[1,2,32,1024]{3,2,1,0:T(8,128)(2,1)S(1)} %maximum_bitcast_fusion), channel_id=1, source_target_pairs={{0,8},{8,0},{1,9},{9,1},{2,10},{10,2},{3,11},{11,3},{4,12},{12,4},... | collective-permute-start | bytes 393224 | tf_op jit(solution)/shard_map/ppermute | solution.py:277
  32.8 7.9 %collective-permute-done.2 = bf16[1,2,32,1024]{3,2,1,0:T(8,128)(2,1)S(1)} collective-permute-done((bf16[1,2,32,1024]{3,2,1,0:T(8,128)(2,1)S(1)}, bf16[1,2,32,1024]{3,2,1,0:T(8,128)(2,1)S(1)}, u32[]{:S(2)}, u32[]{:S(2)}) %collective-permute-start.2) | collective-permute-done | bytes 131104 | tf_op jit(solution)/shard_map/ppermute | solution.py:277
  40.8 6.4 %all-to-all-done = bf16[64,16,384]{2,1,0:T(8,128)(2,1)S(1)} async-done(((bf16[64,16,384]{2,1,0:T(8,128)(2,1)}), bf16[64,16,384]{2,1,0:T(8,128)(2,1)S(1)}, u32[]{:S(2)}, u32[]{:S(2)}) %all-to-all-start) | async-done | bytes 786464 | tf_op jit(solution)/shard_map/all_to_all | solution.py:23
  47.2 1.2 shard_map.128
  48.5 4.2 %all-to-all-start.1 = ((bf16[8,128,256]{2,1,0:T(8,128)(2,1)}), bf16[8,128,256]{2,1,0:T(8,128)(2,1)S(1)}, u32[]{:S(2)}, u32[]{:S(2)}) async-start(bf16[8,128,256]{2,1,0:T(8,128)(2,1)} %get-tuple-element.26), calls=%async_computation.1 | async-start | bytes 1048576 | tf_op jit(solution)/shard_map/all_to_all | solution.py:23
  52.7 3.4 %collective-permute-start.3 = (bf16[2,2,32,1024]{3,2,1,0:T(8,128)(2,1)S(1)}, bf16[2,2,32,1024]{3,2,1,0:T(8,128)(2,1)S(1)}, u32[]{:S(2)}, u32[]{:S(2)}) collective-permute-start(bf16[2,2,32,1024]{3,2,1,0:T(8,128)(2,1)S(1)} %pad_maximum_fusion.1.near), channel_id=1, source_target_pairs={{0,2},{2,0},{4,6},{6,4},{1,3},{3,1},{5,7},{7,5},{8,10},{10,8},{12,... | collective-permute-start | bytes 786440 | tf_op jit(solution)/shard_map/ppermute | solution.py:277
  56.0 3.1 %collective-permute-start.4 = (bf16[1,2,16,1024]{3,2,1,0:T(8,128)(2,1)S(1)}, bf16[1,2,16,1024]{3,2,1,0:T(8,128)(2,1)S(1)}, u32[]{:S(2)}, u32[]{:S(2)}) collective-permute-start(bf16[1,2,16,1024]{3,2,1,0:T(8,128)(2,1)S(1)} %bitcast.50), channel_id=1, source_target_pairs={{0,256},{64,320},{128,384},{192,448},{256,0},{320,64},{384,128},{4... | collective-permute-start | bytes 196616 | tf_op jit(solution)/shard_map/ppermute | solution.py:277
  59.1 6.9 %collective-permute-done.3.away = bf16[2,2,32,1024]{3,2,1,0:T(8,128)(2,1)S(1)} collective-permute-done((bf16[2,2,32,1024]{3,2,1,0:T(8,128)(2,1)S(1)}, bf16[2,2,32,1024]{3,2,1,0:T(8,128)(2,1)S(1)}, u32[]{:S(2)}, u32[]{:S(2)}) %collective-permute-start.3) | collective-permute-done | bytes 262176 | tf_op jit(solution)/shard_map/ppermute | solution.py:277
  66.0 1.1 shard_map.129
  67.1 17.1 %all_to_all.30 = bf16[8,16,1024]{2,1,0:T(8,128)(2,1)S(1)} all-to-all(bf16[8,16,1024]{2,1,0:T(8,128)(2,1)S(1)} %bitcast.41), channel_id=1, replica_groups=mesh['rep'=8,'pair'=4,'odd'=2,'x'=4,'core'=2] {'pair','core'}, dimensions={0} | all-to-all | bytes 524288 | tf_op jit(solution)/shard_map/all_to_all | solution.py:23
  84.3 0.7 copy-done.2
  84.9 0.9 shard_map.130
  85.8 15.0 %all_to_all.31.got = bf16[8,144,128]{2,1,0:T(8,128)(2,1)S(1)} all-to-all(bf16[8,144,128]{2,1,0:T(8,128)(2,1)S(1)} %bitcast.40), channel_id=1, replica_groups=mesh['rep'=8,'pair'=4,'odd'=2,'x'=4,'core'=2] {'pair','core'}, dimensions={0} | all-to-all | bytes 589824 | tf_op jit(solution)/shard_map/all_to_all | solution.py:23
  100.8 1.2 shard_map.131
  102.0 4.4 %all-to-all-start.4 = ((bf16[8,272,128]{2,1,0:T(8,128)(2,1)}), bf16[8,272,128]{2,1,0:T(8,128)(2,1)S(1)}, u32[]{:S(2)}, u32[]{:S(2)}) async-start(bf16[8,272,128]{2,1,0:T(8,128)(2,1)} %shard_map.131), calls=%async_computation.4 | async-start | bytes 1114112 | tf_op jit(solution)/shard_map/all_to_all | solution.py:23
  106.5 2.3 %collective-permute-start.5 = (bf16[2,2,16,1024]{3,2,1,0:T(8,128)(2,1)S(1)}, bf16[2,2,16,1024]{3,2,1,0:T(8,128)(2,1)S(1)}, u32[]{:S(2)}, u32[]{:S(2)}) collective-permute-start(bf16[2,2,16,1024]{3,2,1,0:T(8,128)(2,1)S(1)} %get-tuple-element.36), channel_id=1, source_target_pairs={{0,128},{64,192},{128,0},{192,64},{256,384},{320,448},{384,256},{4... | collective-permute-start | bytes 393224 | tf_op jit(solution)/shard_map/ppermute | solution.py:277
  108.8 5.7 %all-to-all-done.4.got = bf16[8,272,128]{2,1,0:T(8,128)(2,1)S(1)} async-done(((bf16[8,272,128]{2,1,0:T(8,128)(2,1)}), bf16[8,272,128]{2,1,0:T(8,128)(2,1)S(1)}, u32[]{:S(2)}, u32[]{:S(2)}) %all-to-all-start.4) | async-done | bytes 557088 | tf_op jit(solution)/shard_map/all_to_all | solution.py:23
  114.5 1.2 shard_map.132
  115.7 1.1 collective-permute-done.5
  116.8 6.2 %all-to-all-start.5 = ((bf16[64,16,256]{2,1,0:T(8,128)(2,1)}), bf16[64,16,256]{2,1,0:T(8,128)(2,1)S(1)}, u32[]{:S(2)}, u32[]{:S(2)}) async-start(bf16[64,16,256]{2,1,0:T(8,128)(2,1)} %bitcast.14), calls=%async_computation.5 | async-start | bytes 1048576 | tf_op jit(solution)/shard_map/all_to_all | solution.py:23
  123.1 0.1 slice_reduce_fusion.1
  123.2 3.3 %collective-permute-start.6 = (bf16[4,2,16,1024]{3,2,1,0:T(8,128)(2,1)S(1)}, bf16[4,2,16,1024]{3,2,1,0:T(8,128)(2,1)S(1)}, u32[]{:S(2)}, u32[]{:S(2)}) collective-permute-start(bf16[4,2,16,1024]{3,2,1,0:T(8,128)(2,1)S(1)} %bitcast.43), channel_id=1, source_target_pairs={{0,64},{64,0},{128,192},{192,128},{256,320},{320,256},{384,448},{4... | collective-permute-start | bytes 786440 | tf_op jit(solution)/shard_map/ppermute | solution.py:277
  126.6 0.5 copy-done.7
  127.1 0.7 multiply_divide_fusion
  127.8 14.5 %collective-permute-done.6 = bf16[4,2,16,1024]{3,2,1,0:T(8,128)(2,1)S(1)} collective-permute-done((bf16[4,2,16,1024]{3,2,1,0:T(8,128)(2,1)S(1)}, bf16[4,2,16,1024]{3,2,1,0:T(8,128)(2,1)S(1)}, u32[]{:S(2)}, u32[]{:S(2)}) %collective-permute-start.6) | collective-permute-done | bytes 262176 | tf_op jit(solution)/shard_map/ppermute | solution.py:277
  142.4 1.0 shard_map.133
  (29 shorter events, 0.4 us)
Async XLA Ops:
  2.6 17.8 %copy-start.4 = (bf16[2,16,1024]{2,1,0:T(8,128)(2,1)S(1)}, bf16[2,16,1024]{2,1,0:T(8,128)(2,1)}, u32[]{:S(2)}) copy-start(bf16[2,16,1024]{2,1,0:T(8,128)(2,1)} %param.11) | copy-start | bytes 196612
  2.6 44.6 %all-to-all-start = ((bf16[64,16,384]{2,1,0:T(8,128)(2,1)}), bf16[64,16,384]{2,1,0:T(8,128)(2,1)S(1)}, u32[]{:S(2)}, u32[]{:S(2)}) async-start(bf16[64,16,384]{2,1,0:T(8,128)(2,1)} %bitcast.42), calls=%async_computation | async-start | bytes 1572864 | tf_op jit(solution)/shard_map/all_to_all | solution.py:23
  20.4 3.2 %collective-permute-start = (bf16[16,1024]{1,0:T(8,128)(2,1)S(1)}, bf16[16,1024]{1,0:T(8,128)(2,1)S(1)}, u32[]{:S(2)}, u32[]{:S(2)}) collective-permute-start(bf16[16,1024]{1,0:T(8,128)(2,1)S(1)} %get-tuple-element.49), channel_id=1, source_target_pairs={{0,1},{1,0},{2,3},{3,2},{4,5},{5,4},{6,7},{7,6},{8,9},{9,8},{10,11... | collective-permute-start | bytes 98312 | tf_op jit(solution)/shard_map/ppermute | solution.py:27
  23.7 6.8 %collective-permute-start.1 = (bf16[1,32,1024]{2,1,0:T(8,128)(2,1)S(1)}, bf16[1,32,1024]{2,1,0:T(8,128)(2,1)S(1)}, u32[]{:S(2)}, u32[]{:S(2)}) collective-permute-start(bf16[1,32,1024]{2,1,0:T(8,128)(2,1)S(1)} %bitcast.46), channel_id=1, source_target_pairs={{0,4},{2,6},{4,0},{6,2},{1,5},{3,7},{5,1},{7,3},{8,12},{10,14},{12... | collective-permute-start | bytes 196616 | tf_op jit(solution)/shard_map/ppermute | solution.py:277
  30.5 10.3 %collective-permute-start.2 = (bf16[1,2,32,1024]{3,2,1,0:T(8,128)(2,1)S(1)}, bf16[1,2,32,1024]{3,2,1,0:T(8,128)(2,1)S(1)}, u32[]{:S(2)}, u32[]{:S(2)}) collective-permute-start(bf16[1,2,32,1024]{3,2,1,0:T(8,128)(2,1)S(1)} %maximum_bitcast_fusion), channel_id=1, source_target_pairs={{0,8},{8,0},{1,9},{9,1},{2,10},{10,2},{3,11},{11,3},{4,12},{12,4},... | collective-permute-start | bytes 393224 | tf_op jit(solution)/shard_map/ppermute | solution.py:277
  48.5 7.6 %copy-start.5 = (bf16[2,16,1024]{2,1,0:T(8,128)(2,1)S(1)}, bf16[2,16,1024]{2,1,0:T(8,128)(2,1)}, u32[]{:S(2)}) copy-start(bf16[2,16,1024]{2,1,0:T(8,128)(2,1)} %param.9) | copy-start | bytes 196612
  48.5 17.6 %all-to-all-start.1 = ((bf16[8,128,256]{2,1,0:T(8,128)(2,1)}), bf16[8,128,256]{2,1,0:T(8,128)(2,1)S(1)}, u32[]{:S(2)}, u32[]{:S(2)}) async-start(bf16[8,128,256]{2,1,0:T(8,128)(2,1)} %get-tuple-element.26), calls=%async_computation.1 | async-start | bytes 1048576 | tf_op jit(solution)/shard_map/all_to_all | solution.py:23
  52.7 13.4 %collective-permute-start.3 = (bf16[2,2,32,1024]{3,2,1,0:T(8,128)(2,1)S(1)}, bf16[2,2,32,1024]{3,2,1,0:T(8,128)(2,1)S(1)}, u32[]{:S(2)}, u32[]{:S(2)}) collective-permute-start(bf16[2,2,32,1024]{3,2,1,0:T(8,128)(2,1)S(1)} %pad_maximum_fusion.1.near), channel_id=1, source_target_pairs={{0,2},{2,0},{4,6},{6,4},{1,3},{3,1},{5,7},{7,5},{8,10},{10,8},{12,... | collective-permute-start | bytes 786440 | tf_op jit(solution)/shard_map/ppermute | solution.py:277
  56.0 11.1 %collective-permute-start.4 = (bf16[1,2,16,1024]{3,2,1,0:T(8,128)(2,1)S(1)}, bf16[1,2,16,1024]{3,2,1,0:T(8,128)(2,1)S(1)}, u32[]{:S(2)}, u32[]{:S(2)}) collective-permute-start(bf16[1,2,16,1024]{3,2,1,0:T(8,128)(2,1)S(1)} %bitcast.50), channel_id=1, source_target_pairs={{0,256},{64,320},{128,384},{192,448},{256,0},{320,64},{384,128},{4... | collective-permute-start | bytes 196616 | tf_op jit(solution)/shard_map/ppermute | solution.py:277
  67.1 17.2 %copy-start = (f32[2,16,1024]{2,1,0:T(8,128)S(1)}, f32[2,16,1024]{2,1,0:T(8,128)}, u32[]{:S(2)}) copy-start(f32[2,16,1024]{2,1,0:T(8,128)} %moment.1) | copy-start | bytes 393220
  67.1 17.2 %copy-start.1 = (s32[2,16,1024]{2,1,0:T(8,128)S(1)}, s32[2,16,1024]{2,1,0:T(8,128)}, u32[]{:S(2)}) copy-start(s32[2,16,1024]{2,1,0:T(8,128)} %codes.1) | copy-start | bytes 393220
  67.1 17.1 %copy-start.3 = (f32[2,8]{1,0:T(2,128)S(1)}, f32[2,8]{1,0:T(2,128)}, u32[]{:S(2)}) copy-start(f32[2,8]{1,0:T(2,128)} %span.1) | copy-start | bytes 196
  84.3 0.7 copy-start.2
  102.0 12.5 %all-to-all-start.4 = ((bf16[8,272,128]{2,1,0:T(8,128)(2,1)}), bf16[8,272,128]{2,1,0:T(8,128)(2,1)S(1)}, u32[]{:S(2)}, u32[]{:S(2)}) async-start(bf16[8,272,128]{2,1,0:T(8,128)(2,1)} %shard_map.131), calls=%async_computation.4 | async-start | bytes 1114112 | tf_op jit(solution)/shard_map/all_to_all | solution.py:23
  106.5 10.3 %collective-permute-start.5 = (bf16[2,2,16,1024]{3,2,1,0:T(8,128)(2,1)S(1)}, bf16[2,2,16,1024]{3,2,1,0:T(8,128)(2,1)S(1)}, u32[]{:S(2)}, u32[]{:S(2)}) collective-permute-start(bf16[2,2,16,1024]{3,2,1,0:T(8,128)(2,1)S(1)} %get-tuple-element.36), channel_id=1, source_target_pairs={{0,128},{64,192},{128,0},{192,64},{256,384},{320,448},{384,256},{4... | collective-permute-start | bytes 393224 | tf_op jit(solution)/shard_map/ppermute | solution.py:277
  116.8 25.6 %all-to-all-start.5 = ((bf16[64,16,256]{2,1,0:T(8,128)(2,1)}), bf16[64,16,256]{2,1,0:T(8,128)(2,1)S(1)}, u32[]{:S(2)}, u32[]{:S(2)}) async-start(bf16[64,16,256]{2,1,0:T(8,128)(2,1)} %bitcast.14), calls=%async_computation.5 | async-start | bytes 1048576 | tf_op jit(solution)/shard_map/all_to_all | solution.py:23
  123.2 3.3 %copy-start.6 = (f32[2,8]{1,0:T(2,128)}, f32[2,8]{1,0:T(2,128)S(1)}, u32[]{:S(2)}) copy-start(f32[2,8]{1,0:T(2,128)S(1)} %get-tuple-element.44) | copy-start | bytes 196
  123.2 19.1 %collective-permute-start.6 = (bf16[4,2,16,1024]{3,2,1,0:T(8,128)(2,1)S(1)}, bf16[4,2,16,1024]{3,2,1,0:T(8,128)(2,1)S(1)}, u32[]{:S(2)}, u32[]{:S(2)}) collective-permute-start(bf16[4,2,16,1024]{3,2,1,0:T(8,128)(2,1)S(1)} %bitcast.43), channel_id=1, source_target_pairs={{0,64},{64,0},{128,192},{192,128},{256,320},{320,256},{384,448},{4... | collective-permute-start | bytes 786440 | tf_op jit(solution)/shard_map/ppermute | solution.py:277
  126.5 0.6 copy-start.7

commit v6 on v5

--- a/solution.py
+++ b/solution.py
@@ -6,9 +6,9 @@
 from jax.sharding import Mesh, PartitionSpec as P
 
 F = ("pair", "odd", "x", "core")
-A = ("odd", "x")
-ZB = ("rep", "pair", "core")
-B = ("pair", "core")
+A = ("x", "core")
+ZB = ("rep", "pair", "odd")
+B = ("pair", "odd")
 BF16, F32 = jnp.bfloat16, jnp.float32
 VMEM = pl.BlockSpec(memory_space=pltpu.VMEM)
 ANY = pl.BlockSpec(memory_space=pl.ANY)
@@ -69,9 +69,9 @@
     )
     part = part.astype(BF16)
     for to in range(8):
-        for pair in range(4):
-            start = pair * 256 + to * 32
-            out[to, pair * 32 : pair * 32 + 32] = part[start : start + 32]
+        for y in range(8):
+            start = y * 128 + to * 16
+            out[to, y * 16 : y * 16 + 16] = part[start : start + 16]
 
 
 def left_part(grads):
@@ -85,14 +85,16 @@
     )(grads)
 
 
-def right_kernel(got, near, away, out, right_out, held, right, sems):
-    odd, x = lax.axis_index("odd"), lax.axis_index("x")
+def right_kernel(got, near, away, other, out, right_out, held, right, sems):
+    at, odd = lax.axis_index("x") * 2 + lax.axis_index("core"), lax.axis_index("odd")
     ring, places = [], []
     for bits in range(8):
-        block = (near, away)[bits % 2]
-        ring.append(block.at[bits // 4, bits // 2 % 2])
-        to = jnp.bitwise_xor(odd, bits // 4) * 4 + jnp.bitwise_xor(x, bits % 4)
-        places.append(right.at[to])
+        block = (near, away)[bits // 2 % 2]
+        to = jnp.bitwise_xor(at, bits)
+        ring.append(block.at[bits // 4, bits % 2, odd])
+        places.append(right.at[odd, to])
+        ring.append(other.at[bits // 2 % 2, bits // 4, bits % 2])
+        places.append(right.at[1 - odd, to])
     wait = pull([got] + ring, [held] + places, sems)
     wait()
     total = held[0].astype(F32)
@@ -103,19 +105,19 @@
     right_out[...] = basis
 
 
-def right_part(got, near, away):
+def right_part(got, near, away, other):
     return pl.pallas_call(
         right_kernel,
         out_shape=(shape(128, 1024), shape(256, 1024)),
-        in_specs=[ANY] * 3,
+        in_specs=[ANY] * 4,
         out_specs=(VMEM, VMEM),
         scratch_shapes=[
             pltpu.VMEM((8, 128, 256), BF16),
-            pltpu.VMEM((8, 32, 1024), BF16),
-            pltpu.SemaphoreType.DMA((9,)),
+            pltpu.VMEM((2, 8, 16, 1024), BF16),
+            pltpu.SemaphoreType.DMA((17,)),
         ],
         compiler_params=PARAMS,
-    )(got, near, away)
+    )(got, near, away, other)
 
 
 def ends_tile(layers):
@@ -216,10 +218,10 @@
     wait = pull([got], [held], sems)
     wait()
     for half in range(2):
-        for pair in range(4):
-            start = half * 128 + pair * 32
-            rows = held[:, start : start + 32, :].reshape(256, 128)
-            back[pair * 256 : pair * 256 + 256, half * 128 : half * 128 + 128] = rows
+        for y in range(8):
+            start = half * 128 + y * 16
+            rows = held[:, start : start + 16, :].reshape(128, 128)
+            back[y * 128 : y * 128 + 128, half * 128 : half * 128 + 128] = rows
     moved = jnp.dot(left[...], back[...], preferred_element_type=F32).astype(BF16).reshape(8, 16, 256)
     for copy in range(8):
         out[copy] = moved
@@ -270,21 +272,17 @@
 
 
 def on_device(grads, params, left_basis, right_basis, moment, codes, level_low, level_span):
-    core = lax.axis_index("core")
-    pick = lambda values, at: lax.dynamic_index_in_dim(values, at, 0, keepdims=False)
-    both = lambda here, there: jnp.where(core == 0, jnp.stack([here, there]), jnp.stack([there, here]))
-    swap = lambda values: shift(values, "core", 2, 1)
+    odd = lax.axis_index("odd")
     flip = lambda values, axis, size, bit: lax.ppermute(values, axis, [(i, i ^ bit) for i in range(size)])
     tie = lax.optimization_barrier
 
-    right = both(pick(right_basis, core), swap(pick(right_basis, 1 - core))).reshape(1, 32, 1024)
-    right = jnp.concatenate([right, flip(right, "x", 4, 2)])[None]
-    near = jnp.concatenate([right, flip(right, "odd", 2, 1)])
+    near = jnp.stack([right_basis, flip(right_basis, "core", 2, 1)])
+    near = jnp.stack([near, flip(near, "x", 4, 2)])
     away = flip(near, "x", 4, 1)
 
     sent = panels(grads[0], left_basis)
     got = exchange(sent.reshape(64, 16, 384), ZB)
-    got, near = tie((got, near))
+    got, away = tie((got, away))
     part, left_rows = left_part(got.reshape(8, 128, 384))
 
     def joined(olds, other, bit):
@@ -292,8 +290,11 @@
 
     olds = params[None]
 
+    layer = lambda values: lax.dynamic_index_in_dim(values, 1 - odd, 2, keepdims=False)
+    other = flip(jnp.stack([layer(near), layer(away)]), "odd", 2, 1)
+
     got = exchange(part, A)
-    turned, right_rows = right_part(got, near, away)
+    turned, right_rows = right_part(got, near, away, other)
     turned, other = tie((turned, flip(tie((olds, part))[0], "rep", 8, 4)))
     olds = joined(olds, other, 4)
     got = exchange(turned.reshape(8, 16, 1024), B).reshape(4, 2, 16, 1024)

time: 145 us -> 140 us (0.966)
  starting transfers between devices: 54 us -> 67.6 us
  waiting for transfers between devices: 45.5 us -> 34.8 us
  blocking collectives: 32.1 us -> 25 us
    all_to_all x4, starting transfers between devices: 32.6 us -> 41.2 us  [exchange(): return lax.all_to_all(blocks, axes, split_axis=0, concat_axis=0, tiled=True)]
    ppermute x6 -> x7, starting transfers between devices: 19 us -> 26.4 us  [on_device(): lax.ppermute(values, axis, [(i, i ^ bit) for i in range(size)])]
    all_to_all x2, blocking collectives: 32.1 us -> 25 us  [exchange(): return lax.all_to_all(blocks, axes, split_axis=0, concat_axis=0, tiled=True)]
    all_to_all x4, waiting for transfers between devices: 12.1 us -> 6.11 us  [exchange(): return lax.all_to_all(blocks, axes, split_axis=0, concat_axis=0, tiled=True)]
    ppermute x6 -> x7, waiting for transfers between devices: 32.5 us -> 28.7 us  [on_device(): lax.ppermute(values, axis, [(i, i ^ bit) for i in range(size)])]
    ppermute x1 -> x0, starting transfers between devices: 2.36 us -> none  [shift(): lax.ppermute(block, axis, [(i, (i + by) % size) for i in range(size)])]
  transfers between devices with their start and end apart: 11 -> 11, of which waited for: 8 -> 9; matrix products, arithmetic and copies ran while one was open for 1% -> 1% of each run, Pallas kernels for 2% -> 2%
where the time goes in v6:
time: 140 us; the launch traced here: 139 us
  starting transfers between devices  67.6 us (48%)
  waiting for transfers between devices  34.8 us (25%)
  blocking collectives  25 us (18%)
  Pallas kernels  8.72 us (6%)
  local copies, waits for them, and re-layouts  1.47 us (1%)
    all_to_all x4, starting transfers between devices, exchange(): return lax.all_to_all(blocks, axes, split_axis=0, concat_axis=0, tiled=True)  41.2 us
    ppermute x7, waiting for transfers between devices, on_device(): lax.ppermute(values, axis, [(i, i ^ bit) for i in range(size)])  28.7 us
    ppermute x7, starting transfers between devices, on_device(): lax.ppermute(values, axis, [(i, i ^ bit) for i in range(size)])  26.4 us
    all_to_all x2, blocking collectives, exchange(): return lax.all_to_all(blocks, axes, split_axis=0, concat_axis=0, tiled=True)  25 us
    all_to_all x4, waiting for transfers between devices, exchange(): return lax.all_to_all(blocks, axes, split_axis=0, concat_axis=0, tiled=True)  6.11 us
  transfers between devices with their start and end apart: 11, of which 9 were waited for; matrix products, arithmetic and copies ran while one was open for 1% of the time, Pallas kernels for 2%

profile of v6, /device:TPU:1, one launch (start us, length us, event | category | flops | bytes accessed | tf_op | source)
XLA Modules:
  0.0 139.3 jit_solution(5563920947460494258)
XLA Ops:
  0.6 2.0 %shard_map.127 = bf16[32,2,16,384]{3,2,1,0:T(8,128)(2,1)} custom-call(bf16[2,16,8192]{2,1,0:T(8,128)(2,1)} %bitcast.48, bf16[2,16,1024]{2,1,0:T(8,128)(2,1)} %left.1), custom_call_target="tpu_custom_call" | custom-call | tf_op jit(solution)/shard_map/pallas_call | solution.py:54
  2.6 17.3 %all-to-all-start = ((bf16[64,16,384]{2,1,0:T(8,128)(2,1)}), bf16[64,16,384]{2,1,0:T(8,128)(2,1)S(1)}, u32[]{:S(2)}, u32[]{:S(2)}) async-start(bf16[64,16,384]{2,1,0:T(8,128)(2,1)} %bitcast.45), calls=%async_computation | async-start | bytes 1572864 | tf_op jit(solution)/shard_map/all_to_all | solution.py:23
  19.9 2.9 %collective-permute-start = (bf16[2,16,1024]{2,1,0:T(8,128)(2,1)S(1)}, bf16[2,16,1024]{2,1,0:T(8,128)(2,1)S(1)}, u32[]{:S(2)}, u32[]{:S(2)}) collective-permute-start(bf16[2,16,1024]{2,1,0:T(8,128)(2,1)S(1)} %copy-done.4), channel_id=1, source_target_pairs={{0,1},{1,0},{2,3},{3,2},{4,5},{5,4},{6,7},{7,6},{8,9},{9,8},{10,11... | collective-permute-start | bytes 196616 | tf_op jit(solution)/shard_map/ppermute | solution.py:276
  22.8 0.9 collective-permute-done
  23.7 4.7 %collective-permute-start.1 = (bf16[2,2,16,1024]{3,2,1,0:T(8,128)(2,1)S(1)}, bf16[2,2,16,1024]{3,2,1,0:T(8,128)(2,1)S(1)}, u32[]{:S(2)}, u32[]{:S(2)}) collective-permute-start(bf16[2,2,16,1024]{3,2,1,0:T(8,128)(2,1)S(1)} %get-tuple-element.49), channel_id=1, source_target_pairs={{0,4},{2,6},{4,0},{6,2},{1,5},{3,7},{5,1},{7,3},{8,12},{10,14},{12... | collective-permute-start | bytes 393224 | tf_op jit(solution)/shard_map/ppermute | solution.py:276
  28.4 3.5 %collective-permute-done.1 = bf16[2,2,16,1024]{3,2,1,0:T(8,128)(2,1)S(1)} collective-permute-done((bf16[2,2,16,1024]{3,2,1,0:T(8,128)(2,1)S(1)}, bf16[2,2,16,1024]{3,2,1,0:T(8,128)(2,1)S(1)}, u32[]{:S(2)}, u32[]{:S(2)}) %collective-permute-start.1) | collective-permute-done | bytes 131104 | tf_op jit(solution)/shard_map/ppermute | solution.py:276
  31.9 3.1 %collective-permute-start.2 = (bf16[2,2,2,16,1024]{4,3,2,1,0:T(8,128)(2,1)S(1)}, bf16[2,2,2,16,1024]{4,3,2,1,0:T(8,128)(2,1)S(1)}, u32[]{:S(2)}, u32[]{:S(2)}) collective-permute-start(bf16[2,2,2,16,1024]{4,3,2,1,0:T(8,128)(2,1)S(1)} %pad_maximum_fusion.1.near), channel_id=1, source_target_pairs={{0,2},{2,0},{4,6},{6,4},{1,3},{3,1},{5,7},{7,5},{8,10},{10,8},{12,... | collective-permute-start | bytes 786440 | tf_op jit(solution)/shard_map/ppermute | solution.py:276
  35.0 5.3 %collective-permute-done.2.away = bf16[2,2,2,16,1024]{4,3,2,1,0:T(8,128)(2,1)S(1)} collective-permute-done((bf16[2,2,2,16,1024]{4,3,2,1,0:T(8,128)(2,1)S(1)}, bf16[2,2,2,16,1024]{4,3,2,1,0:T(8,128)(2,1)S(1)}, u32[]{:S(2)}, u32[]{:S(2)}) %collective-permute-start.2) | collective-permute-done | bytes 262176 | tf_op jit(solution)/shard_map/ppermute | solution.py:276
  40.4 1.4 %all-to-all-done = bf16[64,16,384]{2,1,0:T(8,128)(2,1)S(1)} async-done(((bf16[64,16,384]{2,1,0:T(8,128)(2,1)}), bf16[64,16,384]{2,1,0:T(8,128)(2,1)S(1)}, u32[]{:S(2)}, u32[]{:S(2)}) %all-to-all-start) | async-done | bytes 786464 | tf_op jit(solution)/shard_map/all_to_all | solution.py:23
  41.8 1.2 shard_map.128
  43.0 7.6 %all-to-all-start.1 = ((bf16[8,128,256]{2,1,0:T(8,128)(2,1)}), bf16[8,128,256]{2,1,0:T(8,128)(2,1)S(1)}, u32[]{:S(2)}, u32[]{:S(2)}) async-start(bf16[8,128,256]{2,1,0:T(8,128)(2,1)} %get-tuple-element.26), calls=%async_computation.1 | async-start | bytes 1048576 | tf_op jit(solution)/shard_map/all_to_all | solution.py:23
  50.7 3.0 %collective-permute-start.3 = (bf16[2,2,2,16,1024]{4,3,2,1,0:T(8,128)(2,1)S(1)}, bf16[2,2,2,16,1024]{4,3,2,1,0:T(8,128)(2,1)S(1)}, u32[]{:S(2)}, u32[]{:S(2)}) collective-permute-start(bf16[2,2,2,16,1024]{4,3,2,1,0:T(8,128)(2,1)S(1)} %pad_maximum_fusion.2), channel_id=1, source_target_pairs={{0,8},{8,0},{1,9},{9,1},{2,10},{10,2},{3,11},{11,3},{4,12},{12,4},... | collective-permute-start | bytes 786440 | tf_op jit(solution)/shard_map/ppermute | solution.py:276
  53.7 4.7 %collective-permute-start.4 = (bf16[1,2,16,1024]{3,2,1,0:T(8,128)(2,1)S(1)}, bf16[1,2,16,1024]{3,2,1,0:T(8,128)(2,1)S(1)}, u32[]{:S(2)}, u32[]{:S(2)}) collective-permute-start(bf16[1,2,16,1024]{3,2,1,0:T(8,128)(2,1)S(1)} %bitcast.54), channel_id=1, source_target_pairs={{0,256},{64,320},{128,384},{192,448},{256,0},{320,64},{384,128},{4... | collective-permute-start | bytes 196616 | tf_op jit(solution)/shard_map/ppermute | solution.py:276
  58.4 2.1 %collective-permute-done.3.other = bf16[2,2,2,16,1024]{4,3,2,1,0:T(8,128)(2,1)S(1)} collective-permute-done((bf16[2,2,2,16,1024]{4,3,2,1,0:T(8,128)(2,1)S(1)}, bf16[2,2,2,16,1024]{4,3,2,1,0:T(8,128)(2,1)S(1)}, u32[]{:S(2)}, u32[]{:S(2)}) %collective-permute-start.3) | collective-permute-done | bytes 262176 | tf_op jit(solution)/shard_map/ppermute | solution.py:276
  60.5 1.2 shard_map.129
  61.7 0.9 collective-permute-done.4
  62.6 12.9 %all_to_all.30 = bf16[8,16,1024]{2,1,0:T(8,128)(2,1)S(1)} all-to-all(bf16[8,16,1024]{2,1,0:T(8,128)(2,1)S(1)} %bitcast.44), channel_id=1, replica_groups=mesh['rep'=8,'pair'=4,'odd'=2,'x'=4,'core'=2] {'pair','odd'}, dimensions={0} | all-to-all | bytes 524288 | tf_op jit(solution)/shard_map/all_to_all | solution.py:23
  75.5 0.7 copy-done.2
  76.2 0.9 shard_map.130
  77.1 12.1 %all_to_all.31.got = bf16[8,144,128]{2,1,0:T(8,128)(2,1)S(1)} all-to-all(bf16[8,144,128]{2,1,0:T(8,128)(2,1)S(1)} %bitcast.43), channel_id=1, replica_groups=mesh['rep'=8,'pair'=4,'odd'=2,'x'=4,'core'=2] {'pair','odd'}, dimensions={0} | all-to-all | bytes 589824 | tf_op jit(solution)/shard_map/all_to_all | solution.py:23
  89.1 1.2 shard_map.131
  90.3 9.7 %all-to-all-start.4 = ((bf16[8,272,128]{2,1,0:T(8,128)(2,1)}), bf16[8,272,128]{2,1,0:T(8,128)(2,1)S(1)}, u32[]{:S(2)}, u32[]{:S(2)}) async-start(bf16[8,272,128]{2,1,0:T(8,128)(2,1)} %shard_map.131), calls=%async_computation.4 | async-start | bytes 1114112 | tf_op jit(solution)/shard_map/all_to_all | solution.py:23
  100.0 5.1 %collective-permute-start.5 = (bf16[2,2,16,1024]{3,2,1,0:T(8,128)(2,1)S(1)}, bf16[2,2,16,1024]{3,2,1,0:T(8,128)(2,1)S(1)}, u32[]{:S(2)}, u32[]{:S(2)}) collective-permute-start(bf16[2,2,16,1024]{3,2,1,0:T(8,128)(2,1)S(1)} %get-tuple-element.36), channel_id=1, source_target_pairs={{0,128},{64,192},{128,0},{192,64},{256,384},{320,448},{384,256},{4... | collective-permute-start | bytes 393224 | tf_op jit(solution)/shard_map/ppermute | solution.py:276
  105.1 4.7 %all-to-all-done.4.got = bf16[8,272,128]{2,1,0:T(8,128)(2,1)S(1)} async-done(((bf16[8,272,128]{2,1,0:T(8,128)(2,1)}), bf16[8,272,128]{2,1,0:T(8,128)(2,1)S(1)}, u32[]{:S(2)}, u32[]{:S(2)}) %all-to-all-start.4) | async-done | bytes 557088 | tf_op jit(solution)/shard_map/all_to_all | solution.py:23
  109.8 1.2 shard_map.132
  111.0 0.8 collective-permute-done.5
  111.8 6.7 %all-to-all-start.5 = ((bf16[64,16,256]{2,1,0:T(8,128)(2,1)}), bf16[64,16,256]{2,1,0:T(8,128)(2,1)S(1)}, u32[]{:S(2)}, u32[]{:S(2)}) async-start(bf16[64,16,256]{2,1,0:T(8,128)(2,1)} %bitcast.16), calls=%async_computation.5 | async-start | bytes 1048576 | tf_op jit(solution)/shard_map/all_to_all | solution.py:23
  118.6 2.9 %collective-permute-start.6 = (bf16[4,2,16,1024]{3,2,1,0:T(8,128)(2,1)S(1)}, bf16[4,2,16,1024]{3,2,1,0:T(8,128)(2,1)S(1)}, u32[]{:S(2)}, u32[]{:S(2)}) collective-permute-start(bf16[4,2,16,1024]{3,2,1,0:T(8,128)(2,1)S(1)} %bitcast.46), channel_id=1, source_target_pairs={{0,64},{64,0},{128,192},{192,128},{256,320},{320,256},{384,448},{4... | collective-permute-start | bytes 786440 | tf_op jit(solution)/shard_map/ppermute | solution.py:276
  121.6 0.5 copy-done.7
  122.2 0.7 multiply_divide_fusion
  122.9 15.2 %collective-permute-done.6 = bf16[4,2,16,1024]{3,2,1,0:T(8,128)(2,1)S(1)} collective-permute-done((bf16[4,2,16,1024]{3,2,1,0:T(8,128)(2,1)S(1)}, bf16[4,2,16,1024]{3,2,1,0:T(8,128)(2,1)S(1)}, u32[]{:S(2)}, u32[]{:S(2)}) %collective-permute-start.6) | collective-permute-done | bytes 262176 | tf_op jit(solution)/shard_map/ppermute | solution.py:276
  138.2 1.0 shard_map.133
  (30 shorter events, 0.5 us)
Async XLA Ops:
  2.6 17.3 %copy-start.4 = (bf16[2,16,1024]{2,1,0:T(8,128)(2,1)S(1)}, bf16[2,16,1024]{2,1,0:T(8,128)(2,1)}, u32[]{:S(2)}) copy-start(bf16[2,16,1024]{2,1,0:T(8,128)(2,1)} %param.11) | copy-start | bytes 196612
  2.6 39.1 %all-to-all-start = ((bf16[64,16,384]{2,1,0:T(8,128)(2,1)}), bf16[64,16,384]{2,1,0:T(8,128)(2,1)S(1)}, u32[]{:S(2)}, u32[]{:S(2)}) async-start(bf16[64,16,384]{2,1,0:T(8,128)(2,1)} %bitcast.45), calls=%async_computation | async-start | bytes 1572864 | tf_op jit(solution)/shard_map/all_to_all | solution.py:23
  19.9 3.8 %collective-permute-start = (bf16[2,16,1024]{2,1,0:T(8,128)(2,1)S(1)}, bf16[2,16,1024]{2,1,0:T(8,128)(2,1)S(1)}, u32[]{:S(2)}, u32[]{:S(2)}) collective-permute-start(bf16[2,16,1024]{2,1,0:T(8,128)(2,1)S(1)} %copy-done.4), channel_id=1, source_target_pairs={{0,1},{1,0},{2,3},{3,2},{4,5},{5,4},{6,7},{7,6},{8,9},{9,8},{10,11... | collective-permute-start | bytes 196616 | tf_op jit(solution)/shard_map/ppermute | solution.py:276
  23.7 8.1 %collective-permute-start.1 = (bf16[2,2,16,1024]{3,2,1,0:T(8,128)(2,1)S(1)}, bf16[2,2,16,1024]{3,2,1,0:T(8,128)(2,1)S(1)}, u32[]{:S(2)}, u32[]{:S(2)}) collective-permute-start(bf16[2,2,16,1024]{3,2,1,0:T(8,128)(2,1)S(1)} %get-tuple-element.49), channel_id=1, source_target_pairs={{0,4},{2,6},{4,0},{6,2},{1,5},{3,7},{5,1},{7,3},{8,12},{10,14},{12... | collective-permute-start | bytes 393224 | tf_op jit(solution)/shard_map/ppermute | solution.py:276
  31.9 8.5 %collective-permute-start.2 = (bf16[2,2,2,16,1024]{4,3,2,1,0:T(8,128)(2,1)S(1)}, bf16[2,2,2,16,1024]{4,3,2,1,0:T(8,128)(2,1)S(1)}, u32[]{:S(2)}, u32[]{:S(2)}) collective-permute-start(bf16[2,2,2,16,1024]{4,3,2,1,0:T(8,128)(2,1)S(1)} %pad_maximum_fusion.1.near), channel_id=1, source_target_pairs={{0,2},{2,0},{4,6},{6,4},{1,3},{3,1},{5,7},{7,5},{8,10},{10,8},{12,... | collective-permute-start | bytes 786440 | tf_op jit(solution)/shard_map/ppermute | solution.py:276
  43.0 17.5 %all-to-all-start.1 = ((bf16[8,128,256]{2,1,0:T(8,128)(2,1)}), bf16[8,128,256]{2,1,0:T(8,128)(2,1)S(1)}, u32[]{:S(2)}, u32[]{:S(2)}) async-start(bf16[8,128,256]{2,1,0:T(8,128)(2,1)} %get-tuple-element.26), calls=%async_computation.1 | async-start | bytes 1048576 | tf_op jit(solution)/shard_map/all_to_all | solution.py:23
  50.6 3.0 %copy-start.5 = (bf16[2,16,1024]{2,1,0:T(8,128)(2,1)S(1)}, bf16[2,16,1024]{2,1,0:T(8,128)(2,1)}, u32[]{:S(2)}) copy-start(bf16[2,16,1024]{2,1,0:T(8,128)(2,1)} %param.9) | copy-start | bytes 196612
  50.7 9.8 %collective-permute-start.3 = (bf16[2,2,2,16,1024]{4,3,2,1,0:T(8,128)(2,1)S(1)}, bf16[2,2,2,16,1024]{4,3,2,1,0:T(8,128)(2,1)S(1)}, u32[]{:S(2)}, u32[]{:S(2)}) collective-permute-start(bf16[2,2,2,16,1024]{4,3,2,1,0:T(8,128)(2,1)S(1)} %pad_maximum_fusion.2), channel_id=1, source_target_pairs={{0,8},{8,0},{1,9},{9,1},{2,10},{10,2},{3,11},{11,3},{4,12},{12,4},... | collective-permute-start | bytes 786440 | tf_op jit(solution)/shard_map/ppermute | solution.py:276
  53.7 8.9 %collective-permute-start.4 = (bf16[1,2,16,1024]{3,2,1,0:T(8,128)(2,1)S(1)}, bf16[1,2,16,1024]{3,2,1,0:T(8,128)(2,1)S(1)}, u32[]{:S(2)}, u32[]{:S(2)}) collective-permute-start(bf16[1,2,16,1024]{3,2,1,0:T(8,128)(2,1)S(1)} %bitcast.54), channel_id=1, source_target_pairs={{0,256},{64,320},{128,384},{192,448},{256,0},{320,64},{384,128},{4... | collective-permute-start | bytes 196616 | tf_op jit(solution)/shard_map/ppermute | solution.py:276
  62.6 12.9 %copy-start = (f32[2,16,1024]{2,1,0:T(8,128)S(1)}, f32[2,16,1024]{2,1,0:T(8,128)}, u32[]{:S(2)}) copy-start(f32[2,16,1024]{2,1,0:T(8,128)} %moment.1) | copy-start | bytes 393220
  62.6 12.9 %copy-start.1 = (s32[2,16,1024]{2,1,0:T(8,128)S(1)}, s32[2,16,1024]{2,1,0:T(8,128)}, u32[]{:S(2)}) copy-start(s32[2,16,1024]{2,1,0:T(8,128)} %codes.1) | copy-start | bytes 393220
  62.6 12.9 %copy-start.3 = (f32[2,8]{1,0:T(2,128)S(1)}, f32[2,8]{1,0:T(2,128)}, u32[]{:S(2)}) copy-start(f32[2,8]{1,0:T(2,128)} %span.1) | copy-start | bytes 196
  75.5 0.7 copy-start.2
  90.3 19.5 %all-to-all-start.4 = ((bf16[8,272,128]{2,1,0:T(8,128)(2,1)}), bf16[8,272,128]{2,1,0:T(8,128)(2,1)S(1)}, u32[]{:S(2)}, u32[]{:S(2)}) async-start(bf16[8,272,128]{2,1,0:T(8,128)(2,1)} %shard_map.131), calls=%async_computation.4 | async-start | bytes 1114112 | tf_op jit(solution)/shard_map/all_to_all | solution.py:23
  100.0 11.8 %collective-permute-start.5 = (bf16[2,2,16,1024]{3,2,1,0:T(8,128)(2,1)S(1)}, bf16[2,2,16,1024]{3,2,1,0:T(8,128)(2,1)S(1)}, u32[]{:S(2)}, u32[]{:S(2)}) collective-permute-start(bf16[2,2,16,1024]{3,2,1,0:T(8,128)(2,1)S(1)} %get-tuple-element.36), channel_id=1, source_target_pairs={{0,128},{64,192},{128,0},{192,64},{256,384},{320,448},{384,256},{4... | collective-permute-start | bytes 393224 | tf_op jit(solution)/shard_map/ppermute | solution.py:276
  111.8 26.4 %all-to-all-start.5 = ((bf16[64,16,256]{2,1,0:T(8,128)(2,1)}), bf16[64,16,256]{2,1,0:T(8,128)(2,1)S(1)}, u32[]{:S(2)}, u32[]{:S(2)}) async-start(bf16[64,16,256]{2,1,0:T(8,128)(2,1)} %bitcast.16), calls=%async_computation.5 | async-start | bytes 1048576 | tf_op jit(solution)/shard_map/all_to_all | solution.py:23
  118.6 2.9 %copy-start.6 = (f32[2,8]{1,0:T(2,128)}, f32[2,8]{1,0:T(2,128)S(1)}, u32[]{:S(2)}) copy-start(f32[2,8]{1,0:T(2,128)S(1)} %get-tuple-element.44) | copy-start | bytes 196
  118.6 19.5 %collective-permute-start.6 = (bf16[4,2,16,1024]{3,2,1,0:T(8,128)(2,1)S(1)}, bf16[4,2,16,1024]{3,2,1,0:T(8,128)(2,1)S(1)}, u32[]{:S(2)}, u32[]{:S(2)}) collective-permute-start(bf16[4,2,16,1024]{3,2,1,0:T(8,128)(2,1)S(1)} %bitcast.46), channel_id=1, source_target_pairs={{0,64},{64,0},{128,192},{192,128},{256,320},{320,256},{384,448},{4... | collective-permute-start | bytes 786440 | tf_op jit(solution)/shard_map/ppermute | solution.py:276
  121.6 0.6 copy-start.7

commit v7 on v6

--- a/solution.py
+++ b/solution.py
@@ -56,8 +56,13 @@
     )(grads, left)
 
 
-def left_kernel(grads, out, left, held, sems):
+def left_kernel(grads, low, span, out, left, levels, held, sems):
     wait = pull([grads], [held], sems)
+    for which, values in enumerate((low, span)):
+        for layer in range(2):
+            for group in range(8):
+                value = values[layer : layer + 1, group : group + 1]
+                levels[which, layer, group : group + 1, :] = jnp.broadcast_to(value, (1, 128))
     wait()
     total = held[0, :, 0:256].astype(F32)
     for replica in range(1, 8):
@@ -74,15 +79,15 @@
             out[to, y * 16 : y * 16 + 16] = part[start : start + 16]
 
 
-def left_part(grads):
+def left_part(grads, low, span):
     return pl.pallas_call(
         left_kernel,
-        out_shape=(shape(8, 128, 256), shape(128, 1024)),
-        in_specs=[ANY],
-        out_specs=(VMEM, VMEM),
+        out_shape=(shape(8, 128, 256), shape(128, 1024), shape(2, 2, 8, 128, of=F32)),
+        in_specs=[ANY, VMEM, VMEM],
+        out_specs=(VMEM,) * 3,
         scratch_shapes=[pltpu.VMEM((8, 128, 384), BF16), pltpu.SemaphoreType.DMA((1,))],
         compiler_params=PARAMS,
-    )(grads)
+    )(grads, low, span)
 
 
 def right_kernel(got, near, away, other, out, right_out, held, right, sems):
@@ -142,7 +147,7 @@
     return layers
 
 
-def moments_kernel(got, moment, codes, low, span, out, moment_new, second_new, held, sems):
+def moments_kernel(got, moment, codes, levels, params, out, moment_new, second_new, held, sems):
     wait = pull([got], [held], sems)
     wait()
     ends = []
@@ -155,8 +160,8 @@
                 turn += held[part, layer, :, lanes].astype(F32)
             mean = 0.9 * moment[layer, :, lanes] + 0.1 * turn
             code = codes[layer, :, lanes].astype(F32)
-            at = (slice(layer, layer + 1), slice(group, group + 1))
-            second = low[at] + code / 15.0 * span[at]
+            low = levels[0, layer, group : group + 1]
+            second = low + code / 15.0 * levels[1, layer, group : group + 1]
             second = 0.95 * second + 0.05 * turn * turn
             moment_new[layer, :, lanes] = mean
             second_new[layer, :, lanes] = second
@@ -172,13 +177,16 @@
     for copy in range(4):
         for to in range(2):
             out[copy, to, 128:144] = tile
-
-
-def moments(got, moment, codes, low, span):
+            for half in range(2):
+                start = copy * 256 + half * 128
+                out[copy, to, 144 + half * 16 : 160 + half * 16] = params[to, :, start : start + 128]
+
+
+def moments(got, moment, codes, levels, params):
     return pl.pallas_call(
         moments_kernel,
         out_shape=(
-            shape(4, 2, 144, 128),
+            shape(4, 2, 176, 128),
             shape(2, 16, 1024, of=F32),
             shape(2, 16, 1024, of=F32),
         ),
@@ -186,16 +194,19 @@
         out_specs=(VMEM, VMEM, VMEM),
         scratch_shapes=[pltpu.VMEM((4, 2, 16, 1024), BF16), pltpu.SemaphoreType.DMA((1,))],
         compiler_params=PARAMS,
-    )(got, moment, codes, low, span)
-
-
-def back_kernel(got, right, out, held, sems):
+    )(got, moment, codes, levels, params)
+
+
+def back_kernel(got, right, out, params, held, sems):
     wait = pull([got], [held], sems)
     wait()
     rows = [held[:, at * 16 : at * 16 + 16, :].reshape(128, 128) for at in range(8)]
     returned = lax.dot_general(
         jnp.concatenate(rows, axis=1), right[...], (((1,), (1,)), ((), ())), preferred_element_type=F32
     ).astype(BF16)
+    for half in range(2):
+        rows = held[:, 144 + half * 16 : 160 + half * 16, :].reshape(128, 128)
+        params[:, half * 128 : half * 128 + 128] = rows
     tile = ends_tile([jnp.concatenate(ends, axis=0) for ends in ends_of(held[:, 128:144, :])])
     for copy in range(8):
         out[copy, 0:128] = returned[:, 0:128]
@@ -206,15 +217,15 @@
 def back_part(got, right):
     return pl.pallas_call(
         back_kernel,
-        out_shape=shape(8, 272, 128),
+        out_shape=(shape(8, 272, 128), shape(128, 256)),
         in_specs=[ANY, VMEM],
-        out_specs=VMEM,
-        scratch_shapes=[pltpu.VMEM((8, 144, 128), BF16), pltpu.SemaphoreType.DMA((1,))],
+        out_specs=(VMEM, VMEM),
+        scratch_shapes=[pltpu.VMEM((8, 176, 128), BF16), pltpu.SemaphoreType.DMA((1,))],
         compiler_params=PARAMS,
     )(got, right)
 
 
-def update_kernel(got, left, out, ends, held, back, sems):
+def update_kernel(got, left, params, out, ends, held, back, sems):
     wait = pull([got], [held], sems)
     wait()
     for half in range(2):
@@ -222,19 +233,22 @@
             start = half * 128 + y * 16
             rows = held[:, start : start + 16, :].reshape(128, 128)
             back[y * 128 : y * 128 + 128, half * 128 : half * 128 + 128] = rows
-    moved = jnp.dot(left[...], back[...], preferred_element_type=F32).astype(BF16).reshape(8, 16, 256)
+    moved = jnp.dot(left[...], back[...], preferred_element_type=F32)
+    new = params[...].astype(F32) * (1.0 - 0.05 * 0.1) - 0.05 * moved
+    new = new.astype(BF16).reshape(8, 16, 256)
     for copy in range(8):
-        out[copy] = moved
+        out[copy] = new
+    out[lax.axis_index("rep")] = moved.astype(BF16).reshape(8, 16, 256)
     for layer, (low, high) in enumerate(ends_of(held[:, 256:272, :])):
         ends[0, layer] = jnp.broadcast_to(low, (8, 128))
         ends[1, layer] = jnp.broadcast_to(high, (8, 128))
 
 
-def update_part(got, left):
+def update_part(got, left, params):
     return pl.pallas_call(
         update_kernel,
         out_shape=(shape(8, 8, 16, 256), shape(2, 2, 8, 128, of=F32)),
-        in_specs=[ANY, VMEM],
+        in_specs=[ANY, VMEM, VMEM],
         out_specs=(VMEM, VMEM),
         scratch_shapes=[
             pltpu.VMEM((8, 272, 128), BF16),
@@ -242,33 +256,53 @@
             pltpu.SemaphoreType.DMA((1,)),
         ],
         compiler_params=PARAMS,
-    )(got, left)
-
-
-def step_kernel(got, olds, params_new, update, held, sems):
+    )(got, left, params)
+
+
+def step_kernel(got, params, second, ends, params_new, update, levels, low_new, span_new, held, sems):
     rep = lax.axis_index("rep")
     wait = pull([got], [held], sems)
     wait()
     for panel in range(4):
+        for block in range(8):
+            start = block * 1024 + panel * 256
+            params_new[:, :, start : start + 256] = held[block, panel]
+    for panel in range(4):
         lanes = slice(panel * 256, panel * 256 + 256)
-        update[:, :, lanes] = held[rep, panel].astype(F32)
-        for block in range(8):
-            change = held[block, panel].astype(F32)
-            old = olds[jnp.bitwise_xor(rep, block), :, :, lanes].astype(F32)
-            new = old * (1.0 - 0.05 * 0.1) - 0.05 * change
-            start = block * 1024 + panel * 256
-            params_new[:, :, start : start + 256] = new.astype(BF16)
-
-
-def step(got, olds):
+        change = held[rep, panel].astype(F32)
+        update[:, :, lanes] = change
+        new = params[:, :, lanes].astype(F32) * (1.0 - 0.05 * 0.1) - 0.05 * change
+        own = pl.ds(pl.multiple_of(rep * 1024 + panel * 256, 256), 256)
+        params_new[:, :, own] = new.astype(BF16)
+    row = lax.broadcasted_iota(jnp.int32, (8, 128), 0)
+    lane = lax.broadcasted_iota(jnp.int32, (8, 128), 1)
+    for layer in range(2):
+        low = ends[0, layer]
+        span = ends[1, layer] - low
+        for out, values in ((low_new, low), (span_new, span)):
+            spread = jnp.sum(jnp.where(row == lane, values, 0.0), axis=0, keepdims=True)
+            out[layer : layer + 1, :] = spread[:, 0:8]
+        for group in range(8):
+            lanes = slice(group * 128, group * 128 + 128)
+            above = second[layer, :, lanes] - low[group : group + 1]
+            levels[layer, :, lanes] = 15.0 * above / span[group : group + 1]
+
+
+def step(got, params, second, ends):
     return pl.pallas_call(
         step_kernel,
-        out_shape=(shape(2, 16, 8192), shape(2, 16, 1024, of=F32)),
-        in_specs=[ANY, VMEM],
-        out_specs=(VMEM, VMEM),
+        out_shape=(
+            shape(2, 16, 8192),
+            shape(2, 16, 1024, of=F32),
+            shape(2, 16, 1024, of=F32),
+            shape(2, 8, of=F32),
+            shape(2, 8, of=F32),
+        ),
+        in_specs=[ANY, VMEM, VMEM, VMEM],
+        out_specs=(VMEM,) * 5,
         scratch_shapes=[pltpu.VMEM((8, 4, 2, 16, 256), BF16), pltpu.SemaphoreType.DMA((1,))],
         compiler_params=PARAMS,
-    )(got, olds)
+    )(got, params, second, ends)
 
 
 def on_device(grads, params, left_basis, right_basis, moment, codes, level_low, level_span):
@@ -283,37 +317,22 @@
     sent = panels(grads[0], left_basis)
     got = exchange(sent.reshape(64, 16, 384), ZB)
     got, away = tie((got, away))
-    part, left_rows = left_part(got.reshape(8, 128, 384))
-
-    def joined(olds, other, bit):
-        return jnp.stack([olds, other], 1).reshape(8 // bit, 2, 16, 1024)
-
-    olds = params[None]
+    part, left_rows, spread = left_part(got.reshape(8, 128, 384), level_low, level_span)
 
     layer = lambda values: lax.dynamic_index_in_dim(values, 1 - odd, 2, keepdims=False)
     other = flip(jnp.stack([layer(near), layer(away)]), "odd", 2, 1)
 
     got = exchange(part, A)
     turned, right_rows = right_part(got, near, away, other)
-    turned, other = tie((turned, flip(tie((olds, part))[0], "rep", 8, 4)))
-    olds = joined(olds, other, 4)
     got = exchange(turned.reshape(8, 16, 1024), B).reshape(4, 2, 16, 1024)
-    block, moment_new, second_new = moments(got, moment, codes, level_low, level_span)
-    got = exchange(block.reshape(8, 144, 128), B)
-    block = back_part(got, right_rows)
+    block, moment_new, second_new = moments(got, moment, codes, spread, params)
+    got = exchange(block.reshape(8, 176, 128), B)
+    block, old = back_part(got, right_rows)
     got = exchange(block, A)
-    moved, ends = update_part(got, left_rows)
-    moved, other = tie((moved, flip(tie((olds, block))[0], "rep", 8, 2)))
-    olds = joined(olds, other, 2)
-    olds = joined(olds, flip(olds, "rep", 8, 1), 1)
+    moved, ends = update_part(got, left_rows, old)
     got = exchange(moved.reshape(64, 16, 256), ZB).reshape(8, 4, 2, 16, 256)
 
-    low_new = ends[0, :, :, 0]
-    span_new = ends[1, :, :, 0] - low_new
-    grouped = second_new.reshape(2, 16, 8, 128)
-    levels = 15.0 * (grouped - low_new[:, None, :, None]) / span_new[:, None, :, None]
-    levels = levels.reshape(2, 16, 1024)
-    params_new, update = step(got, olds)
+    params_new, update, levels, low_new, span_new = step(got, params, second_new, ends)
     return (params_new, moment_new, update, levels, low_new, span_new)
 
 

time: 140 us -> 137 us (0.979); the launches traced: 139 us -> 135 us
  blocking collectives: 25 us -> 70.1 us
  starting transfers between devices: 67.6 us -> 38.5 us
  waiting for transfers between devices: 34.8 us -> 17.9 us
  local copies, waits for them, and re-layouts: 1.47 us -> 0.04 us
    all_to_all x2 -> x4, blocking collectives: 25 us -> 70.1 us  [exchange(): return lax.all_to_all(blocks, axes, split_axis=0, concat_axis=0, tiled=True)]
    all_to_all x4 -> x2, starting transfers between devices: 41.2 us -> 24.9 us  [exchange(): return lax.all_to_all(blocks, axes, split_axis=0, concat_axis=0, tiled=True)]
    ppermute x7 -> x4, starting transfers between devices: 26.4 us -> 13.6 us  [on_device(): lax.ppermute(values, axis, [(i, i ^ bit) for i in range(size)])]
    ppermute x7 -> x4, waiting for transfers between devices: 28.7 us -> 16.5 us  [on_device(): lax.ppermute(values, axis, [(i, i ^ bit) for i in range(size)])]
    all_to_all x4 -> x2, waiting for transfers between devices: 6.11 us -> 1.41 us  [exchange(): return lax.all_to_all(blocks, axes, split_axis=0, concat_axis=0, tiled=True)]
  transfers between devices with their start and end apart: 11 -> 6, of which waited for: 9 -> 5; matrix products, arithmetic and copies ran while one was open for 1% -> 0% of each run, Pallas kernels for 2% -> 0%
where the time goes in v7:
time: 137 us; the launch traced here: 135 us
  blocking collectives  70.1 us (51%)
  starting transfers between devices  38.5 us (28%)
  waiting for transfers between devices  17.9 us (13%)
  Pallas kernels  7.36 us (5%)
    all_to_all x4, blocking collectives, exchange(): return lax.all_to_all(blocks, axes, split_axis=0, concat_axis=0, tiled=True)  70.1 us
    all_to_all x2, starting transfers between devices, exchange(): return lax.all_to_all(blocks, axes, split_axis=0, concat_axis=0, tiled=True)  24.9 us
    ppermute x4, waiting for transfers between devices, on_device(): lax.ppermute(values, axis, [(i, i ^ bit) for i in range(size)])  16.5 us
    ppermute x4, starting transfers between devices, on_device(): lax.ppermute(values, axis, [(i, i ^ bit) for i in range(size)])  13.6 us
  transfers between devices with their start and end apart: 6, of which 5 were waited for; matrix products, arithmetic and copies ran while one was open for 0% of the time, Pallas kernels for 0%

profile of v7, /device:TPU:1, one launch (start us, length us, event | category | flops | bytes accessed | tf_op | source)
XLA Modules:
  0.0 134.8 jit_solution(12633824065887192716)
XLA Ops:
  0.6 2.0 %shard_map.127 = bf16[32,2,16,384]{3,2,1,0:T(8,128)(2,1)} custom-call(bf16[2,16,8192]{2,1,0:T(8,128)(2,1)} %bitcast.24, bf16[2,16,1024]{2,1,0:T(8,128)(2,1)} %left.1), custom_call_target="tpu_custom_call" | custom-call | tf_op jit(solution)/shard_map/pallas_call | solution.py:54
  2.6 17.3 %all-to-all-start = ((bf16[64,16,384]{2,1,0:T(8,128)(2,1)}), bf16[64,16,384]{2,1,0:T(8,128)(2,1)S(1)}, u32[]{:S(2)}, u32[]{:S(2)}) async-start(bf16[64,16,384]{2,1,0:T(8,128)(2,1)} %bitcast.23), calls=%async_computation | async-start | bytes 1572864 | tf_op jit(solution)/shard_map/all_to_all | solution.py:23
  19.9 0.0 copy-done.5
  19.9 2.9 %collective-permute-start = (bf16[2,16,1024]{2,1,0:T(8,128)(2,1)S(1)}, bf16[2,16,1024]{2,1,0:T(8,128)(2,1)S(1)}, u32[]{:S(2)}, u32[]{:S(2)}) collective-permute-start(bf16[2,16,1024]{2,1,0:T(8,128)(2,1)S(1)} %copy-done.5), channel_id=1, source_target_pairs={{0,1},{1,0},{2,3},{3,2},{4,5},{5,4},{6,7},{7,6},{8,9},{9,8},{10,11... | collective-permute-start | bytes 196616 | tf_op jit(solution)/shard_map/ppermute | solution.py:310
  22.8 0.9 collective-permute-done
  23.7 4.7 %collective-permute-start.1 = (bf16[2,2,16,1024]{3,2,1,0:T(8,128)(2,1)S(1)}, bf16[2,2,16,1024]{3,2,1,0:T(8,128)(2,1)S(1)}, u32[]{:S(2)}, u32[]{:S(2)}) collective-permute-start(bf16[2,2,16,1024]{3,2,1,0:T(8,128)(2,1)S(1)} %get-tuple-element.45), channel_id=1, source_target_pairs={{0,4},{2,6},{4,0},{6,2},{1,5},{3,7},{5,1},{7,3},{8,12},{10,14},{12... | collective-permute-start | bytes 393224 | tf_op jit(solution)/shard_map/ppermute | solution.py:310
  28.4 3.5 %collective-permute-done.1 = bf16[2,2,16,1024]{3,2,1,0:T(8,128)(2,1)S(1)} collective-permute-done((bf16[2,2,16,1024]{3,2,1,0:T(8,128)(2,1)S(1)}, bf16[2,2,16,1024]{3,2,1,0:T(8,128)(2,1)S(1)}, u32[]{:S(2)}, u32[]{:S(2)}) %collective-permute-start.1) | collective-permute-done | bytes 131104 | tf_op jit(solution)/shard_map/ppermute | solution.py:310
  31.8 3.1 %collective-permute-start.2 = (bf16[2,2,2,16,1024]{4,3,2,1,0:T(8,128)(2,1)S(1)}, bf16[2,2,2,16,1024]{4,3,2,1,0:T(8,128)(2,1)S(1)}, u32[]{:S(2)}, u32[]{:S(2)}) collective-permute-start(bf16[2,2,2,16,1024]{4,3,2,1,0:T(8,128)(2,1)S(1)} %pad_maximum_fusion.near), channel_id=1, source_target_pairs={{0,2},{2,0},{4,6},{6,4},{1,3},{3,1},{5,7},{7,5},{8,10},{10,8},{12,... | collective-permute-start | bytes 786440 | tf_op jit(solution)/shard_map/ppermute | solution.py:310
  35.0 0.0 copy-start.4
  35.0 0.0 copy-start.3
  35.0 5.3 %collective-permute-done.2.away = bf16[2,2,2,16,1024]{4,3,2,1,0:T(8,128)(2,1)S(1)} collective-permute-done((bf16[2,2,2,16,1024]{4,3,2,1,0:T(8,128)(2,1)S(1)}, bf16[2,2,2,16,1024]{4,3,2,1,0:T(8,128)(2,1)S(1)}, u32[]{:S(2)}, u32[]{:S(2)}) %collective-permute-start.2) | collective-permute-done | bytes 262176 | tf_op jit(solution)/shard_map/ppermute | solution.py:310
  40.4 1.4 %all-to-all-done = bf16[64,16,384]{2,1,0:T(8,128)(2,1)S(1)} async-done(((bf16[64,16,384]{2,1,0:T(8,128)(2,1)}), bf16[64,16,384]{2,1,0:T(8,128)(2,1)S(1)}, u32[]{:S(2)}, u32[]{:S(2)}) %all-to-all-start) | async-done | bytes 786464 | tf_op jit(solution)/shard_map/all_to_all | solution.py:23
  41.8 0.0 copy-done.4
  41.8 0.0 copy-done.3
  41.8 1.3 shard_map.128
  43.1 7.6 %all-to-all-start.1 = ((bf16[8,128,256]{2,1,0:T(8,128)(2,1)}), bf16[8,128,256]{2,1,0:T(8,128)(2,1)S(1)}, u32[]{:S(2)}, u32[]{:S(2)}) async-start(bf16[8,128,256]{2,1,0:T(8,128)(2,1)} %get-tuple-element.26), calls=%async_computation.1 | async-start | bytes 1048576 | tf_op jit(solution)/shard_map/all_to_all | solution.py:23
  50.8 3.0 %collective-permute-start.3 = (bf16[2,2,2,16,1024]{4,3,2,1,0:T(8,128)(2,1)S(1)}, bf16[2,2,2,16,1024]{4,3,2,1,0:T(8,128)(2,1)S(1)}, u32[]{:S(2)}, u32[]{:S(2)}) collective-permute-start(bf16[2,2,2,16,1024]{4,3,2,1,0:T(8,128)(2,1)S(1)} %pad_maximum_fusion.1), channel_id=1, source_target_pairs={{0,8},{8,0},{1,9},{9,1},{2,10},{10,2},{3,11},{11,3},{4,12},{12,4},... | collective-permute-start | bytes 786440 | tf_op jit(solution)/shard_map/ppermute | solution.py:310
  53.8 6.8 %collective-permute-done.3.other = bf16[2,2,2,16,1024]{4,3,2,1,0:T(8,128)(2,1)S(1)} collective-permute-done((bf16[2,2,2,16,1024]{4,3,2,1,0:T(8,128)(2,1)S(1)}, bf16[2,2,2,16,1024]{4,3,2,1,0:T(8,128)(2,1)S(1)}, u32[]{:S(2)}, u32[]{:S(2)}) %collective-permute-start.3) | collective-permute-done | bytes 262176 | tf_op jit(solution)/shard_map/ppermute | solution.py:310
  60.6 0.0 all-to-all-done.1.got
  60.6 1.2 shard_map.129
  61.8 0.0 copy-start
  61.8 0.0 copy-start.1
  61.8 0.0 copy-start.2
  61.8 14.4 %all_to_all.30 = bf16[8,16,1024]{2,1,0:T(8,128)(2,1)S(1)} all-to-all(bf16[8,16,1024]{2,1,0:T(8,128)(2,1)S(1)} %bitcast.22), channel_id=1, replica_groups=mesh['rep'=8,'pair'=4,'odd'=2,'x'=4,'core'=2] {'pair','odd'}, dimensions={0} | all-to-all | bytes 524288 | tf_op jit(solution)/shard_map/all_to_all | solution.py:23
  76.3 0.0 copy-done.2
  76.3 0.9 shard_map.130
  77.2 13.8 %all_to_all.31.got = bf16[8,176,128]{2,1,0:T(8,128)(2,1)S(1)} all-to-all(bf16[8,176,128]{2,1,0:T(8,128)(2,1)S(1)} %bitcast.21), channel_id=1, replica_groups=mesh['rep'=8,'pair'=4,'odd'=2,'x'=4,'core'=2] {'pair','odd'}, dimensions={0} | all-to-all | bytes 720896 | tf_op jit(solution)/shard_map/all_to_all | solution.py:23
  91.0 0.5 shard_map.131
  91.5 17.6 %all_to_all.32.got = bf16[8,272,128]{2,1,0:T(8,128)(2,1)S(1)} all-to-all(bf16[8,272,128]{2,1,0:T(8,128)(2,1)S(1)} %get-tuple-element.32), channel_id=1, replica_groups=mesh['rep'=8,'pair'=4,'odd'=2,'x'=4,'core'=2] {'x','core'}, dimensions={0} | all-to-all | bytes 1114112 | tf_op jit(solution)/shard_map/all_to_all | solution.py:23
  109.1 0.4 shard_map.132
  109.5 24.3 %all_to_all.33 = bf16[64,16,256]{2,1,0:T(8,128)(2,1)S(1)} all-to-all(bf16[64,16,256]{2,1,0:T(8,128)(2,1)S(1)} %bitcast.20), channel_id=1, replica_groups=mesh['rep'=8,'pair'=4,'odd'=2,'x'=4,'core'=2] {'rep','pair','odd'}, dimensions={0} | all-to-all | bytes 1048576 | tf_op jit(solution)/shard_map/all_to_all | solution.py:23
  133.8 1.0 shard_map.133
  (8 shorter events, 0.1 us)
Async XLA Ops:
  2.6 17.3 %copy-start.5 = (bf16[2,16,1024]{2,1,0:T(8,128)(2,1)S(1)}, bf16[2,16,1024]{2,1,0:T(8,128)(2,1)}, u32[]{:S(2)}) copy-start(bf16[2,16,1024]{2,1,0:T(8,128)(2,1)} %param.11) | copy-start | bytes 196612
  2.6 39.1 %all-to-all-start = ((bf16[64,16,384]{2,1,0:T(8,128)(2,1)}), bf16[64,16,384]{2,1,0:T(8,128)(2,1)S(1)}, u32[]{:S(2)}, u32[]{:S(2)}) async-start(bf16[64,16,384]{2,1,0:T(8,128)(2,1)} %bitcast.23), calls=%async_computation | async-start | bytes 1572864 | tf_op jit(solution)/shard_map/all_to_all | solution.py:23
  19.9 3.8 %collective-permute-start = (bf16[2,16,1024]{2,1,0:T(8,128)(2,1)S(1)}, bf16[2,16,1024]{2,1,0:T(8,128)(2,1)S(1)}, u32[]{:S(2)}, u32[]{:S(2)}) collective-permute-start(bf16[2,16,1024]{2,1,0:T(8,128)(2,1)S(1)} %copy-done.5), channel_id=1, source_target_pairs={{0,1},{1,0},{2,3},{3,2},{4,5},{5,4},{6,7},{7,6},{8,9},{9,8},{10,11... | collective-permute-start | bytes 196616 | tf_op jit(solution)/shard_map/ppermute | solution.py:310
  23.7 8.1 %collective-permute-start.1 = (bf16[2,2,16,1024]{3,2,1,0:T(8,128)(2,1)S(1)}, bf16[2,2,16,1024]{3,2,1,0:T(8,128)(2,1)S(1)}, u32[]{:S(2)}, u32[]{:S(2)}) collective-permute-start(bf16[2,2,16,1024]{3,2,1,0:T(8,128)(2,1)S(1)} %get-tuple-element.45), channel_id=1, source_target_pairs={{0,4},{2,6},{4,0},{6,2},{1,5},{3,7},{5,1},{7,3},{8,12},{10,14},{12... | collective-permute-start | bytes 393224 | tf_op jit(solution)/shard_map/ppermute | solution.py:310
  31.8 8.5 %collective-permute-start.2 = (bf16[2,2,2,16,1024]{4,3,2,1,0:T(8,128)(2,1)S(1)}, bf16[2,2,2,16,1024]{4,3,2,1,0:T(8,128)(2,1)S(1)}, u32[]{:S(2)}, u32[]{:S(2)}) collective-permute-start(bf16[2,2,2,16,1024]{4,3,2,1,0:T(8,128)(2,1)S(1)} %pad_maximum_fusion.near), channel_id=1, source_target_pairs={{0,2},{2,0},{4,6},{6,4},{1,3},{3,1},{5,7},{7,5},{8,10},{10,8},{12,... | collective-permute-start | bytes 786440 | tf_op jit(solution)/shard_map/ppermute | solution.py:310
  35.0 6.8 %copy-start.4 = (f32[2,8]{1,0:T(2,128)S(1)}, f32[2,8]{1,0:T(2,128)}, u32[]{:S(2)}) copy-start(f32[2,8]{1,0:T(2,128)} %span.1) | copy-start | bytes 196
  35.0 6.7 %copy-start.3 = (f32[2,8]{1,0:T(2,128)S(1)}, f32[2,8]{1,0:T(2,128)}, u32[]{:S(2)}) copy-start(f32[2,8]{1,0:T(2,128)} %low.1) | copy-start | bytes 196
  43.1 17.5 %all-to-all-start.1 = ((bf16[8,128,256]{2,1,0:T(8,128)(2,1)}), bf16[8,128,256]{2,1,0:T(8,128)(2,1)S(1)}, u32[]{:S(2)}, u32[]{:S(2)}) async-start(bf16[8,128,256]{2,1,0:T(8,128)(2,1)} %get-tuple-element.26), calls=%async_computation.1 | async-start | bytes 1048576 | tf_op jit(solution)/shard_map/all_to_all | solution.py:23
  50.8 9.8 %collective-permute-start.3 = (bf16[2,2,2,16,1024]{4,3,2,1,0:T(8,128)(2,1)S(1)}, bf16[2,2,2,16,1024]{4,3,2,1,0:T(8,128)(2,1)S(1)}, u32[]{:S(2)}, u32[]{:S(2)}) collective-permute-start(bf16[2,2,2,16,1024]{4,3,2,1,0:T(8,128)(2,1)S(1)} %pad_maximum_fusion.1), channel_id=1, source_target_pairs={{0,8},{8,0},{1,9},{9,1},{2,10},{10,2},{3,11},{11,3},{4,12},{12,4},... | collective-permute-start | bytes 786440 | tf_op jit(solution)/shard_map/ppermute | solution.py:310
  61.8 14.5 %copy-start = (bf16[2,16,1024]{2,1,0:T(8,128)(2,1)S(1)}, bf16[2,16,1024]{2,1,0:T(8,128)(2,1)}, u32[]{:S(2)}) copy-start(bf16[2,16,1024]{2,1,0:T(8,128)(2,1)} %params.3) | copy-start | bytes 196612
  61.8 14.5 %copy-start.1 = (f32[2,16,1024]{2,1,0:T(8,128)S(1)}, f32[2,16,1024]{2,1,0:T(8,128)}, u32[]{:S(2)}) copy-start(f32[2,16,1024]{2,1,0:T(8,128)} %moment.1) | copy-start | bytes 393220
  61.8 14.4 %copy-start.2 = (s32[2,16,1024]{2,1,0:T(8,128)S(1)}, s32[2,16,1024]{2,1,0:T(8,128)}, u32[]{:S(2)}) copy-start(s32[2,16,1024]{2,1,0:T(8,128)} %codes.1) | copy-start | bytes 393220

commit v8 on v7

--- a/solution.py
+++ b/solution.py
@@ -90,15 +90,15 @@
     )(grads, low, span)
 
 
-def right_kernel(got, near, away, other, out, right_out, held, right, sems):
+def right_kernel(got, own, one, two, three, other, out, right_out, held, right, sems):
     at, odd = lax.axis_index("x") * 2 + lax.axis_index("core"), lax.axis_index("odd")
     ring, places = [], []
     for bits in range(8):
-        block = (near, away)[bits // 2 % 2]
+        block = (own, one, two, three)[bits // 2]
         to = jnp.bitwise_xor(at, bits)
-        ring.append(block.at[bits // 4, bits % 2, odd])
+        ring.append(block.at[bits % 2, odd])
         places.append(right.at[odd, to])
-        ring.append(other.at[bits // 2 % 2, bits // 4, bits % 2])
+        ring.append(other.at[bits // 2, bits % 2])
         places.append(right.at[1 - odd, to])
     wait = pull([got] + ring, [held] + places, sems)
     wait()
@@ -110,11 +110,11 @@
     right_out[...] = basis
 
 
-def right_part(got, near, away, other):
+def right_part(got, rights, other):
     return pl.pallas_call(
         right_kernel,
         out_shape=(shape(128, 1024), shape(256, 1024)),
-        in_specs=[ANY] * 4,
+        in_specs=[ANY] * 6,
         out_specs=(VMEM, VMEM),
         scratch_shapes=[
             pltpu.VMEM((8, 128, 256), BF16),
@@ -122,7 +122,7 @@
             pltpu.SemaphoreType.DMA((17,)),
         ],
         compiler_params=PARAMS,
-    )(got, near, away, other)
+    )(got, *rights, other)
 
 
 def ends_tile(layers):
@@ -311,19 +311,18 @@
     tie = lax.optimization_barrier
 
     near = jnp.stack([right_basis, flip(right_basis, "core", 2, 1)])
-    near = jnp.stack([near, flip(near, "x", 4, 2)])
-    away = flip(near, "x", 4, 1)
+    rights = [near] + [flip(near, "x", 4, bits) for bits in (1, 2, 3)]
 
     sent = panels(grads[0], left_basis)
     got = exchange(sent.reshape(64, 16, 384), ZB)
-    got, away = tie((got, away))
+    got, rights = tie((got, rights))
     part, left_rows, spread = left_part(got.reshape(8, 128, 384), level_low, level_span)
 
-    layer = lambda values: lax.dynamic_index_in_dim(values, 1 - odd, 2, keepdims=False)
-    other = flip(jnp.stack([layer(near), layer(away)]), "odd", 2, 1)
+    layer = lambda values: lax.dynamic_index_in_dim(values, 1 - odd, 1, keepdims=False)
+    other = flip(jnp.stack([layer(values) for values in rights]), "odd", 2, 1)
 
     got = exchange(part, A)
-    turned, right_rows = right_part(got, near, away, other)
+    turned, right_rows = right_part(got, rights, other)
     got = exchange(turned.reshape(8, 16, 1024), B).reshape(4, 2, 16, 1024)
     block, moment_new, second_new = moments(got, moment, codes, spread, params)
     got = exchange(block.reshape(8, 176, 128), B)

time: 137 us -> 134 us (0.978)
  blocking collectives: 70.1 us -> 67.4 us
    ppermute x4 -> x5, waiting for transfers between devices: 16.5 us -> 11.5 us  [on_device(): lax.ppermute(values, axis, [(i, i ^ bit) for i in range(size)])]
    all_to_all x2, waiting for transfers between devices: 1.41 us -> 5.24 us  [exchange(): return lax.all_to_all(blocks, axes, split_axis=0, concat_axis=0, tiled=True)]
    all_to_all x4, blocking collectives: 70.1 us -> 67.4 us  [exchange(): return lax.all_to_all(blocks, axes, split_axis=0, concat_axis=0, tiled=True)]
    ppermute x4 -> x5, starting transfers between devices: 13.6 us -> 14.8 us  [on_device(): lax.ppermute(values, axis, [(i, i ^ bit) for i in range(size)])]
  transfers between devices with their start and end apart: 6 -> 7, of which waited for: 5 -> 5; matrix products, arithmetic and copies ran while one was open for 0% -> 0% of each run, Pallas kernels for 0% -> 0%
where the time goes in v8:
time: 134 us; the launch traced here: 132 us
  blocking collectives  67.4 us (50%)
  starting transfers between devices  39.7 us (30%)
  waiting for transfers between devices  16.8 us (13%)
  Pallas kernels  7.36 us (5%)
    all_to_all x4, blocking collectives, exchange(): return lax.all_to_all(blocks, axes, split_axis=0, concat_axis=0, tiled=True)  67.4 us
    all_to_all x2, starting transfers between devices, exchange(): return lax.all_to_all(blocks, axes, split_axis=0, concat_axis=0, tiled=True)  24.9 us
    ppermute x5, starting transfers between devices, on_device(): lax.ppermute(values, axis, [(i, i ^ bit) for i in range(size)])  14.8 us
    ppermute x5, waiting for transfers between devices, on_device(): lax.ppermute(values, axis, [(i, i ^ bit) for i in range(size)])  11.5 us
    all_to_all x2, waiting for transfers between devices, exchange(): return lax.all_to_all(blocks, axes, split_axis=0, concat_axis=0, tiled=True)  5.24 us
  transfers between devices with their start and end apart: 7, of which 5 were waited for; matrix products, arithmetic and copies ran while one was open for 0% of the time, Pallas kernels for 0%

profile of v8, /device:TPU:1, one launch (start us, length us, event | category | flops | bytes accessed | tf_op | source)
XLA Modules:
  0.0 132.2 jit_solution(3200323022073464853)
XLA Ops:
  0.6 2.0 %shard_map.127 = bf16[32,2,16,384]{3,2,1,0:T(8,128)(2,1)} custom-call(bf16[2,16,8192]{2,1,0:T(8,128)(2,1)} %bitcast.25, bf16[2,16,1024]{2,1,0:T(8,128)(2,1)} %left.1), custom_call_target="tpu_custom_call" | custom-call | tf_op jit(solution)/shard_map/pallas_call | solution.py:54
  2.6 17.3 %all-to-all-start = ((bf16[64,16,384]{2,1,0:T(8,128)(2,1)}), bf16[64,16,384]{2,1,0:T(8,128)(2,1)S(1)}, u32[]{:S(2)}, u32[]{:S(2)}) async-start(bf16[64,16,384]{2,1,0:T(8,128)(2,1)} %bitcast.24), calls=%async_computation | async-start | bytes 1572864 | tf_op jit(solution)/shard_map/all_to_all | solution.py:23
  19.9 0.0 copy-done.5
  19.9 2.9 %collective-permute-start = (bf16[2,16,1024]{2,1,0:T(8,128)(2,1)S(1)}, bf16[2,16,1024]{2,1,0:T(8,128)(2,1)S(1)}, u32[]{:S(2)}, u32[]{:S(2)}) collective-permute-start(bf16[2,16,1024]{2,1,0:T(8,128)(2,1)S(1)} %copy-done.5), channel_id=1, source_target_pairs={{0,1},{1,0},{2,3},{3,2},{4,5},{5,4},{6,7},{7,6},{8,9},{9,8},{10,11... | collective-permute-start | bytes 196616 | tf_op jit(solution)/shard_map/ppermute | solution.py:310
  22.8 0.9 collective-permute-done
  23.7 4.4 %collective-permute-start.3 = (bf16[2,2,16,1024]{3,2,1,0:T(8,128)(2,1)S(1)}, bf16[2,2,16,1024]{3,2,1,0:T(8,128)(2,1)S(1)}, u32[]{:S(2)}, u32[]{:S(2)}) collective-permute-start(bf16[2,2,16,1024]{3,2,1,0:T(8,128)(2,1)S(1)} %pad_maximum_fusion.1.own), channel_id=1, source_target_pairs={{0,6},{2,4},{4,2},{6,0},{1,7},{3,5},{5,3},{7,1},{8,14},{10,12},{12... | collective-permute-start | bytes 393224 | tf_op jit(solution)/shard_map/ppermute | solution.py:310
  28.1 2.4 %collective-permute-start.2 = (bf16[2,2,16,1024]{3,2,1,0:T(8,128)(2,1)S(1)}, bf16[2,2,16,1024]{3,2,1,0:T(8,128)(2,1)S(1)}, u32[]{:S(2)}, u32[]{:S(2)}) collective-permute-start(bf16[2,2,16,1024]{3,2,1,0:T(8,128)(2,1)S(1)} %pad_maximum_fusion.1.own), channel_id=1, source_target_pairs={{0,4},{2,6},{4,0},{6,2},{1,5},{3,7},{5,1},{7,3},{8,12},{10,14},{12... | collective-permute-start | bytes 393224 | tf_op jit(solution)/shard_map/ppermute | solution.py:310
  30.5 2.2 %collective-permute-start.1 = (bf16[2,2,16,1024]{3,2,1,0:T(8,128)(2,1)S(1)}, bf16[2,2,16,1024]{3,2,1,0:T(8,128)(2,1)S(1)}, u32[]{:S(2)}, u32[]{:S(2)}) collective-permute-start(bf16[2,2,16,1024]{3,2,1,0:T(8,128)(2,1)S(1)} %pad_maximum_fusion.1.own), channel_id=1, source_target_pairs={{0,2},{2,0},{4,6},{6,4},{1,3},{3,1},{5,7},{7,5},{8,10},{10,8},{12,... | collective-permute-start | bytes 393224 | tf_op jit(solution)/shard_map/ppermute | solution.py:310
  32.7 0.0 copy-start.4
  32.7 0.0 copy-start.3
  32.7 0.0 collective-permute-done.3.three
  32.7 3.2 %collective-permute-done.2.two = bf16[2,2,16,1024]{3,2,1,0:T(8,128)(2,1)S(1)} collective-permute-done((bf16[2,2,16,1024]{3,2,1,0:T(8,128)(2,1)S(1)}, bf16[2,2,16,1024]{3,2,1,0:T(8,128)(2,1)S(1)}, u32[]{:S(2)}, u32[]{:S(2)}) %collective-permute-start.2) | collective-permute-done | bytes 131104 | tf_op jit(solution)/shard_map/ppermute | solution.py:310
  35.9 0.6 collective-permute-done.1.one
  36.5 5.2 %all-to-all-done = bf16[64,16,384]{2,1,0:T(8,128)(2,1)S(1)} async-done(((bf16[64,16,384]{2,1,0:T(8,128)(2,1)}), bf16[64,16,384]{2,1,0:T(8,128)(2,1)S(1)}, u32[]{:S(2)}, u32[]{:S(2)}) %all-to-all-start) | async-done | bytes 786464 | tf_op jit(solution)/shard_map/all_to_all | solution.py:23
  41.8 0.0 copy-done.4
  41.8 1.3 %shard_map.128 = (bf16[8,128,256]{2,1,0:T(8,128)(2,1)}, bf16[128,1024]{1,0:T(8,128)(2,1)S(1)}, f32[2,2,8,128]{3,2,1,0:T(8,128)S(1)}) custom-call(bf16[8,128,384]{2,1,0:T(8,128)(2,1)S(1)} %bitcast.18, f32[2,8]{1,0:T(2,128)S(1)} %copy-done.3, f32[2,8]{1,0:T(2,128)S(1)} %copy-done.4), custom_call_target="tpu_custom_call" | custom-call | tf_op jit(solution)/shard_map/pallas_call | solution.py:83
  43.1 7.6 %all-to-all-start.1 = ((bf16[8,128,256]{2,1,0:T(8,128)(2,1)}), bf16[8,128,256]{2,1,0:T(8,128)(2,1)S(1)}, u32[]{:S(2)}, u32[]{:S(2)}) async-start(bf16[8,128,256]{2,1,0:T(8,128)(2,1)} %get-tuple-element.29), calls=%async_computation.1 | async-start | bytes 1048576 | tf_op jit(solution)/shard_map/all_to_all | solution.py:23
  50.8 3.0 %collective-permute-start.4 = (bf16[4,2,16,1024]{3,2,1,0:T(8,128)(2,1)S(1)}, bf16[4,2,16,1024]{3,2,1,0:T(8,128)(2,1)S(1)}, u32[]{:S(2)}, u32[]{:S(2)}) collective-permute-start(bf16[4,2,16,1024]{3,2,1,0:T(8,128)(2,1)S(1)} %pad_maximum_fusion), channel_id=1, source_target_pairs={{0,8},{8,0},{1,9},{9,1},{2,10},{10,2},{3,11},{11,3},{4,12},{12,4},... | collective-permute-start | bytes 786440 | tf_op jit(solution)/shard_map/ppermute | solution.py:310
  53.8 6.8 %collective-permute-done.4.other = bf16[4,2,16,1024]{3,2,1,0:T(8,128)(2,1)S(1)} collective-permute-done((bf16[4,2,16,1024]{3,2,1,0:T(8,128)(2,1)S(1)}, bf16[4,2,16,1024]{3,2,1,0:T(8,128)(2,1)S(1)}, u32[]{:S(2)}, u32[]{:S(2)}) %collective-permute-start.4) | collective-permute-done | bytes 262176 | tf_op jit(solution)/shard_map/ppermute | solution.py:310
  60.7 0.0 all-to-all-done.1.got
  60.7 1.2 shard_map.129
  61.8 0.0 copy-start
  61.9 0.0 copy-start.1
  61.9 0.0 copy-start.2
  61.9 14.4 %all_to_all.30 = bf16[8,16,1024]{2,1,0:T(8,128)(2,1)S(1)} all-to-all(bf16[8,16,1024]{2,1,0:T(8,128)(2,1)S(1)} %bitcast.23), channel_id=1, replica_groups=mesh['rep'=8,'pair'=4,'odd'=2,'x'=4,'core'=2] {'pair','odd'}, dimensions={0} | all-to-all | bytes 524288 | tf_op jit(solution)/shard_map/all_to_all | solution.py:23
  76.3 0.9 shard_map.130
  77.3 13.8 %all_to_all.31.got = bf16[8,176,128]{2,1,0:T(8,128)(2,1)S(1)} all-to-all(bf16[8,176,128]{2,1,0:T(8,128)(2,1)S(1)} %bitcast.22), channel_id=1, replica_groups=mesh['rep'=8,'pair'=4,'odd'=2,'x'=4,'core'=2] {'pair','odd'}, dimensions={0} | all-to-all | bytes 720896 | tf_op jit(solution)/shard_map/all_to_all | solution.py:23
  91.1 0.5 shard_map.131
  91.6 17.6 %all_to_all.32.got = bf16[8,272,128]{2,1,0:T(8,128)(2,1)S(1)} all-to-all(bf16[8,272,128]{2,1,0:T(8,128)(2,1)S(1)} %get-tuple-element.38), channel_id=1, replica_groups=mesh['rep'=8,'pair'=4,'odd'=2,'x'=4,'core'=2] {'x','core'}, dimensions={0} | all-to-all | bytes 1114112 | tf_op jit(solution)/shard_map/all_to_all | solution.py:23
  109.2 0.4 shard_map.132
  109.6 21.6 %all_to_all.33 = bf16[64,16,256]{2,1,0:T(8,128)(2,1)S(1)} all-to-all(bf16[64,16,256]{2,1,0:T(8,128)(2,1)S(1)} %bitcast.21), channel_id=1, replica_groups=mesh['rep'=8,'pair'=4,'odd'=2,'x'=4,'core'=2] {'rep','pair','odd'}, dimensions={0} | all-to-all | bytes 1048576 | tf_op jit(solution)/shard_map/all_to_all | solution.py:23
  131.2 1.0 shard_map.133
  (9 shorter events, 0.1 us)
Async XLA Ops:
  2.6 17.3 %copy-start.5 = (bf16[2,16,1024]{2,1,0:T(8,128)(2,1)S(1)}, bf16[2,16,1024]{2,1,0:T(8,128)(2,1)}, u32[]{:S(2)}) copy-start(bf16[2,16,1024]{2,1,0:T(8,128)(2,1)} %param.11) | copy-start | bytes 196612
  2.6 39.1 %all-to-all-start = ((bf16[64,16,384]{2,1,0:T(8,128)(2,1)}), bf16[64,16,384]{2,1,0:T(8,128)(2,1)S(1)}, u32[]{:S(2)}, u32[]{:S(2)}) async-start(bf16[64,16,384]{2,1,0:T(8,128)(2,1)} %bitcast.24), calls=%async_computation | async-start | bytes 1572864 | tf_op jit(solution)/shard_map/all_to_all | solution.py:23
  19.9 3.8 %collective-permute-start = (bf16[2,16,1024]{2,1,0:T(8,128)(2,1)S(1)}, bf16[2,16,1024]{2,1,0:T(8,128)(2,1)S(1)}, u32[]{:S(2)}, u32[]{:S(2)}) collective-permute-start(bf16[2,16,1024]{2,1,0:T(8,128)(2,1)S(1)} %copy-done.5), channel_id=1, source_target_pairs={{0,1},{1,0},{2,3},{3,2},{4,5},{5,4},{6,7},{7,6},{8,9},{9,8},{10,11... | collective-permute-start | bytes 196616 | tf_op jit(solution)/shard_map/ppermute | solution.py:310
  23.7 9.0 %collective-permute-start.3 = (bf16[2,2,16,1024]{3,2,1,0:T(8,128)(2,1)S(1)}, bf16[2,2,16,1024]{3,2,1,0:T(8,128)(2,1)S(1)}, u32[]{:S(2)}, u32[]{:S(2)}) collective-permute-start(bf16[2,2,16,1024]{3,2,1,0:T(8,128)(2,1)S(1)} %pad_maximum_fusion.1.own), channel_id=1, source_target_pairs={{0,6},{2,4},{4,2},{6,0},{1,7},{3,5},{5,3},{7,1},{8,14},{10,12},{12... | collective-permute-start | bytes 393224 | tf_op jit(solution)/shard_map/ppermute | solution.py:310
  28.1 7.8 %collective-permute-start.2 = (bf16[2,2,16,1024]{3,2,1,0:T(8,128)(2,1)S(1)}, bf16[2,2,16,1024]{3,2,1,0:T(8,128)(2,1)S(1)}, u32[]{:S(2)}, u32[]{:S(2)}) collective-permute-start(bf16[2,2,16,1024]{3,2,1,0:T(8,128)(2,1)S(1)} %pad_maximum_fusion.1.own), channel_id=1, source_target_pairs={{0,4},{2,6},{4,0},{6,2},{1,5},{3,7},{5,1},{7,3},{8,12},{10,14},{12... | collective-permute-start | bytes 393224 | tf_op jit(solution)/shard_map/ppermute | solution.py:310
  30.5 6.0 %collective-permute-start.1 = (bf16[2,2,16,1024]{3,2,1,0:T(8,128)(2,1)S(1)}, bf16[2,2,16,1024]{3,2,1,0:T(8,128)(2,1)S(1)}, u32[]{:S(2)}, u32[]{:S(2)}) collective-permute-start(bf16[2,2,16,1024]{3,2,1,0:T(8,128)(2,1)S(1)} %pad_maximum_fusion.1.own), channel_id=1, source_target_pairs={{0,2},{2,0},{4,6},{6,4},{1,3},{3,1},{5,7},{7,5},{8,10},{10,8},{12,... | collective-permute-start | bytes 393224 | tf_op jit(solution)/shard_map/ppermute | solution.py:310
  32.7 9.1 %copy-start.4 = (f32[2,8]{1,0:T(2,128)S(1)}, f32[2,8]{1,0:T(2,128)}, u32[]{:S(2)}) copy-start(f32[2,8]{1,0:T(2,128)} %span.1) | copy-start | bytes 196
  32.7 9.1 %copy-start.3 = (f32[2,8]{1,0:T(2,128)S(1)}, f32[2,8]{1,0:T(2,128)}, u32[]{:S(2)}) copy-start(f32[2,8]{1,0:T(2,128)} %low.1) | copy-start | bytes 196
  43.1 17.5 %all-to-all-start.1 = ((bf16[8,128,256]{2,1,0:T(8,128)(2,1)}), bf16[8,128,256]{2,1,0:T(8,128)(2,1)S(1)}, u32[]{:S(2)}, u32[]{:S(2)}) async-start(bf16[8,128,256]{2,1,0:T(8,128)(2,1)} %get-tuple-element.29), calls=%async_computation.1 | async-start | bytes 1048576 | tf_op jit(solution)/shard_map/all_to_all | solution.py:23
  50.8 9.8 %collective-permute-start.4 = (bf16[4,2,16,1024]{3,2,1,0:T(8,128)(2,1)S(1)}, bf16[4,2,16,1024]{3,2,1,0:T(8,128)(2,1)S(1)}, u32[]{:S(2)}, u32[]{:S(2)}) collective-permute-start(bf16[4,2,16,1024]{3,2,1,0:T(8,128)(2,1)S(1)} %pad_maximum_fusion), channel_id=1, source_target_pairs={{0,8},{8,0},{1,9},{9,1},{2,10},{10,2},{3,11},{11,3},{4,12},{12,4},... | collective-permute-start | bytes 786440 | tf_op jit(solution)/shard_map/ppermute | solution.py:310
  61.8 14.5 %copy-start = (bf16[2,16,1024]{2,1,0:T(8,128)(2,1)S(1)}, bf16[2,16,1024]{2,1,0:T(8,128)(2,1)}, u32[]{:S(2)}) copy-start(bf16[2,16,1024]{2,1,0:T(8,128)(2,1)} %params.3) | copy-start | bytes 196612
  61.9 14.5 %copy-start.1 = (f32[2,16,1024]{2,1,0:T(8,128)S(1)}, f32[2,16,1024]{2,1,0:T(8,128)}, u32[]{:S(2)}) copy-start(f32[2,16,1024]{2,1,0:T(8,128)} %moment.1) | copy-start | bytes 393220
  61.9 14.4 %copy-start.2 = (s32[2,16,1024]{2,1,0:T(8,128)S(1)}, s32[2,16,1024]{2,1,0:T(8,128)}, u32[]{:S(2)}) copy-start(s32[2,16,1024]{2,1,0:T(8,128)} %codes.1) | copy-start | bytes 393220

commit v9 on v8

--- a/solution.py
+++ b/solution.py
@@ -91,15 +91,12 @@
 
 
 def right_kernel(got, own, one, two, three, other, out, right_out, held, right, sems):
-    at, odd = lax.axis_index("x") * 2 + lax.axis_index("core"), lax.axis_index("odd")
+    x, odd = lax.axis_index("x"), lax.axis_index("odd")
     ring, places = [], []
-    for bits in range(8):
-        block = (own, one, two, three)[bits // 2]
-        to = jnp.bitwise_xor(at, bits)
-        ring.append(block.at[bits % 2, odd])
-        places.append(right.at[odd, to])
-        ring.append(other.at[bits // 2, bits % 2])
-        places.append(right.at[1 - odd, to])
+    for bits, block in enumerate((own, one, two, three)):
+        to = jnp.bitwise_xor(x, bits)
+        ring += [block.at[:, odd], other.at[bits]]
+        places += [right.at[odd, to], right.at[1 - odd, to]]
     wait = pull([got] + ring, [held] + places, sems)
     wait()
     total = held[0].astype(F32)
@@ -118,8 +115,8 @@
         out_specs=(VMEM, VMEM),
         scratch_shapes=[
             pltpu.VMEM((8, 128, 256), BF16),
-            pltpu.VMEM((2, 8, 16, 1024), BF16),
-            pltpu.SemaphoreType.DMA((17,)),
+            pltpu.VMEM((2, 4, 2, 16, 1024), BF16),
+            pltpu.SemaphoreType.DMA((9,)),
         ],
         compiler_params=PARAMS,
     )(got, *rights, other)
@@ -310,7 +307,10 @@
     flip = lambda values, axis, size, bit: lax.ppermute(values, axis, [(i, i ^ bit) for i in range(size)])
     tie = lax.optimization_barrier
 
-    near = jnp.stack([right_basis, flip(right_basis, "core", 2, 1)])
+    near = flip(right_basis, "core", 2, 1)
+    near = jnp.where(
+        lax.axis_index("core") == 0, jnp.stack([right_basis, near]), jnp.stack([near, right_basis])
+    )
     rights = [near] + [flip(near, "x", 4, bits) for bits in (1, 2, 3)]
 
     sent = panels(grads[0], left_basis)

time: 134 us -> 133 us (level)
  no operation moved by 1% of the time
where the time goes in v9:
time: 133 us; the launch traced here: 132 us
  blocking collectives  67.4 us (51%)
  starting transfers between devices  39.7 us (30%)
  waiting for transfers between devices  16.8 us (13%)
  Pallas kernels  7.1 us (5%)
    all_to_all x4, blocking collectives, exchange(): return lax.all_to_all(blocks, axes, split_axis=0, concat_axis=0, tiled=True)  67.4 us
    all_to_all x2, starting transfers between devices, exchange(): return lax.all_to_all(blocks, axes, split_axis=0, concat_axis=0, tiled=True)  24.9 us
    ppermute x5, starting transfers between devices, on_device(): lax.ppermute(values, axis, [(i, i ^ bit) for i in range(size)])  14.8 us
    ppermute x5, waiting for transfers between devices, on_device(): lax.ppermute(values, axis, [(i, i ^ bit) for i in range(size)])  11.5 us
    all_to_all x2, waiting for transfers between devices, exchange(): return lax.all_to_all(blocks, axes, split_axis=0, concat_axis=0, tiled=True)  5.24 us
  transfers between devices with their start and end apart: 7, of which 5 were waited for; matrix products, arithmetic and copies ran while one was open for 0% of the time, Pallas kernels for 0%

profile of v9, /device:TPU:1, one launch (start us, length us, event | category | flops | bytes accessed | tf_op | source)
XLA Modules:
  0.0 131.9 jit_solution(16143037235304701443)
XLA Ops:
  0.6 2.0 %shard_map.127 = bf16[32,2,16,384]{3,2,1,0:T(8,128)(2,1)} custom-call(bf16[2,16,8192]{2,1,0:T(8,128)(2,1)} %bitcast.25, bf16[2,16,1024]{2,1,0:T(8,128)(2,1)} %left.1), custom_call_target="tpu_custom_call" | custom-call | tf_op jit(solution)/shard_map/pallas_call | solution.py:54
  2.6 17.3 %all-to-all-start = ((bf16[64,16,384]{2,1,0:T(8,128)(2,1)}), bf16[64,16,384]{2,1,0:T(8,128)(2,1)S(1)}, u32[]{:S(2)}, u32[]{:S(2)}) async-start(bf16[64,16,384]{2,1,0:T(8,128)(2,1)} %bitcast.24), calls=%async_computation | async-start | bytes 1572864 | tf_op jit(solution)/shard_map/all_to_all | solution.py:23
  19.9 0.0 copy-done.5
  19.9 2.9 %collective-permute-start = (bf16[2,16,1024]{2,1,0:T(8,128)(2,1)S(1)}, bf16[2,16,1024]{2,1,0:T(8,128)(2,1)S(1)}, u32[]{:S(2)}, u32[]{:S(2)}) collective-permute-start(bf16[2,16,1024]{2,1,0:T(8,128)(2,1)S(1)} %copy-done.5), channel_id=1, source_target_pairs={{0,1},{1,0},{2,3},{3,2},{4,5},{5,4},{6,7},{7,6},{8,9},{9,8},{10,11... | collective-permute-start | bytes 196616 | tf_op jit(solution)/shard_map/ppermute | solution.py:307
  22.8 0.9 collective-permute-done
  23.7 4.4 %collective-permute-start.3 = (bf16[2,2,16,1024]{3,2,1,0:T(8,128)(2,1)S(1)}, bf16[2,2,16,1024]{3,2,1,0:T(8,128)(2,1)S(1)}, u32[]{:S(2)}, u32[]{:S(2)}) collective-permute-start(bf16[2,2,16,1024]{3,2,1,0:T(8,128)(2,1)S(1)} %maximum_select_fusion.own), channel_id=1, source_target_pairs={{0,6},{2,4},{4,2},{6,0},{1,7},{3,5},{5,3},{7,1},{8,14},{10,12},{12... | collective-permute-start | bytes 393224 | tf_op jit(solution)/shard_map/ppermute | solution.py:307
  28.1 2.4 %collective-permute-start.2 = (bf16[2,2,16,1024]{3,2,1,0:T(8,128)(2,1)S(1)}, bf16[2,2,16,1024]{3,2,1,0:T(8,128)(2,1)S(1)}, u32[]{:S(2)}, u32[]{:S(2)}) collective-permute-start(bf16[2,2,16,1024]{3,2,1,0:T(8,128)(2,1)S(1)} %maximum_select_fusion.own), channel_id=1, source_target_pairs={{0,4},{2,6},{4,0},{6,2},{1,5},{3,7},{5,1},{7,3},{8,12},{10,14},{12... | collective-permute-start | bytes 393224 | tf_op jit(solution)/shard_map/ppermute | solution.py:307
  30.5 2.2 %collective-permute-start.1 = (bf16[2,2,16,1024]{3,2,1,0:T(8,128)(2,1)S(1)}, bf16[2,2,16,1024]{3,2,1,0:T(8,128)(2,1)S(1)}, u32[]{:S(2)}, u32[]{:S(2)}) collective-permute-start(bf16[2,2,16,1024]{3,2,1,0:T(8,128)(2,1)S(1)} %maximum_select_fusion.own), channel_id=1, source_target_pairs={{0,2},{2,0},{4,6},{6,4},{1,3},{3,1},{5,7},{7,5},{8,10},{10,8},{12,... | collective-permute-start | bytes 393224 | tf_op jit(solution)/shard_map/ppermute | solution.py:307
  32.7 0.0 copy-start.4
  32.7 0.0 copy-start.3
  32.7 0.0 collective-permute-done.3.three
  32.7 3.2 %collective-permute-done.2.two = bf16[2,2,16,1024]{3,2,1,0:T(8,128)(2,1)S(1)} collective-permute-done((bf16[2,2,16,1024]{3,2,1,0:T(8,128)(2,1)S(1)}, bf16[2,2,16,1024]{3,2,1,0:T(8,128)(2,1)S(1)}, u32[]{:S(2)}, u32[]{:S(2)}) %collective-permute-start.2) | collective-permute-done | bytes 131104 | tf_op jit(solution)/shard_map/ppermute | solution.py:307
  35.9 0.6 collective-permute-done.1.one
  36.5 5.2 %all-to-all-done = bf16[64,16,384]{2,1,0:T(8,128)(2,1)S(1)} async-done(((bf16[64,16,384]{2,1,0:T(8,128)(2,1)}), bf16[64,16,384]{2,1,0:T(8,128)(2,1)S(1)}, u32[]{:S(2)}, u32[]{:S(2)}) %all-to-all-start) | async-done | bytes 786464 | tf_op jit(solution)/shard_map/all_to_all | solution.py:23
  41.8 0.0 copy-done.3
  41.8 1.3 %shard_map.128 = (bf16[8,128,256]{2,1,0:T(8,128)(2,1)}, bf16[128,1024]{1,0:T(8,128)(2,1)S(1)}, f32[2,2,8,128]{3,2,1,0:T(8,128)S(1)}) custom-call(bf16[8,128,384]{2,1,0:T(8,128)(2,1)S(1)} %bitcast.18, f32[2,8]{1,0:T(2,128)S(1)} %copy-done.3, f32[2,8]{1,0:T(2,128)S(1)} %copy-done.4), custom_call_target="tpu_custom_call" | custom-call | tf_op jit(solution)/shard_map/pallas_call | solution.py:83
  43.1 7.6 %all-to-all-start.1 = ((bf16[8,128,256]{2,1,0:T(8,128)(2,1)}), bf16[8,128,256]{2,1,0:T(8,128)(2,1)S(1)}, u32[]{:S(2)}, u32[]{:S(2)}) async-start(bf16[8,128,256]{2,1,0:T(8,128)(2,1)} %get-tuple-element.29), calls=%async_computation.1 | async-start | bytes 1048576 | tf_op jit(solution)/shard_map/all_to_all | solution.py:23
  50.8 3.0 %collective-permute-start.4 = (bf16[4,2,16,1024]{3,2,1,0:T(8,128)(2,1)S(1)}, bf16[4,2,16,1024]{3,2,1,0:T(8,128)(2,1)S(1)}, u32[]{:S(2)}, u32[]{:S(2)}) collective-permute-start(bf16[4,2,16,1024]{3,2,1,0:T(8,128)(2,1)S(1)} %pad_maximum_fusion), channel_id=1, source_target_pairs={{0,8},{8,0},{1,9},{9,1},{2,10},{10,2},{3,11},{11,3},{4,12},{12,4},... | collective-permute-start | bytes 786440 | tf_op jit(solution)/shard_map/ppermute | solution.py:307
  53.8 6.8 %collective-permute-done.4.other = bf16[4,2,16,1024]{3,2,1,0:T(8,128)(2,1)S(1)} collective-permute-done((bf16[4,2,16,1024]{3,2,1,0:T(8,128)(2,1)S(1)}, bf16[4,2,16,1024]{3,2,1,0:T(8,128)(2,1)S(1)}, u32[]{:S(2)}, u32[]{:S(2)}) %collective-permute-start.4) | collective-permute-done | bytes 262176 | tf_op jit(solution)/shard_map/ppermute | solution.py:307
  60.7 0.0 all-to-all-done.1.got
  60.7 0.9 shard_map.129
  61.6 0.0 copy-start
  61.6 0.0 copy-start.1
  61.6 0.0 copy-start.2
  61.6 14.4 %all_to_all.30 = bf16[8,16,1024]{2,1,0:T(8,128)(2,1)S(1)} all-to-all(bf16[8,16,1024]{2,1,0:T(8,128)(2,1)S(1)} %bitcast.23), channel_id=1, replica_groups=mesh['rep'=8,'pair'=4,'odd'=2,'x'=4,'core'=2] {'pair','odd'}, dimensions={0} | all-to-all | bytes 524288 | tf_op jit(solution)/shard_map/all_to_all | solution.py:23
  76.1 0.9 shard_map.130
  77.0 13.8 %all_to_all.31.got = bf16[8,176,128]{2,1,0:T(8,128)(2,1)S(1)} all-to-all(bf16[8,176,128]{2,1,0:T(8,128)(2,1)S(1)} %bitcast.22), channel_id=1, replica_groups=mesh['rep'=8,'pair'=4,'odd'=2,'x'=4,'core'=2] {'pair','odd'}, dimensions={0} | all-to-all | bytes 720896 | tf_op jit(solution)/shard_map/all_to_all | solution.py:23
  90.8 0.5 shard_map.131
  91.3 17.6 %all_to_all.32.got = bf16[8,272,128]{2,1,0:T(8,128)(2,1)S(1)} all-to-all(bf16[8,272,128]{2,1,0:T(8,128)(2,1)S(1)} %get-tuple-element.38), channel_id=1, replica_groups=mesh['rep'=8,'pair'=4,'odd'=2,'x'=4,'core'=2] {'x','core'}, dimensions={0} | all-to-all | bytes 1114112 | tf_op jit(solution)/shard_map/all_to_all | solution.py:23
  108.9 0.4 shard_map.132
  109.3 21.6 %all_to_all.33 = bf16[64,16,256]{2,1,0:T(8,128)(2,1)S(1)} all-to-all(bf16[64,16,256]{2,1,0:T(8,128)(2,1)S(1)} %bitcast.21), channel_id=1, replica_groups=mesh['rep'=8,'pair'=4,'odd'=2,'x'=4,'core'=2] {'rep','pair','odd'}, dimensions={0} | all-to-all | bytes 1048576 | tf_op jit(solution)/shard_map/all_to_all | solution.py:23
  130.9 1.0 shard_map.133
  (9 shorter events, 0.1 us)
Async XLA Ops:
  2.6 17.3 %copy-start.5 = (bf16[2,16,1024]{2,1,0:T(8,128)(2,1)S(1)}, bf16[2,16,1024]{2,1,0:T(8,128)(2,1)}, u32[]{:S(2)}) copy-start(bf16[2,16,1024]{2,1,0:T(8,128)(2,1)} %param.11) | copy-start | bytes 196612
  2.6 39.1 %all-to-all-start = ((bf16[64,16,384]{2,1,0:T(8,128)(2,1)}), bf16[64,16,384]{2,1,0:T(8,128)(2,1)S(1)}, u32[]{:S(2)}, u32[]{:S(2)}) async-start(bf16[64,16,384]{2,1,0:T(8,128)(2,1)} %bitcast.24), calls=%async_computation | async-start | bytes 1572864 | tf_op jit(solution)/shard_map/all_to_all | solution.py:23
  19.9 3.8 %collective-permute-start = (bf16[2,16,1024]{2,1,0:T(8,128)(2,1)S(1)}, bf16[2,16,1024]{2,1,0:T(8,128)(2,1)S(1)}, u32[]{:S(2)}, u32[]{:S(2)}) collective-permute-start(bf16[2,16,1024]{2,1,0:T(8,128)(2,1)S(1)} %copy-done.5), channel_id=1, source_target_pairs={{0,1},{1,0},{2,3},{3,2},{4,5},{5,4},{6,7},{7,6},{8,9},{9,8},{10,11... | collective-permute-start | bytes 196616 | tf_op jit(solution)/shard_map/ppermute | solution.py:307
  23.7 9.0 %collective-permute-start.3 = (bf16[2,2,16,1024]{3,2,1,0:T(8,128)(2,1)S(1)}, bf16[2,2,16,1024]{3,2,1,0:T(8,128)(2,1)S(1)}, u32[]{:S(2)}, u32[]{:S(2)}) collective-permute-start(bf16[2,2,16,1024]{3,2,1,0:T(8,128)(2,1)S(1)} %maximum_select_fusion.own), channel_id=1, source_target_pairs={{0,6},{2,4},{4,2},{6,0},{1,7},{3,5},{5,3},{7,1},{8,14},{10,12},{12... | collective-permute-start | bytes 393224 | tf_op jit(solution)/shard_map/ppermute | solution.py:307
  28.1 7.8 %collective-permute-start.2 = (bf16[2,2,16,1024]{3,2,1,0:T(8,128)(2,1)S(1)}, bf16[2,2,16,1024]{3,2,1,0:T(8,128)(2,1)S(1)}, u32[]{:S(2)}, u32[]{:S(2)}) collective-permute-start(bf16[2,2,16,1024]{3,2,1,0:T(8,128)(2,1)S(1)} %maximum_select_fusion.own), channel_id=1, source_target_pairs={{0,4},{2,6},{4,0},{6,2},{1,5},{3,7},{5,1},{7,3},{8,12},{10,14},{12... | collective-permute-start | bytes 393224 | tf_op jit(solution)/shard_map/ppermute | solution.py:307
  30.5 6.0 %collective-permute-start.1 = (bf16[2,2,16,1024]{3,2,1,0:T(8,128)(2,1)S(1)}, bf16[2,2,16,1024]{3,2,1,0:T(8,128)(2,1)S(1)}, u32[]{:S(2)}, u32[]{:S(2)}) collective-permute-start(bf16[2,2,16,1024]{3,2,1,0:T(8,128)(2,1)S(1)} %maximum_select_fusion.own), channel_id=1, source_target_pairs={{0,2},{2,0},{4,6},{6,4},{1,3},{3,1},{5,7},{7,5},{8,10},{10,8},{12,... | collective-permute-start | bytes 393224 | tf_op jit(solution)/shard_map/ppermute | solution.py:307
  32.7 9.1 %copy-start.4 = (f32[2,8]{1,0:T(2,128)S(1)}, f32[2,8]{1,0:T(2,128)}, u32[]{:S(2)}) copy-start(f32[2,8]{1,0:T(2,128)} %span.1) | copy-start | bytes 196
  32.7 9.1 %copy-start.3 = (f32[2,8]{1,0:T(2,128)S(1)}, f32[2,8]{1,0:T(2,128)}, u32[]{:S(2)}) copy-start(f32[2,8]{1,0:T(2,128)} %low.1) | copy-start | bytes 196
  43.1 17.5 %all-to-all-start.1 = ((bf16[8,128,256]{2,1,0:T(8,128)(2,1)}), bf16[8,128,256]{2,1,0:T(8,128)(2,1)S(1)}, u32[]{:S(2)}, u32[]{:S(2)}) async-start(bf16[8,128,256]{2,1,0:T(8,128)(2,1)} %get-tuple-element.29), calls=%async_computation.1 | async-start | bytes 1048576 | tf_op jit(solution)/shard_map/all_to_all | solution.py:23
  50.8 9.8 %collective-permute-start.4 = (bf16[4,2,16,1024]{3,2,1,0:T(8,128)(2,1)S(1)}, bf16[4,2,16,1024]{3,2,1,0:T(8,128)(2,1)S(1)}, u32[]{:S(2)}, u32[]{:S(2)}) collective-permute-start(bf16[4,2,16,1024]{3,2,1,0:T(8,128)(2,1)S(1)} %pad_maximum_fusion), channel_id=1, source_target_pairs={{0,8},{8,0},{1,9},{9,1},{2,10},{10,2},{3,11},{11,3},{4,12},{12,4},... | collective-permute-start | bytes 786440 | tf_op jit(solution)/shard_map/ppermute | solution.py:307
  61.6 14.5 %copy-start = (bf16[2,16,1024]{2,1,0:T(8,128)(2,1)S(1)}, bf16[2,16,1024]{2,1,0:T(8,128)(2,1)}, u32[]{:S(2)}) copy-start(bf16[2,16,1024]{2,1,0:T(8,128)(2,1)} %params.3) | copy-start | bytes 196612
  61.6 14.5 %copy-start.1 = (f32[2,16,1024]{2,1,0:T(8,128)S(1)}, f32[2,16,1024]{2,1,0:T(8,128)}, u32[]{:S(2)}) copy-start(f32[2,16,1024]{2,1,0:T(8,128)} %moment.1) | copy-start | bytes 393220
  61.6 14.4 %copy-start.2 = (s32[2,16,1024]{2,1,0:T(8,128)S(1)}, s32[2,16,1024]{2,1,0:T(8,128)}, u32[]{:S(2)}) copy-start(s32[2,16,1024]{2,1,0:T(8,128)} %codes.1) | copy-start | bytes 393220

commit v10 on v9

--- a/solution.py
+++ b/solution.py
@@ -90,7 +90,7 @@
     )(grads, low, span)
 
 
-def right_kernel(got, own, one, two, three, other, out, right_out, held, right, sems):
+def right_kernel(got, own, one, two, three, other, out, right, held, sems):
     x, odd = lax.axis_index("x"), lax.axis_index("odd")
     ring, places = [], []
     for bits, block in enumerate((own, one, two, three)):
@@ -104,18 +104,16 @@
         total += held[part].astype(F32)
     basis = right[...].reshape(256, 1024)
     out[...] = jnp.dot(total.astype(BF16), basis, preferred_element_type=F32).astype(BF16)
-    right_out[...] = basis
 
 
 def right_part(got, rights, other):
     return pl.pallas_call(
         right_kernel,
-        out_shape=(shape(128, 1024), shape(256, 1024)),
+        out_shape=(shape(128, 1024), shape(2, 4, 2, 16, 1024)),
         in_specs=[ANY] * 6,
         out_specs=(VMEM, VMEM),
         scratch_shapes=[
             pltpu.VMEM((8, 128, 256), BF16),
-            pltpu.VMEM((2, 4, 2, 16, 1024), BF16),
             pltpu.SemaphoreType.DMA((9,)),
         ],
         compiler_params=PARAMS,
@@ -326,7 +324,7 @@
     got = exchange(turned.reshape(8, 16, 1024), B).reshape(4, 2, 16, 1024)
     block, moment_new, second_new = moments(got, moment, codes, spread, params)
     got = exchange(block.reshape(8, 176, 128), B)
-    block, old = back_part(got, right_rows)
+    block, old = back_part(got, right_rows.reshape(256, 1024))
     got = exchange(block, A)
     moved, ends = update_part(got, left_rows, old)
     got = exchange(moved.reshape(64, 16, 256), ZB).reshape(8, 4, 2, 16, 256)

time: 133 us -> 133 us (level)
  no operation moved by 1% of the time
where the time goes in v10:
time: 133 us; the launch traced here: 132 us
  blocking collectives  67.4 us (51%)
  starting transfers between devices  39.7 us (30%)
  waiting for transfers between devices  16.8 us (13%)
  Pallas kernels  7.09 us (5%)
    all_to_all x4, blocking collectives, exchange(): return lax.all_to_all(blocks, axes, split_axis=0, concat_axis=0, tiled=True)  67.4 us
    all_to_all x2, starting transfers between devices, exchange(): return lax.all_to_all(blocks, axes, split_axis=0, concat_axis=0, tiled=True)  24.9 us
    ppermute x5, starting transfers between devices, on_device(): lax.ppermute(values, axis, [(i, i ^ bit) for i in range(size)])  14.8 us
    ppermute x5, waiting for transfers between devices, on_device(): lax.ppermute(values, axis, [(i, i ^ bit) for i in range(size)])  11.5 us
    all_to_all x2, waiting for transfers between devices, exchange(): return lax.all_to_all(blocks, axes, split_axis=0, concat_axis=0, tiled=True)  5.24 us
  transfers between devices with their start and end apart: 7, of which 5 were waited for; matrix products, arithmetic and copies ran while one was open for 0% of the time, Pallas kernels for 0%

profile of v10, /device:TPU:1, one launch (start us, length us, event | category | flops | bytes accessed | tf_op | source)
XLA Modules:
  0.0 131.9 jit_solution(7880604908199805171)
XLA Ops:
  0.6 2.0 %shard_map.127 = bf16[32,2,16,384]{3,2,1,0:T(8,128)(2,1)} custom-call(bf16[2,16,8192]{2,1,0:T(8,128)(2,1)} %bitcast.27, bf16[2,16,1024]{2,1,0:T(8,128)(2,1)} %left.1), custom_call_target="tpu_custom_call" | custom-call | tf_op jit(solution)/shard_map/pallas_call | solution.py:54
  2.6 17.3 %all-to-all-start = ((bf16[64,16,384]{2,1,0:T(8,128)(2,1)}), bf16[64,16,384]{2,1,0:T(8,128)(2,1)S(1)}, u32[]{:S(2)}, u32[]{:S(2)}) async-start(bf16[64,16,384]{2,1,0:T(8,128)(2,1)} %bitcast.26), calls=%async_computation | async-start | bytes 1572864 | tf_op jit(solution)/shard_map/all_to_all | solution.py:23
  19.9 2.9 %collective-permute-start = (bf16[2,16,1024]{2,1,0:T(8,128)(2,1)S(1)}, bf16[2,16,1024]{2,1,0:T(8,128)(2,1)S(1)}, u32[]{:S(2)}, u32[]{:S(2)}) collective-permute-start(bf16[2,16,1024]{2,1,0:T(8,128)(2,1)S(1)} %copy-done.5), channel_id=1, source_target_pairs={{0,1},{1,0},{2,3},{3,2},{4,5},{5,4},{6,7},{7,6},{8,9},{9,8},{10,11... | collective-permute-start | bytes 196616 | tf_op jit(solution)/shard_map/ppermute | solution.py:305
  22.8 0.9 collective-permute-done
  23.7 4.4 %collective-permute-start.3 = (bf16[2,2,16,1024]{3,2,1,0:T(8,128)(2,1)S(1)}, bf16[2,2,16,1024]{3,2,1,0:T(8,128)(2,1)S(1)}, u32[]{:S(2)}, u32[]{:S(2)}) collective-permute-start(bf16[2,2,16,1024]{3,2,1,0:T(8,128)(2,1)S(1)} %maximum_select_fusion.own), channel_id=1, source_target_pairs={{0,6},{2,4},{4,2},{6,0},{1,7},{3,5},{5,3},{7,1},{8,14},{10,12},{12... | collective-permute-start | bytes 393224 | tf_op jit(solution)/shard_map/ppermute | solution.py:305
  28.1 2.4 %collective-permute-start.2 = (bf16[2,2,16,1024]{3,2,1,0:T(8,128)(2,1)S(1)}, bf16[2,2,16,1024]{3,2,1,0:T(8,128)(2,1)S(1)}, u32[]{:S(2)}, u32[]{:S(2)}) collective-permute-start(bf16[2,2,16,1024]{3,2,1,0:T(8,128)(2,1)S(1)} %maximum_select_fusion.own), channel_id=1, source_target_pairs={{0,4},{2,6},{4,0},{6,2},{1,5},{3,7},{5,1},{7,3},{8,12},{10,14},{12... | collective-permute-start | bytes 393224 | tf_op jit(solution)/shard_map/ppermute | solution.py:305
  30.5 2.2 %collective-permute-start.1 = (bf16[2,2,16,1024]{3,2,1,0:T(8,128)(2,1)S(1)}, bf16[2,2,16,1024]{3,2,1,0:T(8,128)(2,1)S(1)}, u32[]{:S(2)}, u32[]{:S(2)}) collective-permute-start(bf16[2,2,16,1024]{3,2,1,0:T(8,128)(2,1)S(1)} %maximum_select_fusion.own), channel_id=1, source_target_pairs={{0,2},{2,0},{4,6},{6,4},{1,3},{3,1},{5,7},{7,5},{8,10},{10,8},{12,... | collective-permute-start | bytes 393224 | tf_op jit(solution)/shard_map/ppermute | solution.py:305
  32.7 0.0 copy-start.4
  32.7 0.0 copy-start.3
  32.7 0.0 collective-permute-done.3.three
  32.7 3.2 %collective-permute-done.2.two = bf16[2,2,16,1024]{3,2,1,0:T(8,128)(2,1)S(1)} collective-permute-done((bf16[2,2,16,1024]{3,2,1,0:T(8,128)(2,1)S(1)}, bf16[2,2,16,1024]{3,2,1,0:T(8,128)(2,1)S(1)}, u32[]{:S(2)}, u32[]{:S(2)}) %collective-permute-start.2) | collective-permute-done | bytes 131104 | tf_op jit(solution)/shard_map/ppermute | solution.py:305
  35.9 0.6 collective-permute-done.1.one
  36.5 5.2 %all-to-all-done = bf16[64,16,384]{2,1,0:T(8,128)(2,1)S(1)} async-done(((bf16[64,16,384]{2,1,0:T(8,128)(2,1)}), bf16[64,16,384]{2,1,0:T(8,128)(2,1)S(1)}, u32[]{:S(2)}, u32[]{:S(2)}) %all-to-all-start) | async-done | bytes 786464 | tf_op jit(solution)/shard_map/all_to_all | solution.py:23
  41.8 0.0 copy-done.4
  41.8 1.3 %shard_map.128 = (bf16[8,128,256]{2,1,0:T(8,128)(2,1)}, bf16[128,1024]{1,0:T(8,128)(2,1)S(1)}, f32[2,2,8,128]{3,2,1,0:T(8,128)S(1)}) custom-call(bf16[8,128,384]{2,1,0:T(8,128)(2,1)S(1)} %bitcast.19, f32[2,8]{1,0:T(2,128)S(1)} %copy-done.3, f32[2,8]{1,0:T(2,128)S(1)} %copy-done.4), custom_call_target="tpu_custom_call" | custom-call | tf_op jit(solution)/shard_map/pallas_call | solution.py:83
  43.1 7.6 %all-to-all-start.1 = ((bf16[8,128,256]{2,1,0:T(8,128)(2,1)}), bf16[8,128,256]{2,1,0:T(8,128)(2,1)S(1)}, u32[]{:S(2)}, u32[]{:S(2)}) async-start(bf16[8,128,256]{2,1,0:T(8,128)(2,1)} %get-tuple-element.29), calls=%async_computation.1 | async-start | bytes 1048576 | tf_op jit(solution)/shard_map/all_to_all | solution.py:23
  50.8 3.0 %collective-permute-start.4 = (bf16[4,2,16,1024]{3,2,1,0:T(8,128)(2,1)S(1)}, bf16[4,2,16,1024]{3,2,1,0:T(8,128)(2,1)S(1)}, u32[]{:S(2)}, u32[]{:S(2)}) collective-permute-start(bf16[4,2,16,1024]{3,2,1,0:T(8,128)(2,1)S(1)} %pad_maximum_fusion), channel_id=1, source_target_pairs={{0,8},{8,0},{1,9},{9,1},{2,10},{10,2},{3,11},{11,3},{4,12},{12,4},... | collective-permute-start | bytes 786440 | tf_op jit(solution)/shard_map/ppermute | solution.py:305
  53.8 6.8 %collective-permute-done.4.other = bf16[4,2,16,1024]{3,2,1,0:T(8,128)(2,1)S(1)} collective-permute-done((bf16[4,2,16,1024]{3,2,1,0:T(8,128)(2,1)S(1)}, bf16[4,2,16,1024]{3,2,1,0:T(8,128)(2,1)S(1)}, u32[]{:S(2)}, u32[]{:S(2)}) %collective-permute-start.4) | collective-permute-done | bytes 262176 | tf_op jit(solution)/shard_map/ppermute | solution.py:305
  60.7 0.0 all-to-all-done.1.got
  60.7 0.9 shard_map.129
  61.6 0.0 copy-start
  61.6 0.0 copy-start.1
  61.6 0.0 copy-start.2
  61.6 14.4 %all_to_all.30 = bf16[8,16,1024]{2,1,0:T(8,128)(2,1)S(1)} all-to-all(bf16[8,16,1024]{2,1,0:T(8,128)(2,1)S(1)} %bitcast.25), channel_id=1, replica_groups=mesh['rep'=8,'pair'=4,'odd'=2,'x'=4,'core'=2] {'pair','odd'}, dimensions={0} | all-to-all | bytes 524288 | tf_op jit(solution)/shard_map/all_to_all | solution.py:23
  76.1 0.0 copy-done.2
  76.1 0.9 shard_map.130
  77.0 13.8 %all_to_all.31.got = bf16[8,176,128]{2,1,0:T(8,128)(2,1)S(1)} all-to-all(bf16[8,176,128]{2,1,0:T(8,128)(2,1)S(1)} %bitcast.24), channel_id=1, replica_groups=mesh['rep'=8,'pair'=4,'odd'=2,'x'=4,'core'=2] {'pair','odd'}, dimensions={0} | all-to-all | bytes 720896 | tf_op jit(solution)/shard_map/all_to_all | solution.py:23
  90.8 0.5 shard_map.131
  91.3 17.6 %all_to_all.32.got = bf16[8,272,128]{2,1,0:T(8,128)(2,1)S(1)} all-to-all(bf16[8,272,128]{2,1,0:T(8,128)(2,1)S(1)} %get-tuple-element.38), channel_id=1, replica_groups=mesh['rep'=8,'pair'=4,'odd'=2,'x'=4,'core'=2] {'x','core'}, dimensions={0} | all-to-all | bytes 1114112 | tf_op jit(solution)/shard_map/all_to_all | solution.py:23
  108.9 0.4 shard_map.132
  109.3 21.6 %all_to_all.33 = bf16[64,16,256]{2,1,0:T(8,128)(2,1)S(1)} all-to-all(bf16[64,16,256]{2,1,0:T(8,128)(2,1)S(1)} %bitcast.23), channel_id=1, replica_groups=mesh['rep'=8,'pair'=4,'odd'=2,'x'=4,'core'=2] {'rep','pair','odd'}, dimensions={0} | all-to-all | bytes 1048576 | tf_op jit(solution)/shard_map/all_to_all | solution.py:23
  130.9 1.0 shard_map.133
  (9 shorter events, 0.1 us)
Async XLA Ops:
  2.6 17.3 %copy-start.5 = (bf16[2,16,1024]{2,1,0:T(8,128)(2,1)S(1)}, bf16[2,16,1024]{2,1,0:T(8,128)(2,1)}, u32[]{:S(2)}) copy-start(bf16[2,16,1024]{2,1,0:T(8,128)(2,1)} %param.11) | copy-start | bytes 196612
  2.6 39.1 %all-to-all-start = ((bf16[64,16,384]{2,1,0:T(8,128)(2,1)}), bf16[64,16,384]{2,1,0:T(8,128)(2,1)S(1)}, u32[]{:S(2)}, u32[]{:S(2)}) async-start(bf16[64,16,384]{2,1,0:T(8,128)(2,1)} %bitcast.26), calls=%async_computation | async-start | bytes 1572864 | tf_op jit(solution)/shard_map/all_to_all | solution.py:23
  19.9 3.8 %collective-permute-start = (bf16[2,16,1024]{2,1,0:T(8,128)(2,1)S(1)}, bf16[2,16,1024]{2,1,0:T(8,128)(2,1)S(1)}, u32[]{:S(2)}, u32[]{:S(2)}) collective-permute-start(bf16[2,16,1024]{2,1,0:T(8,128)(2,1)S(1)} %copy-done.5), channel_id=1, source_target_pairs={{0,1},{1,0},{2,3},{3,2},{4,5},{5,4},{6,7},{7,6},{8,9},{9,8},{10,11... | collective-permute-start | bytes 196616 | tf_op jit(solution)/shard_map/ppermute | solution.py:305
  23.7 9.0 %collective-permute-start.3 = (bf16[2,2,16,1024]{3,2,1,0:T(8,128)(2,1)S(1)}, bf16[2,2,16,1024]{3,2,1,0:T(8,128)(2,1)S(1)}, u32[]{:S(2)}, u32[]{:S(2)}) collective-permute-start(bf16[2,2,16,1024]{3,2,1,0:T(8,128)(2,1)S(1)} %maximum_select_fusion.own), channel_id=1, source_target_pairs={{0,6},{2,4},{4,2},{6,0},{1,7},{3,5},{5,3},{7,1},{8,14},{10,12},{12... | collective-permute-start | bytes 393224 | tf_op jit(solution)/shard_map/ppermute | solution.py:305
  28.1 7.8 %collective-permute-start.2 = (bf16[2,2,16,1024]{3,2,1,0:T(8,128)(2,1)S(1)}, bf16[2,2,16,1024]{3,2,1,0:T(8,128)(2,1)S(1)}, u32[]{:S(2)}, u32[]{:S(2)}) collective-permute-start(bf16[2,2,16,1024]{3,2,1,0:T(8,128)(2,1)S(1)} %maximum_select_fusion.own), channel_id=1, source_target_pairs={{0,4},{2,6},{4,0},{6,2},{1,5},{3,7},{5,1},{7,3},{8,12},{10,14},{12... | collective-permute-start | bytes 393224 | tf_op jit(solution)/shard_map/ppermute | solution.py:305
  30.5 6.0 %collective-permute-start.1 = (bf16[2,2,16,1024]{3,2,1,0:T(8,128)(2,1)S(1)}, bf16[2,2,16,1024]{3,2,1,0:T(8,128)(2,1)S(1)}, u32[]{:S(2)}, u32[]{:S(2)}) collective-permute-start(bf16[2,2,16,1024]{3,2,1,0:T(8,128)(2,1)S(1)} %maximum_select_fusion.own), channel_id=1, source_target_pairs={{0,2},{2,0},{4,6},{6,4},{1,3},{3,1},{5,7},{7,5},{8,10},{10,8},{12,... | collective-permute-start | bytes 393224 | tf_op jit(solution)/shard_map/ppermute | solution.py:305
  32.7 9.1 %copy-start.4 = (f32[2,8]{1,0:T(2,128)S(1)}, f32[2,8]{1,0:T(2,128)}, u32[]{:S(2)}) copy-start(f32[2,8]{1,0:T(2,128)} %span.1) | copy-start | bytes 196
  32.7 9.1 %copy-start.3 = (f32[2,8]{1,0:T(2,128)S(1)}, f32[2,8]{1,0:T(2,128)}, u32[]{:S(2)}) copy-start(f32[2,8]{1,0:T(2,128)} %low.1) | copy-start | bytes 196
  43.1 17.5 %all-to-all-start.1 = ((bf16[8,128,256]{2,1,0:T(8,128)(2,1)}), bf16[8,128,256]{2,1,0:T(8,128)(2,1)S(1)}, u32[]{:S(2)}, u32[]{:S(2)}) async-start(bf16[8,128,256]{2,1,0:T(8,128)(2,1)} %get-tuple-element.29), calls=%async_computation.1 | async-start | bytes 1048576 | tf_op jit(solution)/shard_map/all_to_all | solution.py:23
  50.8 9.8 %collective-permute-start.4 = (bf16[4,2,16,1024]{3,2,1,0:T(8,128)(2,1)S(1)}, bf16[4,2,16,1024]{3,2,1,0:T(8,128)(2,1)S(1)}, u32[]{:S(2)}, u32[]{:S(2)}) collective-permute-start(bf16[4,2,16,1024]{3,2,1,0:T(8,128)(2,1)S(1)} %pad_maximum_fusion), channel_id=1, source_target_pairs={{0,8},{8,0},{1,9},{9,1},{2,10},{10,2},{3,11},{11,3},{4,12},{12,4},... | collective-permute-start | bytes 786440 | tf_op jit(solution)/shard_map/ppermute | solution.py:305
  61.6 14.5 %copy-start = (bf16[2,16,1024]{2,1,0:T(8,128)(2,1)S(1)}, bf16[2,16,1024]{2,1,0:T(8,128)(2,1)}, u32[]{:S(2)}) copy-start(bf16[2,16,1024]{2,1,0:T(8,128)(2,1)} %params.3) | copy-start | bytes 196612
  61.6 14.5 %copy-start.1 = (f32[2,16,1024]{2,1,0:T(8,128)S(1)}, f32[2,16,1024]{2,1,0:T(8,128)}, u32[]{:S(2)}) copy-start(f32[2,16,1024]{2,1,0:T(8,128)} %moment.1) | copy-start | bytes 393220
  61.6 14.4 %copy-start.2 = (s32[2,16,1024]{2,1,0:T(8,128)S(1)}, s32[2,16,1024]{2,1,0:T(8,128)}, u32[]{:S(2)}) copy-start(s32[2,16,1024]{2,1,0:T(8,128)} %codes.1) | copy-start | bytes 393220
